TPU v7x, 32 devices: a whole 2x2x4 slice. The times are simulated.
32 devices in a mesh: groups: 2 (over x), dp: 8 (over z, y), tensor: 2 (over core).
Axes of the slice: x: 2, y: 2, z: 4, core: 2. Of those that a mesh axis runs over, the one named last changes fastest.
Arguments:
- hidden: bfloat16 [12288, 8192], P(('groups', 'dp', 'tensor')), parts along dimension 0, may hold values from -64 to 64
- norm_gain: bfloat16 [8192], replicated, may hold values from 0.099609375 to 1.8984375
- key_weight: bfloat16 [8192, 512], P(None, 'tensor'), may hold values from -0.0625 to 0.0625
- value_weight: bfloat16 [8192, 512], P(None, 'tensor'), may hold values from -0.0625 to 0.0625
- queries: bfloat16 [12288, 4096], P(('groups', 'dp'), 'tensor'), parts along dimension 0, may hold values from -300 to 300
- segment_ids: int32 [12288], P(('groups', 'dp')), parts along dimension 0, may hold values from 0 to 7, as said below
- prompt_lengths: int32 [16, 8], P(('groups', 'dp')), parts along dimension 0, may hold values from 1 to 192, as said below
- prompt_offsets: int32 [16, 8], P(('groups', 'dp')), parts along dimension 0, may hold values from 0 to 767, as said below
- decode_owner: int32 [16, 8], P(('groups', 'dp')), parts along dimension 0, may hold values from 0 to 7, as said below
- slot_offsets: int32 [16, 8], P(('groups', 'dp')), parts along dimension 0, may hold values from 0 to 1535, as said below
Outputs:
- attended: bfloat16 [12288, 4096], P(('groups', 'dp'), 'tensor'), parts along dimension 0
- key_cache: bfloat16 [16, 1536, 512], P(('groups', 'dp'), None, 'tensor'), parts along dimension 0
- value_cache: bfloat16 [16, 1536, 512], P(('groups', 'dp'), None, 'tensor'), parts along dimension 0
There are 2 independent parts, one for each index of `groups`. A program takes and returns all parts, laid end to end along the dimension named above; an argument that names none is the same for every part. Nothing has to cross between parts.
Inputs may be any that keep to these rules, and one draw needn't show every extreme that they name: `prompt_lengths`: the 8 lengths of a pack sum to 768; every pack has a prompt of exactly 192 tokens. `prompt_offsets`: 0 for a pack's first prompt, then the running sum of the lengths before it. `segment_ids`: row t of a pack belongs to prompt s where prompt_offsets[p, s] <= t < prompt_offsets[p, s] + prompt_lengths[p, s]. `decode_owner`: in every pack each owner receives exactly one prompt. `slot_offsets`: the prompt of pack p lies in slots p * 192 to (p + 1) * 192 - 1 of its owner's cache.
All inputs are finite; a program needn't handle non-finite values.
Results may differ from a plain program's by a relative error of at most 0.011.
Values may be sent and summed in bfloat16 or wider, within the bound.
No kernel may reach another device: no remote copies, remote signals or barrier semaphores. Data moves between devices by JAX's collectives and lax.ppermute only.
A program may use at most 192 MiB of HBM per device.

v0:
```python
import jax
import jax.numpy as jnp
from jax import lax
from jax.sharding import PartitionSpec as P

HD = 128


epsilon = 1e-05
rope_base = 500000.0


def normalize(row_block, gain_vector):
    floats = row_block.astype(jnp.float32)
    factor = lax.rsqrt(jnp.mean(floats * floats, axis=-1, keepdims=True) + epsilon)
    return (floats * factor * gain_vector.astype(jnp.float32)).astype(jnp.bfloat16)


def rotate(key_floats, positions):
    half_dim = HD // 2
    inverse_freq = rope_base ** (-(jnp.arange(half_dim, dtype=jnp.float32) * 2.0) / HD)
    angles = positions.astype(jnp.float32)[:, None] * inverse_freq[None, :]
    cosine = jnp.cos(angles)[:, None, :]
    sine_part = jnp.sin(angles)[:, None, :]
    shaped = key_floats.reshape(key_floats.shape[0], -1, HD)
    first_half = shaped[..., :half_dim]
    second_half = shaped[..., half_dim:]
    turned = jnp.concatenate(
        [
            first_half * cosine - second_half * sine_part,
            second_half * cosine + first_half * sine_part,
        ],
        axis=-1,
    )
    return turned.reshape(key_floats.shape)


def pick_column(chosen, table):
    return jnp.sum(jnp.where(chosen, table, 0), axis=1)


def on_device(
    hidden,
    norm_gain,
    key_weight,
    value_weight,
    queries,
    segment_ids,
    prompt_lengths,
    prompt_offsets,
    decode_owner,
    slot_offsets,
):
    normed = normalize(hidden, norm_gain)
    kv_width = key_weight.shape[1]
    piece = lax.all_gather(normed, "tensor", axis=0, tiled=True)
    key_part = jnp.dot(piece, key_weight, preferred_element_type=jnp.float32)
    value_part = jnp.dot(piece, value_weight, preferred_element_type=jnp.float32)
    projected = jnp.concatenate([key_part, value_part], axis=1)
    tok_rows = projected.shape[0]
    row_index = jnp.arange(tok_rows, dtype=jnp.int32)
    chosen = segment_ids[:, None] == jnp.arange(prompt_offsets.shape[1], dtype=jnp.int32)[None, :]
    within = row_index - pick_column(chosen, prompt_offsets)
    key_rows = rotate(projected[:, :kv_width], within).astype(jnp.bfloat16)
    value_rows = projected[:, kv_width:].astype(jnp.bfloat16)
    kv_heads = kv_width // HD
    group_size = queries.shape[1] // kv_width
    query_block = queries.reshape(tok_rows, kv_heads, group_size, HD)
    key_block = key_rows.reshape(tok_rows, kv_heads, HD)
    value_block = value_rows.reshape(tok_rows, kv_heads, HD)
    scores = jnp.einsum(
        "qgrd,kgd->grqk", query_block, key_block, preferred_element_type=jnp.float32
    ) * HD ** (-0.5)
    query_index = jnp.arange(0, tok_rows, dtype=jnp.int32)
    key_index = jnp.arange(tok_rows, dtype=jnp.int32)
    allowed = (segment_ids[0:tok_rows, None] == segment_ids[None, :tok_rows]) & (
        key_index[None, :] <= query_index[:, None]
    )
    scores = jnp.where(allowed, scores, -1e30)
    maxima = jnp.max(scores, axis=-1, keepdims=True)
    exponent = jnp.exp(scores - maxima)
    totals = jnp.sum(exponent, axis=-1, keepdims=True)
    weights = (exponent / totals).astype(jnp.bfloat16)
    output = jnp.einsum("grqk,kgd->qgrd", weights, value_block, preferred_element_type=jnp.float32)
    pieces_out = output.reshape(tok_rows, -1).astype(jnp.bfloat16)
    packed = jnp.concatenate([key_rows, value_rows], axis=1)
    owner_row = pick_column(chosen, decode_owner)
    slot_row = pick_column(chosen, slot_offsets)
    usable = within < pick_column(chosen, prompt_lengths)
    cache_rows = 2 * tok_rows
    target = jnp.where(usable, owner_row * cache_rows + slot_row + within, -1)
    own_base = lax.axis_index("dp") * cache_rows
    empty_cache = jnp.zeros((cache_rows, 2 * kv_width), jnp.bfloat16)
    rows_in = lax.all_gather(packed, "dp", axis=0, tiled=True)
    target_in = lax.all_gather(target, "dp", axis=0, tiled=True)
    local_row = target_in - own_base
    inside = (local_row >= 0) & (local_row < cache_rows)
    handed = empty_cache.at[jnp.where(inside, local_row, cache_rows)].set(rows_in, mode="drop")
    key_cache = handed[:, :kv_width][None]
    value_cache = handed[:, kv_width:][None]
    return (pieces_out, key_cache, value_cache)


def solution(mesh):
    in_specs = (
        P(("groups", "dp", "tensor"), None),
        P(),
        P(None, "tensor"),
        P(None, "tensor"),
        P(("groups", "dp"), "tensor"),
        P(("groups", "dp")),
        P(("groups", "dp"), None),
        P(("groups", "dp"), None),
        P(("groups", "dp"), None),
        P(("groups", "dp"), None),
    )
    out_specs = (
        P(("groups", "dp"), "tensor"),
        P(("groups", "dp"), None, "tensor"),
        P(("groups", "dp"), None, "tensor"),
    )
    return jax.shard_map(
        on_device, mesh=mesh, in_specs=in_specs, out_specs=out_specs, check_vma=False
    )
```

profile of v0, /device:TPU:16, one launch (start us, length us, event | category | flops | bytes accessed | tf_op | source)
XLA Modules:
  0.0 214.4 jit_solution(13196484163968947907)
XLA Ops:
  7.2 0.9 convert_element_type.39
  8.1 4.3 %fusion.8 = f32[384]{0:T(512)S(1)} fusion(bf16[384,8192]{1,0:T(8,128)(2,1)} %param.10), kind=kLoop, calls=%fused_computation.13 | loop fusion | flops 9436800 | bytes 6292992 | tf_op jit(solution)/shard_map/reduce_sum | solution.py:15
  12.4 4.6 %fusion.10 = bf16[384,8192]{1,0:T(8,128)(2,1)} fusion(bf16[384,8192]{1,0:T(8,128)(2,1)S(1)} %copy-done, f32[8192]{0:T(1024)S(1)} %convert_element_type.39, f32[384]{0:T(512)S(1)} %add_rsqrt_fusion), kind=kLoop, calls=%fused_computation.15 | loop fusion | flops 12582912 | bytes 12617216 | tf_op jit(solution)/shard_map/convert_element_type | solution.py:16
  17.3 0.4 copy-done.4
  17.8 1.4 multiply_cosine_fusion
  19.3 24.2 %all-gather.4.cloned.1.call-done = bf16[768,8192]{1,0:T(8,128)(2,1)} async-done(((bf16[384,8192]{1,0:T(8,128)(2,1)}), bf16[768,8192]{1,0:T(8,128)(2,1)}) %all-gather.4.cloned.1.call-update) | async-done | bytes 12582928 | tf_op jit(solution)/shard_map/all_gather | solution.py:56
  43.4 13.8 %fusion.39 = f32[768,256]{0,1:T(8,128)S(1)} fusion(bf16[768,8192]{1,0:T(8,128)(2,1)} %all-gather.4.cloned.1.call-done, bf16[8192,256]{1,0:T(8,128)(2,1)} %param.12), kind=kOutput, calls=%fused_computation.51 | convolution fusion | flops 3221225472 | bytes 17563648 | tf_op jit(solution)/shard_map/dot_general | solution.py:57
  57.3 0.3 copy.44
  57.6 0.3 copy.43
  58.3 0.9 copy.37
  59.2 9.4 %convolution_convert_fusion = bf16[768,256]{0,1:T(8,128)(2,1)S(1)} fusion(bf16[768,8192]{1,0:T(8,128)(2,1)} %all-gather.4.cloned.1.call-done, bf16[8192,256]{1,0:T(8,128)(2,1)} %param.13), kind=kOutput, calls=%fused_computation.22 | convolution fusion | flops 3221422080 | bytes 17170432 | tf_op jit(solution)/shard_map/dot_general | solution.py:58
  68.6 0.7 copy-done.3
  69.4 0.9 pad_maximum_fusion
  70.3 2.7 %copy.45 = bf16[96,8,16,128]{3,2,1,0:T(8,128)(2,1)} copy(bf16[96,8,16,128]{3,1,2,0:T(8,128)(2,1)S(1)} %bitcast.53) | data formatting | bytes 6291456
  73.0 26.2 %all-gather = s32[8,1,768]{2,1,0:T(1,128)S(1)} all-gather(s32[1,1,768]{2,1,0:T(1,128)S(1)} %reshape.106), channel_id=1, replica_groups=mesh['groups'=2,'dp'=8,'tensor'=2] {'dp'}, dimensions={0}, use_global_device_ids=true | all-gather | bytes 27648 | tf_op jit(solution)/shard_map/all_gather | solution.py:95
  99.2 0.6 compare_select_fusion
  99.9 0.4 fusion.18
  100.2 19.6 %fusion.30 = (f32[2,8,768]{2,1,0:T(8,128)}, f32[2,8,768,768]{2,3,1,0:T(8,128)}) fusion(pred[768,768]{0,1:T(8,128)(4,1)S(1)} %fusion.18, bf16[768,2,8,128]{3,2,1,0:T(8,128)(2,1)} %bitcast.54, bf16[768,2,128]{2,0,1:T(8,128)(2,1)S(1)} %maximum_convert_fusion), kind=kOutput, calls=%fused_computation.50 | convolution fusion | flops 2453668608 | bytes 41926656 | tf_op jit(solution)/shard_map/sub | solution.py:81
  119.8 13.5 %fusion.19 = bf16[2,128,8,768]{3,1,2,0:T(8,128)(2,1)S(1)} fusion(bf16[768,2,128,1]{0,2,3,1:T(8,128)(2,1)} %bitcast.58, f32[2,8,768,768]{2,3,1,0:T(8,128)} %get-tuple-element.30, f32[2,8,768]{2,1,0:T(8,128)} %get-tuple-element.29), kind=kOutput, calls=%fused_computation.21 | convolution fusion | flops 2436366336 | bytes 41336832 | tf_op jit(solution)/shard_map/grqk,kgd->qgrd/dot_general | solution.py:84
  133.3 2.9 %copy.39 = bf16[768,2048]{1,0:T(8,128)(2,1)} copy(bf16[768,2048]{0,1:T(8,128)(2,1)S(1)} %bitcast.55) | data formatting | bytes 6291456
  136.1 33.8 %all-gather.6.cloned.1.call-done = bf16[6144,512]{0,1:T(8,128)(2,1)} async-done(((bf16[768,512]{0,1:T(8,128)(2,1)}), bf16[6144,512]{0,1:T(8,128)(2,1)}) %all-gather.6.cloned.1.call-update) | async-done | bytes 6291472 | tf_op jit(solution)/shard_map/all_gather | solution.py:94
  169.9 8.7 %copy.38 = bf16[6144,512]{1,0:T(8,128)(2,1)} copy(bf16[6144,512]{0,1:T(8,128)(2,1)} %all-gather.6.cloned.1.call-done) | data formatting | bytes 12582912 | tf_op jit(solution)/shard_map/all_gather | solution.py:94
  178.6 27.7 %scatter_custom_fusion = bf16[1536,512]{1,0:T(8,128)(2,1)S(1)} fusion(s32[6144]{0:T(1024)} %compare_select_fusion, bf16[6144,512]{1,0:T(8,128)(2,1)} %copy.38, bf16[]{:T(256)} %constant.11.clone.1), kind=kCustom, calls=%fused_computation.27 | custom fusion | bytes 1573376 | tf_op jit(solution)/shard_map/scatter | solution.py:98
  206.3 1.2 slice_bitcast_fusion
  (29 shorter events, 1.0 us)
Async XLA Ops:
  7.2 36.3 %all-gather.4.cloned.1.call-start = ((), (), s32[]{:S(2)}) async-start(), calls=%async_computation | async-start | bytes 18874368 | tf_op jit(solution)/shard_map/all_gather | solution.py:56
  7.2 5.2 %copy-start = (bf16[384,8192]{1,0:T(8,128)(2,1)S(1)}, bf16[384,8192]{1,0:T(8,128)(2,1)}, u32[]{:S(2)}) copy-start(bf16[384,8192]{1,0:T(8,128)(2,1)} %param.10) | copy-start | bytes 18874372
  17.0 0.7 copy-start.4
  17.0 0.7 copy-start.5
  17.0 0.7 copy-start.6
  17.0 0.7 copy-start.7
  17.0 0.7 copy-start.8
  17.0 152.9 %all-gather.6.cloned.1.call-start = ((), (), s32[]{:S(2)}) async-start(), calls=%async_computation.1 | async-start | bytes 7077888 | tf_op jit(solution)/shard_map/all_gather | solution.py:94
  59.2 10.1 %copy-start.2 = (bf16[768,2,128]{0,2,1:T(8,128)(2,1)S(1)}, bf16[768,2,128]{0,2,1:T(8,128)(2,1)}, u32[]{:S(2)}) copy-start(bf16[768,2,128]{0,2,1:T(8,128)(2,1)} %copy.37) | copy-start | bytes 1179652
  59.2 11.1 %copy-start.1 = (bf16[768,2048]{1,0:T(8,128)(2,1)S(1)}, bf16[768,2048]{1,0:T(8,128)(2,1)}, u32[]{:S(2)}) copy-start(bf16[768,2048]{1,0:T(8,128)(2,1)} %param.14) | copy-start | bytes 9437188
  68.6 0.7 copy-start.3
Sparse Core Ops, SparseCore 0:
  17.2 26.2 all-gather.3
  70.4 99.4 all-gather.5
where the time goes:
time: 217 us; the launch traced here: 214 us
  waiting for transfers between devices  58 us (27%)
  matrix products  56.2 us (26%)
  local copies, waits for them, and re-layouts  45.8 us (21%)
  blocking collectives  26.2 us (12%)
  between operations  14.2 us (7%)
  other arithmetic  13.7 us (6%)
    all_gather x1, waiting for transfers between devices, on_device(): rows_in = lax.all_gather(packed, 'dp', axis=0, tiled=True)  33.8 us
    scatter x1, local copies, waits for them, and re-layouts, on_device(): empty_cache.at[jnp.where(inside, local_row, cache_rows)]  27.7 us
    all_gather x1, blocking collectives, on_device(): target_in = lax.all_gather(target, 'dp', axis=0, tiled=True)  26.2 us
    all_gather x1, waiting for transfers between devices, on_device(): piece = lax.all_gather(normed, 'tensor', axis=0, tiled=True)  24.2 us
    sub x1, matrix products, on_device(): exponent = jnp.exp(scores - maxima)  19.6 us
    dot_general x1, matrix products, on_device(): key_part = jnp.dot(piece, key_weight, preferred_element_type=jnp.float32)  13.8 us
    dot_general x1, matrix products, on_device(): jnp.einsum('grqk,kgd->qgrd', weights, value_block, preferred_element_type...  13.5 us
    dot_general x1, matrix products, on_device(): jnp.dot(piece, value_weight, preferred_element_type=jnp.float32)  9.36 us
  transfers between devices with their start and end apart: 2, of which 2 were waited for; matrix products, arithmetic and copies ran while one was open for 19% of the time, Pallas kernels for 0%

commit v1 on v0

v1 whole, which is shorter than its diff:
```python
import functools

import jax
import jax.numpy as jnp
import numpy as np
from jax import lax
from jax.experimental import pallas as pl
from jax.experimental.pallas import tpu as pltpu
from jax.sharding import PartitionSpec as P

HD = 128
EPSILON = 1e-05
ROPE_BASE = 500000.0
MIB = 1024 * 1024
SMEM = pl.BlockSpec(memory_space=pltpu.SMEM)
VMEM = pl.BlockSpec(memory_space=pltpu.VMEM)


def prompt_start(rows, offset_ref):
    start = jnp.zeros_like(rows)
    for s in range(offset_ref.shape[1]):
        offset = offset_ref[0, s]
        start = jnp.where(rows >= offset, jnp.maximum(start, offset), start)
    return start


def rotation_tables(block, offset_ref, cos_ref, sin_ref):
    position = lax.broadcasted_iota(jnp.int32, (block, HD), 0).astype(jnp.float32)
    lane = lax.broadcasted_iota(jnp.int32, (block, HD), 1)
    half = lax.broadcasted_iota(jnp.int32, (1, HD), 1) % (HD // 2)
    inverse = jnp.zeros((1, HD), jnp.float32)
    for i in range(HD // 2):
        inverse = jnp.where(half == i, np.float32(ROPE_BASE ** (-2.0 * i / HD)), inverse)
    angle = position * inverse
    cosine = jnp.cos(angle)
    sine = jnp.where(lane < HD // 2, -1.0, 1.0) * jnp.sin(angle)
    for s in range(offset_ref.shape[1]):
        rows = pl.ds(offset_ref[0, s], block)
        cos_ref[rows, :] = cosine
        sin_ref[rows, :] = sine


def project(h_ref, gain_ref, wk_ref, wv_ref, acc_k, acc_v, squares, chunk, ready=None):
    for c in range(h_ref.shape[1] // chunk):
        if ready is not None:
            ready(c)
        at = slice(c * chunk, (c + 1) * chunk)
        h = h_ref[:, at]
        scaled = h * gain_ref[:, at]
        key = jnp.dot(scaled, wk_ref[at, :], preferred_element_type=jnp.float32)
        value = jnp.dot(scaled, wv_ref[at, :], preferred_element_type=jnp.float32)
        parts = [h[:, j * HD : (j + 1) * HD].astype(jnp.float32) for j in range(chunk // HD)]
        total = sum(p * p for p in parts)
        if c == 0:
            acc_k[...], acc_v[...], squares[...] = key, value, total
        else:
            acc_k[...] += key
            acc_v[...] += value
            squares[...] += total


def finish(width, cosine, sine, acc_k, acc_v, squares):
    factor = lax.rsqrt(jnp.sum(squares[...], axis=1, keepdims=True) / width + EPSILON)
    keys = []
    for h in range(acc_k.shape[1] // HD):
        x = acc_k[:, h * HD : (h + 1) * HD] * factor
        keys.append((x * cosine + pltpu.roll(x, HD // 2, 1) * sine).astype(jnp.bfloat16))
    return jnp.concatenate(keys, axis=1), (acc_v[...] * factor).astype(jnp.bfloat16)


def own_kernel(
    block, chunk, offset_ref, h_hbm, wk_hbm, wv_hbm, gain_ref,
    out_ref, cos_ref, sin_ref, wk_ref, wv_ref, h_ref, acc_k, acc_v, squares, cos_pad, sin_pad, sems
):
    rows, width = h_hbm.shape
    cols = acc_k.shape[1]

    def copies(c):
        at = pl.ds(c * chunk, chunk)
        return (
            pltpu.make_async_copy(h_hbm.at[:, at], h_ref.at[:, at], sems.at[c, 0]),
            pltpu.make_async_copy(wk_hbm.at[at, :], wk_ref.at[at, :], sems.at[c, 1]),
            pltpu.make_async_copy(wv_hbm.at[at, :], wv_ref.at[at, :], sems.at[c, 2]),
        )

    def ready(c):
        for copy in copies(c):
            copy.wait()

    for c in range(width // chunk):
        for copy in copies(c):
            copy.start()
    rotation_tables(block, offset_ref, cos_pad, sin_pad)
    cos_ref[...] = cos_pad[: cos_ref.shape[0], :]
    sin_ref[...] = sin_pad[: sin_ref.shape[0], :]
    project(h_ref, gain_ref, wk_ref, wv_ref, acc_k, acc_v, squares, chunk, ready)
    here = pl.ds(pl.multiple_of(lax.axis_index("tensor") * rows, rows), rows)
    keys, values = finish(width, cos_pad[here, :], sin_pad[here, :], acc_k, acc_v, squares)
    out_ref[:, :cols] = keys
    out_ref[:, cols:] = values


def own_rows(block, offsets, hidden, wk, wv, gain, tok_rows, chunk=1024):
    rows, width = hidden.shape
    cols = wk.shape[1]
    hbm = pl.BlockSpec(memory_space=pltpu.HBM)
    f32 = jnp.float32
    return pl.pallas_call(
        functools.partial(own_kernel, block, chunk),
        in_specs=[SMEM, hbm, hbm, hbm, VMEM],
        out_specs=[VMEM] * 5,
        out_shape=[
            jax.ShapeDtypeStruct((rows, 2 * cols), jnp.bfloat16),
            jax.ShapeDtypeStruct((tok_rows, HD), f32),
            jax.ShapeDtypeStruct((tok_rows, HD), f32),
            jax.ShapeDtypeStruct(wk.shape, wk.dtype),
            jax.ShapeDtypeStruct(wv.shape, wv.dtype),
        ],
        scratch_shapes=[
            pltpu.VMEM((rows, width), jnp.bfloat16),
            pltpu.VMEM((rows, cols), f32),
            pltpu.VMEM((rows, cols), f32),
            pltpu.VMEM((rows, HD), f32),
            pltpu.VMEM((tok_rows + block, HD), f32),
            pltpu.VMEM((tok_rows + block, HD), f32),
            pltpu.SemaphoreType.DMA((width // chunk, 3)),
        ],
        compiler_params=pltpu.CompilerParams(vmem_limit_bytes=44 * MIB),
        cost_estimate=pl.CostEstimate(
            flops=4 * rows * width * cols, bytes_accessed=2 * (rows * width + 2 * width * cols), transcendentals=0
        ),
        name="own_rows",
    )(offsets, hidden, wk, wv, gain)


def select_block(block, cols, owner, places, kv_ref, out_ref):
    offset_ref, length_ref, owner_ref, slot_ref = places
    offset = jnp.int32(0)
    length = jnp.int32(0)
    slot = jnp.int32(0)
    for s in range(owner_ref.shape[1]):
        hit = owner_ref[0, s] == owner
        offset = jnp.where(hit, offset_ref[0, s], offset)
        length = jnp.where(hit, length_ref[0, s], length)
        slot = jnp.where(hit, slot_ref[0, s], slot)
    span = block + 16
    start = jnp.minimum((offset // 16) * 16, kv_ref.shape[0] - span)
    start = pl.multiple_of(start, 16)
    place = lax.broadcasted_iota(jnp.int32, (block, span), 0) + (lax.axis_index("dp") * block - slot)
    token = lax.broadcasted_iota(jnp.int32, (block, span), 1) + (start - offset)
    chosen = (place == token) & (place >= 0) & (place < length)
    picked = jnp.dot(
        jnp.where(chosen, 1.0, 0.0).astype(jnp.bfloat16),
        kv_ref[pl.ds(start, span), :],
        preferred_element_type=jnp.float32,
    ).astype(jnp.bfloat16)
    out_ref[0] = picked[:, :cols]
    out_ref[1] = picked[:, cols:]


def peer_kernel(
    far, block, chunk, offset_ref, length_ref, owner_ref, slot_ref,
    h_ref, wk_ref, wv_ref, gain_ref, cos_ref, sin_ref, own_ref, kv_ref, *rest
):
    blocks, (acc_k, acc_v, squares) = rest[: len(far)], rest[len(far) :]
    rows, width = h_ref.shape
    cols = acc_k.shape[1]
    mine = lax.axis_index("tensor")
    there = pl.ds(pl.multiple_of((1 - mine) * rows, rows), rows)
    here = pl.ds(pl.multiple_of(mine * rows, rows), rows)
    project(h_ref, gain_ref, wk_ref, wv_ref, acc_k, acc_v, squares, chunk)
    keys, values = finish(width, cos_ref[there, :], sin_ref[there, :], acc_k, acc_v, squares)
    kv_ref[there, :cols] = keys
    kv_ref[there, cols:] = values
    kv_ref[here, :] = own_ref[...]
    places = (offset_ref, length_ref, owner_ref, slot_ref)
    for k, out_ref in zip(far, blocks):
        select_block(block, cols, jnp.bitwise_xor(lax.axis_index("dp"), k), places, kv_ref, out_ref)


def peer_rows(far, block, places, peer, wk, wv, gain, cosine, sine, own, chunk=1024):
    rows, width = peer.shape
    cols = wk.shape[1]
    tok_rows = cosine.shape[0]
    return pl.pallas_call(
        functools.partial(peer_kernel, far, block, chunk),
        in_specs=[SMEM] * 4 + [VMEM] * 7,
        out_specs=[VMEM] * (1 + len(far)),
        out_shape=[jax.ShapeDtypeStruct((tok_rows, 2 * cols), jnp.bfloat16)]
        + [jax.ShapeDtypeStruct((2, block, cols), jnp.bfloat16)] * len(far),
        scratch_shapes=[
            pltpu.VMEM((rows, cols), jnp.float32),
            pltpu.VMEM((rows, cols), jnp.float32),
            pltpu.VMEM((rows, HD), jnp.float32),
        ],
        compiler_params=pltpu.CompilerParams(vmem_limit_bytes=28 * MIB),
        cost_estimate=pl.CostEstimate(
            flops=4 * rows * width * cols, bytes_accessed=2 * (rows * width + 2 * width * cols), transcendentals=0
        ),
        name="peer_rows",
    )(*places, peer, wk, wv, gain, cosine, sine, own)


def attend_kernel(tile, window, skipped, near, block, *refs):
    places, (q_ref, kv_ref), rest = refs[:4], refs[4:6], refs[6:]
    if skipped:
        rest = rest[1:]
    out_ref, blocks = rest[0], rest[1:]
    step = pl.program_id(0)
    cols = kv_ref.shape[1] // 2
    groups = cols // HD
    heads = q_ref.shape[1] // HD // groups

    if near:
        @pl.when(step == 0)
        def _():
            for k, block_ref in zip(near, blocks):
                select_block(block, cols, jnp.bitwise_xor(lax.axis_index("dp"), k), places, kv_ref, block_ref)

    first = (step + skipped) * tile
    start = pl.multiple_of(jnp.maximum(first + tile - window, 0), 16)
    row = first + lax.broadcasted_iota(jnp.int32, (tile, window), 0)
    key = start + lax.broadcasted_iota(jnp.int32, (tile, window), 1)
    allowed = (key <= row) & (key >= prompt_start(row, places[0]))
    bias = jnp.where(allowed, 0.0, -1e30)[None]
    ones = jnp.ones((window, HD), jnp.bfloat16)
    scale = HD**-0.5 * float(np.log2(np.e))
    for g in range(groups):
        at = [slice((g * heads + h) * HD, (g * heads + h + 1) * HD) for h in range(heads)]
        q = jnp.concatenate([q_ref[:, a] for a in at], axis=0)
        k = kv_ref[pl.ds(start, window), g * HD : (g + 1) * HD]
        v = kv_ref[pl.ds(start, window), cols + g * HD : cols + (g + 1) * HD]
        scores = lax.dot_general(q, k, (((1,), (1,)), ((), ())), preferred_element_type=jnp.float32)
        scores = scores.reshape(heads, tile, window) * scale + bias
        exponent = jnp.exp2(scores - jnp.max(scores, axis=2, keepdims=True))
        exponent = exponent.astype(jnp.bfloat16).reshape(heads * tile, window)
        summed = jnp.dot(exponent, jnp.concatenate([v, ones], axis=1), preferred_element_type=jnp.float32)
        result = (summed[:, :HD] / summed[:, HD:]).astype(jnp.bfloat16)
        for h, a in enumerate(at):
            out_ref[:, a] = result[h * tile : (h + 1) * tile]


def attend(places, queries, kv, longest, near=(), before=None, tile=64):
    rows, width = queries.shape
    window = tile + longest
    steps = rows // tile // 2
    skipped = 0 if before is None else steps
    cols = kv.shape[1] // 2
    rows_at = pl.BlockSpec((tile, width), lambda i: (i + skipped, 0))
    return pl.pallas_call(
        functools.partial(attend_kernel, tile, window, skipped, near, longest),
        grid=(steps,),
        in_specs=[SMEM] * 4
        + [rows_at, pl.BlockSpec(kv.shape, lambda i: (0, 0))]
        + ([pl.BlockSpec(memory_space=pl.ANY)] if skipped else []),
        out_specs=[rows_at] + [pl.BlockSpec((2, longest, cols), lambda i: (0, 0, 0))] * len(near),
        out_shape=[jax.ShapeDtypeStruct((rows, width), jnp.bfloat16)]
        + [jax.ShapeDtypeStruct((2, longest, cols), jnp.bfloat16)] * len(near),
        input_output_aliases={6: 0} if skipped else {},
        compiler_params=pltpu.CompilerParams(vmem_limit_bytes=32 * MIB),
        cost_estimate=pl.CostEstimate(
            flops=2 * rows * width * window,
            bytes_accessed=2 * rows * width,
            transcendentals=rows * window * width // HD // 2,
        ),
        name="attend_rest" if skipped else "attend_first",
    )(*places, queries, kv, *([before] if skipped else []))


def gather_kernel(n_dp, block, *refs):
    blocks, (key_ref, value_ref, sems) = refs[:n_dp], refs[n_dp:]
    me = lax.axis_index("dp")
    copies = []
    for k in range(n_dp):
        rows = pl.ds(pl.multiple_of(jnp.bitwise_xor(me, k) * block, block), block)
        for n, out_ref in enumerate((key_ref, value_ref)):
            copies.append(pltpu.make_async_copy(blocks[k].at[n], out_ref.at[rows, :], sems.at[k, n]))
    for copy in copies:
        copy.start()
    for copy in copies:
        copy.wait()


def on_device(
    hidden, norm_gain, key_weight, value_weight, queries,
    segment_ids, prompt_lengths, prompt_offsets, decode_owner, slot_offsets,
):
    n_dp = lax.axis_size("dp")
    half, width = hidden.shape
    tok_rows = queries.shape[0]
    cols = key_weight.shape[1]
    block = 2 * tok_rows // n_dp
    gain = norm_gain.reshape(1, width)

    peer = lax.ppermute(hidden, "tensor", [(0, 1), (1, 0)])
    own, cosine, sine, wk, wv = own_rows(
        block, prompt_offsets, hidden, key_weight, value_weight, gain, tok_rows
    )
    places = [prompt_offsets, prompt_lengths, decode_owner, slot_offsets]
    far = tuple(range(n_dp // 2, n_dp))
    near = tuple(range(n_dp // 2))
    swap = lambda a, k: a if k == 0 else lax.ppermute(a, "dp", [(p, p ^ k) for p in range(n_dp)])
    kv, *blocks = peer_rows(far, block, places, peer, wk, wv, gain, cosine, sine, own)
    received = {k: swap(a, k) for k, a in zip(far, blocks)}
    attended, *blocks = attend(places, queries, kv, block, near)
    received.update({k: swap(a, k) for k, a in zip(near, blocks)})
    attended = attend(places, queries, kv, block, (), attended)[0]
    cache = jax.ShapeDtypeStruct((n_dp * block, cols), jnp.bfloat16)
    anywhere = pl.BlockSpec(memory_space=pl.ANY)
    key_cache, value_cache = pl.pallas_call(
        functools.partial(gather_kernel, n_dp, block),
        in_specs=[VMEM] * n_dp,
        out_specs=[anywhere] * 2,
        out_shape=[cache, cache],
        scratch_shapes=[pltpu.SemaphoreType.DMA((n_dp, 2))],
        compiler_params=pltpu.CompilerParams(vmem_limit_bytes=8 * MIB),
        name="place_blocks",
    )(*[received[k] for k in range(n_dp)])
    return attended, key_cache[None], value_cache[None]


def solution(mesh):
    rows = P(("groups", "dp"))
    in_specs = (
        P(("groups", "dp", "tensor"), None),
        P(),
        P(None, "tensor"),
        P(None, "tensor"),
        P(("groups", "dp"), "tensor"),
        rows, rows, rows, rows, rows,
    )
    out_specs = (
        P(("groups", "dp"), "tensor"),
        P(("groups", "dp"), None, "tensor"),
        P(("groups", "dp"), None, "tensor"),
    )
    return jax.shard_map(on_device, mesh=mesh, in_specs=in_specs, out_specs=out_specs, check_vma=False)
```

time: 217 us -> 58.3 us (0.27); the launches traced: 214 us -> 57.9 us
  matrix products: 56.2 us -> 0 us
  local copies, waits for them, and re-layouts: 45.8 us -> 1.41 us
  waiting for transfers between devices: 58 us -> 15.3 us
  blocking collectives: 26.2 us -> 0 us
  Pallas kernels: 0 us -> 23.7 us
  starting transfers between devices: 0.26 us -> 16.7 us
  other arithmetic: 13.7 us -> 0 us
  between operations: 14.2 us -> 0.7 us
    all_gather x2 -> x0, waiting for transfers between devices: 57.9 us -> none  [the longest x1 33.8 us: on_device(): rows_in = lax.all_gather(packed, 'dp', axis=0, tiled=True)]
    dot_general x3 -> x0, matrix products: 36.7 us -> none  [the longest x1 13.8 us: on_device(): key_part = jnp.dot(piece, key_weight, preferred_element_type=jnp.float32)]
    scatter x1 -> x0, local copies, waits for them, and re-layouts: 27.7 us -> none  [on_device(): empty_cache.at[jnp.where(inside, local_row, cache_rows)]]
    all_gather x1 -> x0, blocking collectives: 26.2 us -> none  [on_device(): target_in = lax.all_gather(target, 'dp', axis=0, tiled=True)]
    pallas_call x0 -> x5, Pallas kernels: none -> 23.7 us  [the longest x2 11 us: attend(): pl.pallas_call(functools.partial(attend_kernel, tile, window, skipped, ne...]
    sub x1 -> x0, matrix products: 19.6 us -> none  [on_device(): exponent = jnp.exp(scores - maxima)]
    ppermute x0 -> x8, starting transfers between devices: none -> 16.7 us  [the longest x7 16.7 us: on_device(): lax.ppermute(a, 'dp', [(p, p ^ k) for p in range(n_dp)])]
    ppermute x0 -> x8, waiting for transfers between devices: none -> 15.3 us  [the longest x7 13 us: on_device(): lax.ppermute(a, 'dp', [(p, p ^ k) for p in range(n_dp)])]
  transfers between devices with their start and end apart: 2 -> 8, of which waited for: 2 -> 4; matrix products, arithmetic and copies ran while one was open for 19% -> 1% of each run, Pallas kernels for 0% -> 30%
where the time goes in v1:
time: 58.3 us; the launch traced here: 57.9 us
  Pallas kernels  23.7 us (41%)
  starting transfers between devices  16.7 us (29%)
  waiting for transfers between devices  15.3 us (26%)
  local copies, waits for them, and re-layouts  1.41 us (2%)
  between operations  0.7 us (1%)
    ppermute x7, starting transfers between devices, on_device(): lax.ppermute(a, 'dp', [(p, p ^ k) for p in range(n_dp)])  16.7 us
    ppermute x7, waiting for transfers between devices, on_device(): lax.ppermute(a, 'dp', [(p, p ^ k) for p in range(n_dp)])  13 us
    pallas_call x2, Pallas kernels, attend(): pl.pallas_call(functools.partial(attend_kernel, tile, window, skipped, ne...  11 us
    pallas_call x1, Pallas kernels, own_rows(): pl.pallas_call(functools.partial(own_kernel, block, chunk), in_specs=[SME...  6.63 us
    pallas_call x1, Pallas kernels, peer_rows(): pl.pallas_call(functools.partial(peer_kernel, far, block, chunk), in_spec...  4.78 us
    ppermute x1, waiting for transfers between devices, on_device(): peer = lax.ppermute(hidden, 'tensor', [(0, 1), (1, 0)])  2.31 us
    pallas_call x1, Pallas kernels, on_device(): pl.pallas_call(functools.partial(gather_kernel, n_dp, block), in_specs=[V...  1.28 us
  transfers between devices with their start and end apart: 8, of which 4 were waited for; matrix products, arithmetic and copies ran while one was open for 1% of the time, Pallas kernels for 30%

profile of v1, /device:TPU:16, one launch (start us, length us, event | category | flops | bytes accessed | tf_op | source)
XLA Modules:
  0.0 57.9 jit_solution(6884405127326518017)
XLA Ops:
  0.6 0.1 collective-permute-start
  0.7 0.7 %reshape.9.gain_ref = bf16[1,8192]{1,0:T(2,128)(2,1)S(1)} reshape(bf16[8192]{0:T(1024)(128)(2,1)} %param.11) | data formatting | bytes 32768 | tf_op jit(solution)/shard_map/reshape | solution.py:293
  1.5 0.0 copy-start.1
  1.5 0.6 %copy-done.1 = s32[1,8]{1,0:T(1,128)S(1)} copy-done((s32[1,8]{1,0:T(1,128)S(1)}, s32[1,8]{1,0:T(1,128)}, u32[]{:S(2)}) %copy-start.1) | copy-done | bytes 56
  2.1 6.6 %own_rows.1 = (bf16[384,512]{1,0:T(8,128)(2,1)S(1)}, f32[768,128]{1,0:T(8,128)S(1)}, f32[768,128]{1,0:T(8,128)S(1)}, bf16[8192,256]{1,0:T(8,128)(2,1)S(1)}, bf16[8192,256]{1,0:T(8,128)(2,1)S(1)}) custom-call(s32[1,8]{1,0:T(1,128)S(1)} %copy-done.1, bf16[384,8192]{1,0:T(8,128)(2,1)} %h_hbm.1, bf16[8192,256]{1,0:T(8,128)(2,1)} %wk_hbm.1, ...), custom_call_target="tpu_custom_call" | custom-call | flops 3221225472 | bytes 14680064 | tf_op jit(solution)/shard_map/own_rows/pallas_call | solution.py:108
  8.8 2.3 %collective-permute-done.h_ref = bf16[384,8192]{1,0:T(8,128)(2,1)S(1)} collective-permute-done((bf16[384,8192]{1,0:T(8,128)(2,1)}, bf16[384,8192]{1,0:T(8,128)(2,1)S(1)}, u32[]{:S(2)}, u32[]{:S(2)}) %collective-permute-start) | collective-permute-done | bytes 6291488 | tf_op jit(solution)/shard_map/ppermute | solution.py:295
  11.1 0.0 copy-start
  11.1 4.8 %peer_rows.1 = (bf16[768,512]{1,0:T(8,128)(2,1)S(1)}, bf16[2,192,256]{2,1,0:T(8,128)(2,1)S(1)}, bf16[2,192,256]{2,1,0:T(8,128)(2,1)S(1)}, bf16[2,192,256]{2,1,0:T(8,128)(2,1)S(1)}, bf16[2,192,256]{2,1,0:T(8,128)(2,1)S(1)}) custom-call(s32[1,8]{1,0:T(1,128)S(1)} %copy-done.1, s32[1,8]{1,0:T(1,128)S(1)} %copy-done.2, s32[1,8]{1,0:T(1,128)S(1)} %copy-done.3, ...), custom_call_target="tpu_custom_call" | custom-call | flops 3221225472 | bytes 14680064 | tf_op jit(solution)/shard_map/peer_rows/pallas_call | solution.py:185
  15.9 0.1 collective-permute-start.4
  16.0 3.9 %collective-permute-start.5 = (bf16[2,192,256]{2,1,0:T(8,128)(2,1)S(1)}, bf16[2,192,256]{2,1,0:T(8,128)(2,1)S(1)}, u32[]{:S(2)}, u32[]{:S(2)}) collective-permute-start(bf16[2,192,256]{2,1,0:T(8,128)(2,1)S(1)} %get-tuple-element.32), channel_id=1, source_target_pairs={{0,10},{2,8},{4,14},{6,12},{8,2},{10,0},{12,6},{14,4},{1,11},{3,9}... | collective-permute-start | bytes 589832 | tf_op jit(solution)/shard_map/ppermute | solution.py:302
  19.8 0.4 collective-permute-start.6
  20.3 1.5 %collective-permute-start.7 = (bf16[2,192,256]{2,1,0:T(8,128)(2,1)S(1)}, bf16[2,192,256]{2,1,0:T(8,128)(2,1)S(1)}, u32[]{:S(2)}, u32[]{:S(2)}) collective-permute-start(bf16[2,192,256]{2,1,0:T(8,128)(2,1)S(1)} %get-tuple-element.34), channel_id=1, source_target_pairs={{0,14},{2,12},{4,10},{6,8},{8,6},{10,4},{12,2},{14,0},{1,15},{3,13... | collective-permute-start | bytes 589832 | tf_op jit(solution)/shard_map/ppermute | solution.py:302
  21.8 5.7 %attend_first.1 = (bf16[768,2048]{1,0:T(8,128)(2,1)}, bf16[2,192,256]{2,1,0:T(8,128)(2,1)S(1)}, bf16[2,192,256]{2,1,0:T(8,128)(2,1)S(1)}, bf16[2,192,256]{2,1,0:T(8,128)(2,1)S(1)}, bf16[2,192,256]{2,1,0:T(8,128)(2,1)S(1)}) custom-call(s32[1,8]{1,0:T(1,128)S(1)} %copy-done.1, s32[1,8]{1,0:T(1,128)S(1)} %copy-done.2, s32[1,8]{1,0:T(1,128)S(1)} %copy-done.3, ...), custom_call_target="tpu_custom_call" | custom-call | flops 805306368 | bytes 3145728 | tf_op jit(solution)/shard_map/attend_first/pallas_call | solution.py:250
  27.5 1.5 %collective-permute-start.1 = (bf16[2,192,256]{2,1,0:T(8,128)(2,1)S(1)}, bf16[2,192,256]{2,1,0:T(8,128)(2,1)S(1)}, u32[]{:S(2)}, u32[]{:S(2)}) collective-permute-start(bf16[2,192,256]{2,1,0:T(8,128)(2,1)S(1)} %get-tuple-element.28), channel_id=1, source_target_pairs={{0,2},{2,0},{4,6},{6,4},{8,10},{10,8},{12,14},{14,12},{1,3},{3,1},... | collective-permute-start | bytes 589832 | tf_op jit(solution)/shard_map/ppermute | solution.py:302
  29.0 9.0 %collective-permute-done.4.refs_4_ = bf16[2,192,256]{2,1,0:T(8,128)(2,1)S(1)} collective-permute-done((bf16[2,192,256]{2,1,0:T(8,128)(2,1)S(1)}, bf16[2,192,256]{2,1,0:T(8,128)(2,1)S(1)}, u32[]{:S(2)}, u32[]{:S(2)}) %collective-permute-start.4) | collective-permute-done | bytes 196640 | tf_op jit(solution)/shard_map/ppermute | solution.py:302
  38.0 4.2 %collective-permute-start.2 = (bf16[2,192,256]{2,1,0:T(8,128)(2,1)S(1)}, bf16[2,192,256]{2,1,0:T(8,128)(2,1)S(1)}, u32[]{:S(2)}, u32[]{:S(2)}) collective-permute-start(bf16[2,192,256]{2,1,0:T(8,128)(2,1)S(1)} %get-tuple-element.29), channel_id=1, source_target_pairs={{0,4},{2,6},{4,0},{6,2},{8,12},{10,14},{12,8},{14,10},{1,5},{3,7},... | collective-permute-start | bytes 589832 | tf_op jit(solution)/shard_map/ppermute | solution.py:302
  42.2 0.1 collective-permute-done.5.refs_5_
  42.3 5.1 %collective-permute-start.3 = (bf16[2,192,256]{2,1,0:T(8,128)(2,1)S(1)}, bf16[2,192,256]{2,1,0:T(8,128)(2,1)S(1)}, u32[]{:S(2)}, u32[]{:S(2)}) collective-permute-start(bf16[2,192,256]{2,1,0:T(8,128)(2,1)S(1)} %get-tuple-element.30), channel_id=1, source_target_pairs={{0,6},{2,4},{4,2},{6,0},{8,14},{10,12},{12,10},{14,8},{1,7},{3,5},... | collective-permute-start | bytes 589832 | tf_op jit(solution)/shard_map/ppermute | solution.py:302
  47.4 5.3 %attend_rest.1 = bf16[768,2048]{1,0:T(8,128)(2,1)} custom-call(s32[1,8]{1,0:T(1,128)S(1)} %copy-done.1, s32[1,8]{1,0:T(1,128)S(1)} %copy-done.2, s32[1,8]{1,0:T(1,128)S(1)} %copy-done.3, s32[1,8]{1,0:T(1,128)S(1)} %copy-done.4, bf16[768,2048]{1,0:T(8,128)(2,1)S(1)} %copy-done, ...), custom_call_target="tpu_custom_call", output_to_operand_aliasing={{}: (6, {})} | custom-call | flops 805306368 | bytes 3145728 | tf_op jit(solution)/shard_map/attend_rest/pallas_call | solution.py:250
  52.6 0.0 collective-permute-done.6.refs_6_
  52.6 3.9 %collective-permute-done.7.refs_7_ = bf16[2,192,256]{2,1,0:T(8,128)(2,1)S(1)} collective-permute-done((bf16[2,192,256]{2,1,0:T(8,128)(2,1)S(1)}, bf16[2,192,256]{2,1,0:T(8,128)(2,1)S(1)}, u32[]{:S(2)}, u32[]{:S(2)}) %collective-permute-start.7) | collective-permute-done | bytes 196640 | tf_op jit(solution)/shard_map/ppermute | solution.py:302
  56.6 0.0 collective-permute-done.1.refs_1_
  56.6 0.0 collective-permute-done.2.refs_2_
  56.6 1.3 %place_blocks.1 = (bf16[1536,256]{1,0:T(8,128)(2,1)}, bf16[1536,256]{1,0:T(8,128)(2,1)}) custom-call(bf16[2,192,256]{2,1,0:T(8,128)(2,1)S(1)} %get-tuple-element.27.refs_0_, bf16[2,192,256]{2,1,0:T(8,128)(2,1)S(1)} %collective-permute-done.1.refs_1_, bf16[2,192,256]{2,1,0:T(8,128)(2,1)S(1)} %collective-permute-done.2.refs_2_, ...), custom_call_target="tpu_custom_call" | custom-call | tf_op jit(solution)/shard_map/place_blocks/pallas_call | solution.py:310
  (8 shorter events, 0.0 us)
Async XLA Ops:
  0.6 10.4 %collective-permute-start = (bf16[384,8192]{1,0:T(8,128)(2,1)}, bf16[384,8192]{1,0:T(8,128)(2,1)S(1)}, u32[]{:S(2)}, u32[]{:S(2)}) collective-permute-start(bf16[384,8192]{1,0:T(8,128)(2,1)} %h_hbm.1), channel_id=1, source_target_pairs={{0,1},{1,0},{2,3},{3,2},{4,5},{5,4},{6,7},{7,6},{8,9},{9,8},{10,11... | collective-permute-start | bytes 18874376 | tf_op jit(solution)/shard_map/ppermute | solution.py:295
  1.5 0.7 %copy-start.1 = (s32[1,8]{1,0:T(1,128)S(1)}, s32[1,8]{1,0:T(1,128)}, u32[]{:S(2)}) copy-start(s32[1,8]{1,0:T(1,128)} %refs_0_.3) | copy-start | bytes 100
  2.1 9.0 %copy-start.2 = (s32[1,8]{1,0:T(1,128)S(1)}, s32[1,8]{1,0:T(1,128)}, u32[]{:S(2)}) copy-start(s32[1,8]{1,0:T(1,128)} %refs_1_.3) | copy-start | bytes 100
  2.1 9.0 %copy-start.3 = (s32[1,8]{1,0:T(1,128)S(1)}, s32[1,8]{1,0:T(1,128)}, u32[]{:S(2)}) copy-start(s32[1,8]{1,0:T(1,128)} %refs_2_.3) | copy-start | bytes 100
  2.1 9.0 %copy-start.4 = (s32[1,8]{1,0:T(1,128)S(1)}, s32[1,8]{1,0:T(1,128)}, u32[]{:S(2)}) copy-start(s32[1,8]{1,0:T(1,128)} %refs_3_.3) | copy-start | bytes 100
  11.1 10.7 %copy-start = (bf16[768,2048]{1,0:T(8,128)(2,1)S(1)}, bf16[768,2048]{1,0:T(8,128)(2,1)}, u32[]{:S(2)}) copy-start(bf16[768,2048]{1,0:T(8,128)(2,1)} %refs_4_.3) | copy-start | bytes 9437188
  15.9 22.2 %collective-permute-start.4 = (bf16[2,192,256]{2,1,0:T(8,128)(2,1)S(1)}, bf16[2,192,256]{2,1,0:T(8,128)(2,1)S(1)}, u32[]{:S(2)}, u32[]{:S(2)}) collective-permute-start(bf16[2,192,256]{2,1,0:T(8,128)(2,1)S(1)} %get-tuple-element.31), channel_id=1, source_target_pairs={{0,8},{2,10},{4,12},{6,14},{8,0},{10,2},{12,4},{14,6},{1,9},{3,11}... | collective-permute-start | bytes 589832 | tf_op jit(solution)/shard_map/ppermute | solution.py:302
  16.0 26.3 %collective-permute-start.5 = (bf16[2,192,256]{2,1,0:T(8,128)(2,1)S(1)}, bf16[2,192,256]{2,1,0:T(8,128)(2,1)S(1)}, u32[]{:S(2)}, u32[]{:S(2)}) collective-permute-start(bf16[2,192,256]{2,1,0:T(8,128)(2,1)S(1)} %get-tuple-element.32), channel_id=1, source_target_pairs={{0,10},{2,8},{4,14},{6,12},{8,2},{10,0},{12,6},{14,4},{1,11},{3,9}... | collective-permute-start | bytes 589832 | tf_op jit(solution)/shard_map/ppermute | solution.py:302
  19.8 32.8 %collective-permute-start.6 = (bf16[2,192,256]{2,1,0:T(8,128)(2,1)S(1)}, bf16[2,192,256]{2,1,0:T(8,128)(2,1)S(1)}, u32[]{:S(2)}, u32[]{:S(2)}) collective-permute-start(bf16[2,192,256]{2,1,0:T(8,128)(2,1)S(1)} %get-tuple-element.33), channel_id=1, source_target_pairs={{0,12},{2,14},{4,8},{6,10},{8,4},{10,6},{12,0},{14,2},{1,13},{3,15... | collective-permute-start | bytes 589832 | tf_op jit(solution)/shard_map/ppermute | solution.py:302
  20.3 36.3 %collective-permute-start.7 = (bf16[2,192,256]{2,1,0:T(8,128)(2,1)S(1)}, bf16[2,192,256]{2,1,0:T(8,128)(2,1)S(1)}, u32[]{:S(2)}, u32[]{:S(2)}) collective-permute-start(bf16[2,192,256]{2,1,0:T(8,128)(2,1)S(1)} %get-tuple-element.34), channel_id=1, source_target_pairs={{0,14},{2,12},{4,10},{6,8},{8,6},{10,4},{12,2},{14,0},{1,15},{3,13... | collective-permute-start | bytes 589832 | tf_op jit(solution)/shard_map/ppermute | solution.py:302
  27.5 29.0 %collective-permute-start.1 = (bf16[2,192,256]{2,1,0:T(8,128)(2,1)S(1)}, bf16[2,192,256]{2,1,0:T(8,128)(2,1)S(1)}, u32[]{:S(2)}, u32[]{:S(2)}) collective-permute-start(bf16[2,192,256]{2,1,0:T(8,128)(2,1)S(1)} %get-tuple-element.28), channel_id=1, source_target_pairs={{0,2},{2,0},{4,6},{6,4},{8,10},{10,8},{12,14},{14,12},{1,3},{3,1},... | collective-permute-start | bytes 589832 | tf_op jit(solution)/shard_map/ppermute | solution.py:302
  38.0 18.5 %collective-permute-start.2 = (bf16[2,192,256]{2,1,0:T(8,128)(2,1)S(1)}, bf16[2,192,256]{2,1,0:T(8,128)(2,1)S(1)}, u32[]{:S(2)}, u32[]{:S(2)}) collective-permute-start(bf16[2,192,256]{2,1,0:T(8,128)(2,1)S(1)} %get-tuple-element.29), channel_id=1, source_target_pairs={{0,4},{2,6},{4,0},{6,2},{8,12},{10,14},{12,8},{14,10},{1,5},{3,7},... | collective-permute-start | bytes 589832 | tf_op jit(solution)/shard_map/ppermute | solution.py:302
  42.3 14.3 %collective-permute-start.3 = (bf16[2,192,256]{2,1,0:T(8,128)(2,1)S(1)}, bf16[2,192,256]{2,1,0:T(8,128)(2,1)S(1)}, u32[]{:S(2)}, u32[]{:S(2)}) collective-permute-start(bf16[2,192,256]{2,1,0:T(8,128)(2,1)S(1)} %get-tuple-element.30), channel_id=1, source_target_pairs={{0,6},{2,4},{4,2},{6,0},{8,14},{10,12},{12,10},{14,8},{1,7},{3,5},... | collective-permute-start | bytes 589832 | tf_op jit(solution)/shard_map/ppermute | solution.py:302

commit v2 on v1

--- a/solution.py
+++ b/solution.py
@@ -40,12 +40,12 @@
         sin_ref[rows, :] = sine
 
 
-def project(h_ref, gain_ref, wk_ref, wv_ref, acc_k, acc_v, squares, chunk, ready=None):
+def project(h_ref, rows, gain_ref, wk_ref, wv_ref, acc_k, acc_v, squares, chunk, ready=None):
     for c in range(h_ref.shape[1] // chunk):
         if ready is not None:
             ready(c)
         at = slice(c * chunk, (c + 1) * chunk)
-        h = h_ref[:, at]
+        h = h_ref[rows, at]
         scaled = h * gain_ref[:, at]
         key = jnp.dot(scaled, wk_ref[at, :], preferred_element_type=jnp.float32)
         value = jnp.dot(scaled, wv_ref[at, :], preferred_element_type=jnp.float32)
@@ -93,7 +93,7 @@
     rotation_tables(block, offset_ref, cos_pad, sin_pad)
     cos_ref[...] = cos_pad[: cos_ref.shape[0], :]
     sin_ref[...] = sin_pad[: sin_ref.shape[0], :]
-    project(h_ref, gain_ref, wk_ref, wv_ref, acc_k, acc_v, squares, chunk, ready)
+    project(h_ref, slice(None), gain_ref, wk_ref, wv_ref, acc_k, acc_v, squares, chunk, ready)
     here = pl.ds(pl.multiple_of(lax.axis_index("tensor") * rows, rows), rows)
     keys, values = finish(width, cos_pad[here, :], sin_pad[here, :], acc_k, acc_v, squares)
     out_ref[:, :cols] = keys
@@ -158,6 +158,53 @@
     out_ref[1] = picked[:, cols:]
 
 
+def first_kernel(
+    owner, block, chunk, offset_ref, length_ref, owner_ref, slot_ref,
+    h_ref, wk_ref, wv_ref, gain_ref, cos_ref, sin_ref, own_ref, block_ref, kv, acc_k, acc_v, squares
+):
+    rows, width = h_ref.shape
+    cols = acc_k.shape[1]
+    span = acc_k.shape[0]
+    mine = lax.axis_index("tensor")
+    owner = jnp.bitwise_xor(lax.axis_index("dp"), owner)
+    here = pl.ds(pl.multiple_of(mine * rows, rows), rows)
+    kv[here, :] = own_ref[...]
+    offset = jnp.int32(0)
+    for s in range(owner_ref.shape[1]):
+        offset = jnp.where(owner_ref[0, s] == owner, offset_ref[0, s], offset)
+    start = jnp.minimum((offset // 16) * 16, 2 * rows - span)
+    local = pl.multiple_of(jnp.clip(start - (1 - mine) * rows, 0, rows - span), 16)
+    there = pl.ds(pl.multiple_of((1 - mine) * rows + local, 16), span)
+    project(h_ref, pl.ds(local, span), gain_ref, wk_ref, wv_ref, acc_k, acc_v, squares, chunk)
+    keys, values = finish(width, cos_ref[there, :], sin_ref[there, :], acc_k, acc_v, squares)
+    kv[there, :cols] = keys
+    kv[there, cols:] = values
+    select_block(block, cols, owner, (offset_ref, length_ref, owner_ref, slot_ref), kv, block_ref)
+
+
+def first_block(owner, block, places, peer, wk, wv, gain, cosine, sine, own, chunk=1024):
+    rows, width = peer.shape
+    cols = wk.shape[1]
+    span = block + 16
+    return pl.pallas_call(
+        functools.partial(first_kernel, owner, block, chunk),
+        in_specs=[SMEM] * 4 + [VMEM] * 7,
+        out_specs=VMEM,
+        out_shape=jax.ShapeDtypeStruct((2, block, cols), jnp.bfloat16),
+        scratch_shapes=[
+            pltpu.VMEM((2 * rows, 2 * cols), jnp.bfloat16),
+            pltpu.VMEM((span, cols), jnp.float32),
+            pltpu.VMEM((span, cols), jnp.float32),
+            pltpu.VMEM((span, HD), jnp.float32),
+        ],
+        compiler_params=pltpu.CompilerParams(vmem_limit_bytes=28 * MIB),
+        cost_estimate=pl.CostEstimate(
+            flops=4 * span * width * cols, bytes_accessed=2 * (span * width + 2 * width * cols), transcendentals=0
+        ),
+        name="first_block",
+    )(*places, peer, wk, wv, gain, cosine, sine, own)
+
+
 def peer_kernel(
     far, block, chunk, offset_ref, length_ref, owner_ref, slot_ref,
     h_ref, wk_ref, wv_ref, gain_ref, cos_ref, sin_ref, own_ref, kv_ref, *rest
@@ -168,7 +215,7 @@
     mine = lax.axis_index("tensor")
     there = pl.ds(pl.multiple_of((1 - mine) * rows, rows), rows)
     here = pl.ds(pl.multiple_of(mine * rows, rows), rows)
-    project(h_ref, gain_ref, wk_ref, wv_ref, acc_k, acc_v, squares, chunk)
+    project(h_ref, slice(None), gain_ref, wk_ref, wv_ref, acc_k, acc_v, squares, chunk)
     keys, values = finish(width, cos_ref[there, :], sin_ref[there, :], acc_k, acc_v, squares)
     kv_ref[there, :cols] = keys
     kv_ref[there, cols:] = values
@@ -201,27 +248,15 @@
     )(*places, peer, wk, wv, gain, cosine, sine, own)
 
 
-def attend_kernel(tile, window, skipped, near, block, *refs):
-    places, (q_ref, kv_ref), rest = refs[:4], refs[4:6], refs[6:]
-    if skipped:
-        rest = rest[1:]
-    out_ref, blocks = rest[0], rest[1:]
-    step = pl.program_id(0)
+def attend_kernel(tile, window, offset_ref, q_ref, kv_ref, out_ref):
     cols = kv_ref.shape[1] // 2
     groups = cols // HD
     heads = q_ref.shape[1] // HD // groups
-
-    if near:
-        @pl.when(step == 0)
-        def _():
-            for k, block_ref in zip(near, blocks):
-                select_block(block, cols, jnp.bitwise_xor(lax.axis_index("dp"), k), places, kv_ref, block_ref)
-
-    first = (step + skipped) * tile
+    first = pl.program_id(0) * tile
     start = pl.multiple_of(jnp.maximum(first + tile - window, 0), 16)
     row = first + lax.broadcasted_iota(jnp.int32, (tile, window), 0)
     key = start + lax.broadcasted_iota(jnp.int32, (tile, window), 1)
-    allowed = (key <= row) & (key >= prompt_start(row, places[0]))
+    allowed = (key <= row) & (key >= prompt_start(row, offset_ref))
     bias = jnp.where(allowed, 0.0, -1e30)[None]
     ones = jnp.ones((window, HD), jnp.bfloat16)
     scale = HD**-0.5 * float(np.log2(np.e))
@@ -240,41 +275,34 @@
             out_ref[:, a] = result[h * tile : (h + 1) * tile]
 
 
-def attend(places, queries, kv, longest, near=(), before=None, tile=64):
+def attend(offsets, queries, kv, longest, tile=64):
     rows, width = queries.shape
     window = tile + longest
-    steps = rows // tile // 2
-    skipped = 0 if before is None else steps
-    cols = kv.shape[1] // 2
-    rows_at = pl.BlockSpec((tile, width), lambda i: (i + skipped, 0))
+    rows_at = pl.BlockSpec((tile, width), lambda i: (i, 0))
     return pl.pallas_call(
-        functools.partial(attend_kernel, tile, window, skipped, near, longest),
-        grid=(steps,),
-        in_specs=[SMEM] * 4
-        + [rows_at, pl.BlockSpec(kv.shape, lambda i: (0, 0))]
-        + ([pl.BlockSpec(memory_space=pl.ANY)] if skipped else []),
-        out_specs=[rows_at] + [pl.BlockSpec((2, longest, cols), lambda i: (0, 0, 0))] * len(near),
-        out_shape=[jax.ShapeDtypeStruct((rows, width), jnp.bfloat16)]
-        + [jax.ShapeDtypeStruct((2, longest, cols), jnp.bfloat16)] * len(near),
-        input_output_aliases={6: 0} if skipped else {},
+        functools.partial(attend_kernel, tile, window),
+        grid=(rows // tile,),
+        in_specs=[SMEM, rows_at, pl.BlockSpec(kv.shape, lambda i: (0, 0))],
+        out_specs=rows_at,
+        out_shape=jax.ShapeDtypeStruct((rows, width), jnp.bfloat16),
         compiler_params=pltpu.CompilerParams(vmem_limit_bytes=32 * MIB),
         cost_estimate=pl.CostEstimate(
-            flops=2 * rows * width * window,
-            bytes_accessed=2 * rows * width,
-            transcendentals=rows * window * width // HD // 2,
+            flops=4 * rows * width * window,
+            bytes_accessed=4 * rows * width,
+            transcendentals=rows * window * width // HD,
         ),
-        name="attend_rest" if skipped else "attend_first",
-    )(*places, queries, kv, *([before] if skipped else []))
-
-
-def gather_kernel(n_dp, block, *refs):
-    blocks, (key_ref, value_ref, sems) = refs[:n_dp], refs[n_dp:]
+        name="attend",
+    )(offsets, queries, kv)
+
+
+def gather_kernel(order, block, *refs):
+    blocks, (key_ref, value_ref, sems) = refs[: len(order)], refs[len(order) :]
     me = lax.axis_index("dp")
     copies = []
-    for k in range(n_dp):
+    for i, k in enumerate(order):
         rows = pl.ds(pl.multiple_of(jnp.bitwise_xor(me, k) * block, block), block)
         for n, out_ref in enumerate((key_ref, value_ref)):
-            copies.append(pltpu.make_async_copy(blocks[k].at[n], out_ref.at[rows, :], sems.at[k, n]))
+            copies.append(pltpu.make_async_copy(blocks[i].at[n], out_ref.at[rows, :], sems.at[i, n]))
     for copy in copies:
         copy.start()
     for copy in copies:
@@ -297,25 +325,28 @@
         block, prompt_offsets, hidden, key_weight, value_weight, gain, tok_rows
     )
     places = [prompt_offsets, prompt_lengths, decode_owner, slot_offsets]
-    far = tuple(range(n_dp // 2, n_dp))
-    near = tuple(range(n_dp // 2))
-    swap = lambda a, k: a if k == 0 else lax.ppermute(a, "dp", [(p, p ^ k) for p in range(n_dp)])
-    kv, *blocks = peer_rows(far, block, places, peer, wk, wv, gain, cosine, sine, own)
-    received = {k: swap(a, k) for k, a in zip(far, blocks)}
-    attended, *blocks = attend(places, queries, kv, block, near)
-    received.update({k: swap(a, k) for k, a in zip(near, blocks)})
-    attended = attend(places, queries, kv, block, (), attended)[0]
+    swap = lambda a, k: lax.ppermute(a, "dp", [(p, p ^ k) for p in range(n_dp)]) if k else a
+    half_dp = n_dp // 2
+    far = list(range(half_dp, n_dp))
+    near = list(range(1, half_dp))
+    order = (far[0], far[1], *near[1:], *far[2:], near[0], 0)
+    first = first_block(order[0], block, places, peer, wk, wv, gain, cosine, sine, own)
+    kv, *blocks = peer_rows(order[1:], block, places, peer, wk, wv, gain, cosine, sine, own)
+    first = swap(first, order[0])
+    first, *blocks[4:-1] = lax.optimization_barrier((first, *blocks[4:-1]))
+    received = [first] + [swap(a, k) for k, a in zip(order[1:], blocks)]
+    attended = attend(prompt_offsets, queries, kv, block)
     cache = jax.ShapeDtypeStruct((n_dp * block, cols), jnp.bfloat16)
     anywhere = pl.BlockSpec(memory_space=pl.ANY)
     key_cache, value_cache = pl.pallas_call(
-        functools.partial(gather_kernel, n_dp, block),
+        functools.partial(gather_kernel, order, block),
         in_specs=[VMEM] * n_dp,
         out_specs=[anywhere] * 2,
         out_shape=[cache, cache],
         scratch_shapes=[pltpu.SemaphoreType.DMA((n_dp, 2))],
         compiler_params=pltpu.CompilerParams(vmem_limit_bytes=8 * MIB),
         name="place_blocks",
-    )(*[received[k] for k in range(n_dp)])
+    )(*received)
     return attended, key_cache[None], value_cache[None]
 
 

time: 58.3 us -> 54.2 us (0.930)
  starting transfers between devices: 16.7 us -> 13.5 us
  waiting for transfers between devices: 15.3 us -> 13 us
  Pallas kernels: 23.7 us -> 25.1 us
    ppermute x7, starting transfers between devices: 16.7 us -> 13.4 us  [on_device(): lax.ppermute(a, 'dp', [(p, p ^ k) for p in range(n_dp)])]
    ppermute x7, waiting for transfers between devices: 13 us -> 10.7 us  [on_device(): lax.ppermute(a, 'dp', [(p, p ^ k) for p in range(n_dp)])]
    pallas_call x3, Pallas kernels: 12.3 us -> 13.5 us  [the longest x1 9.32 us: attend(): pl.pallas_call(functools.partial(attend_kernel, tile, window), grid=(rows...]
  transfers between devices with their start and end apart: 8 -> 8, of which waited for: 4 -> 5; matrix products, arithmetic and copies ran while one was open for 1% -> 1% of each run, Pallas kernels for 30% -> 39%
where the time goes in v2:
time: 54.2 us; the launch traced here: 53.7 us
  Pallas kernels  25.1 us (46%)
  starting transfers between devices  13.5 us (25%)
  waiting for transfers between devices  13 us (24%)
  local copies, waits for them, and re-layouts  1.41 us (3%)
  between operations  0.7 us (1%)
    ppermute x7, starting transfers between devices, on_device(): lax.ppermute(a, 'dp', [(p, p ^ k) for p in range(n_dp)])  13.4 us
    ppermute x7, waiting for transfers between devices, on_device(): lax.ppermute(a, 'dp', [(p, p ^ k) for p in range(n_dp)])  10.7 us
    pallas_call x1, Pallas kernels, attend(): pl.pallas_call(functools.partial(attend_kernel, tile, window), grid=(rows...  9.32 us
    pallas_call x1, Pallas kernels, own_rows(): pl.pallas_call(functools.partial(own_kernel, block, chunk), in_specs=[SME...  6.63 us
    pallas_call x1, Pallas kernels, peer_rows(): pl.pallas_call(functools.partial(peer_kernel, far, block, chunk), in_spec...  4.93 us
    pallas_call x1, Pallas kernels, first_block(): pl.pallas_call(functools.partial(first_kernel, owner, block, chunk), in_s...  2.95 us
    ppermute x1, waiting for transfers between devices, on_device(): peer = lax.ppermute(hidden, 'tensor', [(0, 1), (1, 0)])  2.31 us
    pallas_call x1, Pallas kernels, on_device(): pl.pallas_call(functools.partial(gather_kernel, order, block), in_specs=[...  1.26 us
  transfers between devices with their start and end apart: 8, of which 5 were waited for; matrix products, arithmetic and copies ran while one was open for 1% of the time, Pallas kernels for 39%

profile of v2, /device:TPU:16, one launch (start us, length us, event | category | flops | bytes accessed | tf_op | source)
XLA Modules:
  0.0 53.7 jit_solution(1364782419305372310)
XLA Ops:
  0.6 0.1 collective-permute-start
  0.7 0.7 %reshape.9.gain_ref = bf16[1,8192]{1,0:T(2,128)(2,1)S(1)} reshape(bf16[8192]{0:T(1024)(128)(2,1)} %param.11) | data formatting | bytes 32768 | tf_op jit(solution)/shard_map/reshape | solution.py:321
  1.5 0.0 copy-start.1
  1.5 0.6 %copy-done.1 = s32[1,8]{1,0:T(1,128)S(1)} copy-done((s32[1,8]{1,0:T(1,128)S(1)}, s32[1,8]{1,0:T(1,128)}, u32[]{:S(2)}) %copy-start.1) | copy-done | bytes 56
  2.1 6.6 %own_rows.1 = (bf16[384,512]{1,0:T(8,128)(2,1)S(1)}, f32[768,128]{1,0:T(8,128)S(1)}, f32[768,128]{1,0:T(8,128)S(1)}, bf16[8192,256]{1,0:T(8,128)(2,1)S(1)}, bf16[8192,256]{1,0:T(8,128)(2,1)S(1)}) custom-call(s32[1,8]{1,0:T(1,128)S(1)} %copy-done.1, bf16[384,8192]{1,0:T(8,128)(2,1)} %h_hbm.1, bf16[8192,256]{1,0:T(8,128)(2,1)} %wk_hbm.1, ...), custom_call_target="tpu_custom_call" | custom-call | flops 3221225472 | bytes 14680064 | tf_op jit(solution)/shard_map/own_rows/pallas_call | solution.py:108
  8.8 2.3 %collective-permute-done.h_ref = bf16[384,8192]{1,0:T(8,128)(2,1)S(1)} collective-permute-done((bf16[384,8192]{1,0:T(8,128)(2,1)}, bf16[384,8192]{1,0:T(8,128)(2,1)S(1)}, u32[]{:S(2)}, u32[]{:S(2)}) %collective-permute-start) | collective-permute-done | bytes 6291488 | tf_op jit(solution)/shard_map/ppermute | solution.py:323
  11.1 3.0 %first_block.1 = bf16[2,192,256]{2,1,0:T(8,128)(2,1)S(1)} custom-call(s32[1,8]{1,0:T(1,128)S(1)} %copy-done.1, s32[1,8]{1,0:T(1,128)S(1)} %copy-done.2, s32[1,8]{1,0:T(1,128)S(1)} %copy-done.3, s32[1,8]{1,0:T(1,128)S(1)} %copy-done.4, bf16[384,8192]{1,0:T(8,128)(2,1)S(1)} %collective-permute-done.h_ref, bf16[8192,256]{1,0:T(8,128)(2,1)S(1)} %get-tuple-element.21.wk_ref, ...), custom_call_target="tpu_custom_call" | custom-call | flops 1744830464 | bytes 11796480 | tf_op jit(solution)/shard_map/first_block/pallas_call | solution.py:189
  14.0 0.0 copy-start
  14.0 0.1 collective-permute-start.1
  14.1 4.9 %peer_rows.1 = (bf16[768,512]{1,0:T(8,128)(2,1)S(1)}, bf16[2,192,256]{2,1,0:T(8,128)(2,1)S(1)}, bf16[2,192,256]{2,1,0:T(8,128)(2,1)S(1)}, bf16[2,192,256]{2,1,0:...) custom-call(s32[1,8]{1,0:T(1,128)S(1)} %copy-done.1, ...), custom_call_target="tpu_custom_call" | custom-call | flops 3221225472 | bytes 14680064 | tf_op jit(solution)/shard_map/peer_rows/pallas_call | solution.py:232
  19.1 3.9 %collective-permute-start.2 = (bf16[2,192,256]{2,1,0:T(8,128)(2,1)S(1)}, bf16[2,192,256]{2,1,0:T(8,128)(2,1)S(1)}, u32[]{:S(2)}, u32[]{:S(2)}) collective-permute-start(bf16[2,192,256]{2,1,0:T(8,128)(2,1)S(1)} %get-tuple-element.30), channel_id=1, source_target_pairs={{0,10},{2,8},{4,14},{6,12},{8,2},{10,0},{12,6},{14,4},{1,11},{3,9}... | collective-permute-start | bytes 589832 | tf_op jit(solution)/shard_map/ppermute | solution.py:328
  23.0 1.6 %collective-permute-start.3 = (bf16[2,192,256]{2,1,0:T(8,128)(2,1)S(1)}, bf16[2,192,256]{2,1,0:T(8,128)(2,1)S(1)}, u32[]{:S(2)}, u32[]{:S(2)}) collective-permute-start(bf16[2,192,256]{2,1,0:T(8,128)(2,1)S(1)} %get-tuple-element.31), channel_id=1, source_target_pairs={{0,4},{2,6},{4,0},{6,2},{8,12},{10,14},{12,8},{14,10},{1,5},{3,7},... | collective-permute-start | bytes 589832 | tf_op jit(solution)/shard_map/ppermute | solution.py:328
  24.6 0.4 collective-permute-start.4
  25.0 0.4 collective-permute-start.5
  25.4 5.6 %collective-permute-start.6 = (bf16[2,192,256]{2,1,0:T(8,128)(2,1)S(1)}, bf16[2,192,256]{2,1,0:T(8,128)(2,1)S(1)}, u32[]{:S(2)}, u32[]{:S(2)}) collective-permute-start(bf16[2,192,256]{2,1,0:T(8,128)(2,1)S(1)} %get-tuple-element.34), channel_id=1, source_target_pairs={{0,14},{2,12},{4,10},{6,8},{8,6},{10,4},{12,2},{14,0},{1,15},{3,13... | collective-permute-start | bytes 589832 | tf_op jit(solution)/shard_map/ppermute | solution.py:328
  31.0 1.5 %collective-permute-done.2.refs_1_ = bf16[2,192,256]{2,1,0:T(8,128)(2,1)S(1)} collective-permute-done((bf16[2,192,256]{2,1,0:T(8,128)(2,1)S(1)}, bf16[2,192,256]{2,1,0:T(8,128)(2,1)S(1)}, u32[]{:S(2)}, u32[]{:S(2)}) %collective-permute-start.2) | collective-permute-done | bytes 196640 | tf_op jit(solution)/shard_map/ppermute | solution.py:328
  32.5 1.4 %collective-permute-start.7 = (bf16[2,192,256]{2,1,0:T(8,128)(2,1)S(1)}, bf16[2,192,256]{2,1,0:T(8,128)(2,1)S(1)}, u32[]{:S(2)}, u32[]{:S(2)}) collective-permute-start(bf16[2,192,256]{2,1,0:T(8,128)(2,1)S(1)} %get-tuple-element.35), channel_id=1, source_target_pairs={{0,2},{2,0},{4,6},{6,4},{8,10},{10,8},{12,14},{14,12},{1,3},{3,1},... | collective-permute-start | bytes 589832 | tf_op jit(solution)/shard_map/ppermute | solution.py:328
  33.9 9.3 %attend.1 = bf16[768,2048]{1,0:T(8,128)(2,1)} custom-call(s32[1,8]{1,0:T(1,128)S(1)} %copy-done.1, bf16[768,2048]{1,0:T(8,128)(2,1)S(1)} %copy-done, bf16[768,512]{1,0:T(8,128)(2,1)S(1)} %get-tuple-element.26.kv_ref), custom_call_target="tpu_custom_call" | custom-call | flops 1610612736 | bytes 6291456 | tf_op jit(solution)/shard_map/attend/pallas_call | solution.py:282
  43.3 1.7 %collective-permute-done.3.refs_2_ = bf16[2,192,256]{2,1,0:T(8,128)(2,1)S(1)} collective-permute-done((bf16[2,192,256]{2,1,0:T(8,128)(2,1)S(1)}, bf16[2,192,256]{2,1,0:T(8,128)(2,1)S(1)}, u32[]{:S(2)}, u32[]{:S(2)}) %collective-permute-start.3) | collective-permute-done | bytes 196640 | tf_op jit(solution)/shard_map/ppermute | solution.py:328
  44.9 2.8 %collective-permute-done.4.refs_3_ = bf16[2,192,256]{2,1,0:T(8,128)(2,1)S(1)} collective-permute-done((bf16[2,192,256]{2,1,0:T(8,128)(2,1)S(1)}, bf16[2,192,256]{2,1,0:T(8,128)(2,1)S(1)}, u32[]{:S(2)}, u32[]{:S(2)}) %collective-permute-start.4) | collective-permute-done | bytes 196640 | tf_op jit(solution)/shard_map/ppermute | solution.py:328
  47.7 0.0 collective-permute-done.5.refs_4_
  47.7 4.8 %collective-permute-done.6.refs_5_ = bf16[2,192,256]{2,1,0:T(8,128)(2,1)S(1)} collective-permute-done((bf16[2,192,256]{2,1,0:T(8,128)(2,1)S(1)}, bf16[2,192,256]{2,1,0:T(8,128)(2,1)S(1)}, u32[]{:S(2)}, u32[]{:S(2)}) %collective-permute-start.6) | collective-permute-done | bytes 196640 | tf_op jit(solution)/shard_map/ppermute | solution.py:328
  52.5 0.0 collective-permute-done.7.refs_6_
  52.5 1.3 %place_blocks.1 = (bf16[1536,256]{1,0:T(8,128)(2,1)}, bf16[1536,256]{1,0:T(8,128)(2,1)}) custom-call(bf16[2,192,256]{2,1,0:T(8,128)(2,1)S(1)} %collective-permute-done.1.refs_0_, bf16[2,192,256]{2,1,0:T(8,128)(2,1)S(1)} %collective-permute-done.2.refs_1_, bf16[2,192,256]{2,1,0:T(8,128)(2,1)S(1)} %collective-permute-done.3.refs_2_, ...), custom_call_target="tpu_custom_call" | custom-call | tf_op jit(solution)/shard_map/place_blocks/pallas_call | solution.py:341
  (8 shorter events, 0.0 us)
Async XLA Ops:
  0.6 10.4 %collective-permute-start = (bf16[384,8192]{1,0:T(8,128)(2,1)}, bf16[384,8192]{1,0:T(8,128)(2,1)S(1)}, u32[]{:S(2)}, u32[]{:S(2)}) collective-permute-start(bf16[384,8192]{1,0:T(8,128)(2,1)} %h_hbm.1), channel_id=1, source_target_pairs={{0,1},{1,0},{2,3},{3,2},{4,5},{5,4},{6,7},{7,6},{8,9},{9,8},{10,11... | collective-permute-start | bytes 18874376 | tf_op jit(solution)/shard_map/ppermute | solution.py:323
  1.5 0.7 %copy-start.1 = (s32[1,8]{1,0:T(1,128)S(1)}, s32[1,8]{1,0:T(1,128)}, u32[]{:S(2)}) copy-start(s32[1,8]{1,0:T(1,128)} %offset_ref.7) | copy-start | bytes 100
  2.1 9.0 %copy-start.2 = (s32[1,8]{1,0:T(1,128)S(1)}, s32[1,8]{1,0:T(1,128)}, u32[]{:S(2)}) copy-start(s32[1,8]{1,0:T(1,128)} %length_ref.3) | copy-start | bytes 100
  2.1 9.0 %copy-start.3 = (s32[1,8]{1,0:T(1,128)S(1)}, s32[1,8]{1,0:T(1,128)}, u32[]{:S(2)}) copy-start(s32[1,8]{1,0:T(1,128)} %owner_ref.3) | copy-start | bytes 100
  2.1 9.0 %copy-start.4 = (s32[1,8]{1,0:T(1,128)S(1)}, s32[1,8]{1,0:T(1,128)}, u32[]{:S(2)}) copy-start(s32[1,8]{1,0:T(1,128)} %slot_ref.3) | copy-start | bytes 100
  14.0 19.9 %copy-start = (bf16[768,2048]{1,0:T(8,128)(2,1)S(1)}, bf16[768,2048]{1,0:T(8,128)(2,1)}, u32[]{:S(2)}) copy-start(bf16[768,2048]{1,0:T(8,128)(2,1)} %q_ref.1) | copy-start | bytes 9437188
  14.0 11.4 %collective-permute-start.1 = (bf16[2,192,256]{2,1,0:T(8,128)(2,1)S(1)}, bf16[2,192,256]{2,1,0:T(8,128)(2,1)S(1)}, u32[]{:S(2)}, u32[]{:S(2)}) collective-permute-start(bf16[2,192,256]{2,1,0:T(8,128)(2,1)S(1)} %first_block.1), channel_id=1, source_target_pairs={{0,8},{2,10},{4,12},{6,14},{8,0},{10,2},{12,4},{14,6},{1,9},{3,11}... | collective-permute-start | bytes 589832 | tf_op jit(solution)/shard_map/ppermute | solution.py:328
  19.1 13.5 %collective-permute-start.2 = (bf16[2,192,256]{2,1,0:T(8,128)(2,1)S(1)}, bf16[2,192,256]{2,1,0:T(8,128)(2,1)S(1)}, u32[]{:S(2)}, u32[]{:S(2)}) collective-permute-start(bf16[2,192,256]{2,1,0:T(8,128)(2,1)S(1)} %get-tuple-element.30), channel_id=1, source_target_pairs={{0,10},{2,8},{4,14},{6,12},{8,2},{10,0},{12,6},{14,4},{1,11},{3,9}... | collective-permute-start | bytes 589832 | tf_op jit(solution)/shard_map/ppermute | solution.py:328
  23.0 21.9 %collective-permute-start.3 = (bf16[2,192,256]{2,1,0:T(8,128)(2,1)S(1)}, bf16[2,192,256]{2,1,0:T(8,128)(2,1)S(1)}, u32[]{:S(2)}, u32[]{:S(2)}) collective-permute-start(bf16[2,192,256]{2,1,0:T(8,128)(2,1)S(1)} %get-tuple-element.31), channel_id=1, source_target_pairs={{0,4},{2,6},{4,0},{6,2},{8,12},{10,14},{12,8},{14,10},{1,5},{3,7},... | collective-permute-start | bytes 589832 | tf_op jit(solution)/shard_map/ppermute | solution.py:328
  24.6 23.1 %collective-permute-start.4 = (bf16[2,192,256]{2,1,0:T(8,128)(2,1)S(1)}, bf16[2,192,256]{2,1,0:T(8,128)(2,1)S(1)}, u32[]{:S(2)}, u32[]{:S(2)}) collective-permute-start(bf16[2,192,256]{2,1,0:T(8,128)(2,1)S(1)} %get-tuple-element.32), channel_id=1, source_target_pairs={{0,6},{2,4},{4,2},{6,0},{8,14},{10,12},{12,10},{14,8},{1,7},{3,5},... | collective-permute-start | bytes 589832 | tf_op jit(solution)/shard_map/ppermute | solution.py:328
  25.0 22.7 %collective-permute-start.5 = (bf16[2,192,256]{2,1,0:T(8,128)(2,1)S(1)}, bf16[2,192,256]{2,1,0:T(8,128)(2,1)S(1)}, u32[]{:S(2)}, u32[]{:S(2)}) collective-permute-start(bf16[2,192,256]{2,1,0:T(8,128)(2,1)S(1)} %get-tuple-element.33), channel_id=1, source_target_pairs={{0,12},{2,14},{4,8},{6,10},{8,4},{10,6},{12,0},{14,2},{1,13},{3,15... | collective-permute-start | bytes 589832 | tf_op jit(solution)/shard_map/ppermute | solution.py:328
  25.4 27.0 %collective-permute-start.6 = (bf16[2,192,256]{2,1,0:T(8,128)(2,1)S(1)}, bf16[2,192,256]{2,1,0:T(8,128)(2,1)S(1)}, u32[]{:S(2)}, u32[]{:S(2)}) collective-permute-start(bf16[2,192,256]{2,1,0:T(8,128)(2,1)S(1)} %get-tuple-element.34), channel_id=1, source_target_pairs={{0,14},{2,12},{4,10},{6,8},{8,6},{10,4},{12,2},{14,0},{1,15},{3,13... | collective-permute-start | bytes 589832 | tf_op jit(solution)/shard_map/ppermute | solution.py:328
  32.5 19.9 %collective-permute-start.7 = (bf16[2,192,256]{2,1,0:T(8,128)(2,1)S(1)}, bf16[2,192,256]{2,1,0:T(8,128)(2,1)S(1)}, u32[]{:S(2)}, u32[]{:S(2)}) collective-permute-start(bf16[2,192,256]{2,1,0:T(8,128)(2,1)S(1)} %get-tuple-element.35), channel_id=1, source_target_pairs={{0,2},{2,0},{4,6},{6,4},{8,10},{10,8},{12,14},{14,12},{1,3},{3,1},... | collective-permute-start | bytes 589832 | tf_op jit(solution)/shard_map/ppermute | solution.py:328

commit v3 on v2

--- a/solution.py
+++ b/solution.py
@@ -296,17 +296,32 @@
 
 
 def gather_kernel(order, block, *refs):
-    blocks, (key_ref, value_ref, sems) = refs[: len(order)], refs[len(order) :]
+    key_ref, value_ref, sems = refs[-3:]
     me = lax.axis_index("dp")
     copies = []
     for i, k in enumerate(order):
         rows = pl.ds(pl.multiple_of(jnp.bitwise_xor(me, k) * block, block), block)
         for n, out_ref in enumerate((key_ref, value_ref)):
-            copies.append(pltpu.make_async_copy(blocks[i].at[n], out_ref.at[rows, :], sems.at[i, n]))
+            copies.append(pltpu.make_async_copy(refs[i].at[n], out_ref.at[rows, :], sems.at[i, n]))
     for copy in copies:
         copy.start()
     for copy in copies:
         copy.wait()
+
+
+def place(order, block, blocks, cache, before=()):
+    n = len(order)
+    anywhere = pl.BlockSpec(memory_space=pl.ANY)
+    return pl.pallas_call(
+        functools.partial(gather_kernel, order, block),
+        in_specs=[VMEM] * n + [anywhere] * len(before),
+        out_specs=[anywhere] * 2,
+        out_shape=[cache, cache],
+        input_output_aliases={n: 0, n + 1: 1} if before else {},
+        scratch_shapes=[pltpu.SemaphoreType.DMA((n, 2))],
+        compiler_params=pltpu.CompilerParams(vmem_limit_bytes=8 * MIB),
+        name="place_rest" if before else "place_first",
+    )(*blocks, *before)
 
 
 def on_device(
@@ -329,7 +344,7 @@
     half_dp = n_dp // 2
     far = list(range(half_dp, n_dp))
     near = list(range(1, half_dp))
-    order = (far[0], far[1], *near[1:], *far[2:], near[0], 0)
+    order = (far[2], far[1], *near[1:], far[0], *far[3:], near[0], 0)
     first = first_block(order[0], block, places, peer, wk, wv, gain, cosine, sine, own)
     kv, *blocks = peer_rows(order[1:], block, places, peer, wk, wv, gain, cosine, sine, own)
     first = swap(first, order[0])
@@ -337,16 +352,11 @@
     received = [first] + [swap(a, k) for k, a in zip(order[1:], blocks)]
     attended = attend(prompt_offsets, queries, kv, block)
     cache = jax.ShapeDtypeStruct((n_dp * block, cols), jnp.bfloat16)
-    anywhere = pl.BlockSpec(memory_space=pl.ANY)
-    key_cache, value_cache = pl.pallas_call(
-        functools.partial(gather_kernel, order, block),
-        in_specs=[VMEM] * n_dp,
-        out_specs=[anywhere] * 2,
-        out_shape=[cache, cache],
-        scratch_shapes=[pltpu.SemaphoreType.DMA((n_dp, 2))],
-        compiler_params=pltpu.CompilerParams(vmem_limit_bytes=8 * MIB),
-        name="place_blocks",
-    )(*received)
+    by_place = dict(zip(order, received))
+    early = (0, *order[: n_dp // 2 + 1])
+    late = tuple(k for k in order if k not in early)
+    caches = place(early, block, [by_place[k] for k in early], cache)
+    key_cache, value_cache = place(late, block, [by_place[k] for k in late], cache, caches)
     return attended, key_cache[None], value_cache[None]
 
 

time: 54.2 us -> 52.6 us (0.970)
  starting transfers between devices: 13.5 us -> 10.8 us
  waiting for transfers between devices: 13 us -> 13.7 us
  Pallas kernels: 25.1 us -> 25.7 us
    ppermute x7, starting transfers between devices: 13.4 us -> 10.8 us  [on_device(): lax.ppermute(a, 'dp', [(p, p ^ k) for p in range(n_dp)])]
    ppermute x7, waiting for transfers between devices: 10.7 us -> 11.4 us  [on_device(): lax.ppermute(a, 'dp', [(p, p ^ k) for p in range(n_dp)])]
    pallas_call x1 -> x2, Pallas kernels: 1.26 us -> 1.89 us  [place(): pl.pallas_call(functools.partial(gather_kernel, order, block), in_specs=[...]
  transfers between devices with their start and end apart: 8 -> 8, of which waited for: 5 -> 4; matrix products, arithmetic and copies ran while one was open for 1% -> 1% of each run, Pallas kernels for 39% -> 42%
where the time goes in v3:
time: 52.6 us; the launch traced here: 52.3 us
  Pallas kernels  25.7 us (49%)
  waiting for transfers between devices  13.7 us (26%)
  starting transfers between devices  10.8 us (21%)
  local copies, waits for them, and re-layouts  1.41 us (3%)
  between operations  0.7 us (1%)
    ppermute x7, waiting for transfers between devices, on_device(): lax.ppermute(a, 'dp', [(p, p ^ k) for p in range(n_dp)])  11.4 us
    ppermute x7, starting transfers between devices, on_device(): lax.ppermute(a, 'dp', [(p, p ^ k) for p in range(n_dp)])  10.8 us
    pallas_call x1, Pallas kernels, attend(): pl.pallas_call(functools.partial(attend_kernel, tile, window), grid=(rows...  9.32 us
    pallas_call x1, Pallas kernels, own_rows(): pl.pallas_call(functools.partial(own_kernel, block, chunk), in_specs=[SME...  6.63 us
    pallas_call x1, Pallas kernels, peer_rows(): pl.pallas_call(functools.partial(peer_kernel, far, block, chunk), in_spec...  4.92 us
    pallas_call x1, Pallas kernels, first_block(): pl.pallas_call(functools.partial(first_kernel, owner, block, chunk), in_s...  2.95 us
    ppermute x1, waiting for transfers between devices, on_device(): peer = lax.ppermute(hidden, 'tensor', [(0, 1), (1, 0)])  2.31 us
    pallas_call x2, Pallas kernels, place(): pl.pallas_call(functools.partial(gather_kernel, order, block), in_specs=[...  1.89 us
  transfers between devices with their start and end apart: 8, of which 4 were waited for; matrix products, arithmetic and copies ran while one was open for 1% of the time, Pallas kernels for 42%

profile of v3, /device:TPU:16, one launch (start us, length us, event | category | flops | bytes accessed | tf_op | source)
XLA Modules:
  0.0 52.3 jit_solution(10860282727113451436)
XLA Ops:
  0.6 0.1 collective-permute-start
  0.7 0.7 %reshape.9.gain_ref = bf16[1,8192]{1,0:T(2,128)(2,1)S(1)} reshape(bf16[8192]{0:T(1024)(128)(2,1)} %param.11) | data formatting | bytes 32768 | tf_op jit(solution)/shard_map/reshape | solution.py:336
  1.5 0.0 copy-start.1
  1.5 0.6 %copy-done.1 = s32[1,8]{1,0:T(1,128)S(1)} copy-done((s32[1,8]{1,0:T(1,128)S(1)}, s32[1,8]{1,0:T(1,128)}, u32[]{:S(2)}) %copy-start.1) | copy-done | bytes 56
  2.1 6.6 %own_rows.1 = (bf16[384,512]{1,0:T(8,128)(2,1)S(1)}, f32[768,128]{1,0:T(8,128)S(1)}, f32[768,128]{1,0:T(8,128)S(1)}, bf16[8192,256]{1,0:T(8,128)(2,1)S(1)}, bf16[8192,256]{1,0:T(8,128)(2,1)S(1)}) custom-call(s32[1,8]{1,0:T(1,128)S(1)} %copy-done.1, bf16[384,8192]{1,0:T(8,128)(2,1)} %h_hbm.1, bf16[8192,256]{1,0:T(8,128)(2,1)} %wk_hbm.1, ...), custom_call_target="tpu_custom_call" | custom-call | flops 3221225472 | bytes 14680064 | tf_op jit(solution)/shard_map/own_rows/pallas_call | solution.py:108
  8.8 2.3 %collective-permute-done.h_ref = bf16[384,8192]{1,0:T(8,128)(2,1)S(1)} collective-permute-done((bf16[384,8192]{1,0:T(8,128)(2,1)}, bf16[384,8192]{1,0:T(8,128)(2,1)S(1)}, u32[]{:S(2)}, u32[]{:S(2)}) %collective-permute-start) | collective-permute-done | bytes 6291488 | tf_op jit(solution)/shard_map/ppermute | solution.py:338
  11.1 3.0 %first_block.1 = bf16[2,192,256]{2,1,0:T(8,128)(2,1)S(1)} custom-call(s32[1,8]{1,0:T(1,128)S(1)} %copy-done.1, s32[1,8]{1,0:T(1,128)S(1)} %copy-done.2, s32[1,8]{1,0:T(1,128)S(1)} %copy-done.3, s32[1,8]{1,0:T(1,128)S(1)} %copy-done.4, bf16[384,8192]{1,0:T(8,128)(2,1)S(1)} %collective-permute-done.h_ref, bf16[8192,256]{1,0:T(8,128)(2,1)S(1)} %get-tuple-element.23.wk_ref, ...), custom_call_target="tpu_custom_call" | custom-call | flops 1744830464 | bytes 11796480 | tf_op jit(solution)/shard_map/first_block/pallas_call | solution.py:189
  14.0 0.0 copy-start
  14.0 0.5 collective-permute-start.1
  14.6 4.9 %peer_rows.1 = (bf16[768,512]{1,0:T(8,128)(2,1)S(1)}, bf16[2,192,256]{2,1,0:T(8,128)(2,1)S(1)}, bf16[2,192,256]{2,1,0:T(8,128)(2,1)S(1)}, bf16[2,192,256]{2,1,0:...) custom-call(s32[1,8]{1,0:T(1,128)S(1)} %copy-done.1, ...), custom_call_target="tpu_custom_call" | custom-call | flops 3221225472 | bytes 14680064 | tf_op jit(solution)/shard_map/peer_rows/pallas_call | solution.py:232
  19.5 4.5 %collective-permute-start.4 = (bf16[2,192,256]{2,1,0:T(8,128)(2,1)S(1)}, bf16[2,192,256]{2,1,0:T(8,128)(2,1)S(1)}, u32[]{:S(2)}, u32[]{:S(2)}) collective-permute-start(bf16[2,192,256]{2,1,0:T(8,128)(2,1)S(1)} %get-tuple-element.35), channel_id=1, source_target_pairs={{0,10},{2,8},{4,14},{6,12},{8,2},{10,0},{12,6},{14,4},{1,11},{3,9}... | collective-permute-start | bytes 589832 | tf_op jit(solution)/shard_map/ppermute | solution.py:343
  24.0 0.0 collective-permute-start.5
  24.0 2.0 %collective-permute-start.6 = (bf16[2,192,256]{2,1,0:T(8,128)(2,1)S(1)}, bf16[2,192,256]{2,1,0:T(8,128)(2,1)S(1)}, u32[]{:S(2)}, u32[]{:S(2)}) collective-permute-start(bf16[2,192,256]{2,1,0:T(8,128)(2,1)S(1)} %get-tuple-element.37), channel_id=1, source_target_pairs={{0,6},{2,4},{4,2},{6,0},{8,14},{10,12},{12,10},{14,8},{1,7},{3,5},... | collective-permute-start | bytes 589832 | tf_op jit(solution)/shard_map/ppermute | solution.py:343
  26.0 0.1 collective-permute-start.7
  26.1 4.2 %collective-permute-done.1.refs_1_ = bf16[2,192,256]{2,1,0:T(8,128)(2,1)S(1)} collective-permute-done((bf16[2,192,256]{2,1,0:T(8,128)(2,1)S(1)}, bf16[2,192,256]{2,1,0:T(8,128)(2,1)S(1)}, u32[]{:S(2)}, u32[]{:S(2)}) %collective-permute-start.1) | collective-permute-done | bytes 196640 | tf_op jit(solution)/shard_map/ppermute | solution.py:343
  30.3 1.4 %collective-permute-start.2 = (bf16[2,192,256]{2,1,0:T(8,128)(2,1)S(1)}, bf16[2,192,256]{2,1,0:T(8,128)(2,1)S(1)}, u32[]{:S(2)}, u32[]{:S(2)}) collective-permute-start(bf16[2,192,256]{2,1,0:T(8,128)(2,1)S(1)} %get-tuple-element.31), channel_id=1, source_target_pairs={{0,14},{2,12},{4,10},{6,8},{8,6},{10,4},{12,2},{14,0},{1,15},{3,13... | collective-permute-start | bytes 589832 | tf_op jit(solution)/shard_map/ppermute | solution.py:343
  31.7 0.1 collective-permute-done.4.refs_2_
  31.8 2.2 %collective-permute-start.3 = (bf16[2,192,256]{2,1,0:T(8,128)(2,1)S(1)}, bf16[2,192,256]{2,1,0:T(8,128)(2,1)S(1)}, u32[]{:S(2)}, u32[]{:S(2)}) collective-permute-start(bf16[2,192,256]{2,1,0:T(8,128)(2,1)S(1)} %get-tuple-element.32), channel_id=1, source_target_pairs={{0,2},{2,0},{4,6},{6,4},{8,10},{10,8},{12,14},{14,12},{1,3},{3,1},... | collective-permute-start | bytes 589832 | tf_op jit(solution)/shard_map/ppermute | solution.py:343
  34.0 9.3 %attend.1 = bf16[768,2048]{1,0:T(8,128)(2,1)} custom-call(s32[1,8]{1,0:T(1,128)S(1)} %copy-done.1, bf16[768,2048]{1,0:T(8,128)(2,1)S(1)} %copy-done, bf16[768,512]{1,0:T(8,128)(2,1)S(1)} %get-tuple-element.28.kv_ref), custom_call_target="tpu_custom_call" | custom-call | flops 1610612736 | bytes 6291456 | tf_op jit(solution)/shard_map/attend/pallas_call | solution.py:282
  43.4 0.0 collective-permute-done.5.refs_3_
  43.4 1.1 %place_first.1 = (bf16[1536,256]{1,0:T(8,128)(2,1)}, bf16[1536,256]{1,0:T(8,128)(2,1)}) custom-call(bf16[2,192,256]{2,1,0:T(8,128)(2,1)S(1)} %get-tuple-element.33.refs_0_, bf16[2,192,256]{2,1,0:T(8,128)(2,1)S(1)} %collective-permute-done.1.refs_1_, bf16[2,192,256]{2,1,0:T(8,128)(2,1)S(1)} %collective-permute-done.4.refs_2_, ...), custom_call_target="tpu_custom_call" | custom-call | tf_op jit(solution)/shard_map/place_first/pallas_call | solution.py:315
  44.5 7.0 %collective-permute-done.2.refs_0_ = bf16[2,192,256]{2,1,0:T(8,128)(2,1)S(1)} collective-permute-done((bf16[2,192,256]{2,1,0:T(8,128)(2,1)S(1)}, bf16[2,192,256]{2,1,0:T(8,128)(2,1)S(1)}, u32[]{:S(2)}, u32[]{:S(2)}) %collective-permute-start.2) | collective-permute-done | bytes 196640 | tf_op jit(solution)/shard_map/ppermute | solution.py:343
  51.6 0.0 collective-permute-done.3.refs_1_
  51.6 0.8 %place_rest.1 = (bf16[1536,256]{1,0:T(8,128)(2,1)}, bf16[1536,256]{1,0:T(8,128)(2,1)}) custom-call(bf16[2,192,256]{2,1,0:T(8,128)(2,1)S(1)} %collective-permute-done.2.refs_0_, bf16[2,192,256]{2,1,0:T(8,128)(2,1)S(1)} %collective-permute-done.3.refs_1_, bf16[1536,256]{1,0:T(8,128)(2,1)} %get-tuple-element.39.refs_2_, ...), custom_call_target="tpu_custom_call", output_to_operand_aliasing={{0}: (2, {}), {1}: (3, {})} | custom-call | tf_op jit(solution)/shard_map/place_rest/pallas_call | solution.py:315
  (9 shorter events, 0.0 us)
Async XLA Ops:
  0.6 10.4 %collective-permute-start = (bf16[384,8192]{1,0:T(8,128)(2,1)}, bf16[384,8192]{1,0:T(8,128)(2,1)S(1)}, u32[]{:S(2)}, u32[]{:S(2)}) collective-permute-start(bf16[384,8192]{1,0:T(8,128)(2,1)} %h_hbm.1), channel_id=1, source_target_pairs={{0,1},{1,0},{2,3},{3,2},{4,5},{5,4},{6,7},{7,6},{8,9},{9,8},{10,11... | collective-permute-start | bytes 18874376 | tf_op jit(solution)/shard_map/ppermute | solution.py:338
  1.5 0.7 %copy-start.1 = (s32[1,8]{1,0:T(1,128)S(1)}, s32[1,8]{1,0:T(1,128)}, u32[]{:S(2)}) copy-start(s32[1,8]{1,0:T(1,128)} %offset_ref.7) | copy-start | bytes 100
  2.1 9.0 %copy-start.2 = (s32[1,8]{1,0:T(1,128)S(1)}, s32[1,8]{1,0:T(1,128)}, u32[]{:S(2)}) copy-start(s32[1,8]{1,0:T(1,128)} %length_ref.3) | copy-start | bytes 100
  2.1 9.0 %copy-start.3 = (s32[1,8]{1,0:T(1,128)S(1)}, s32[1,8]{1,0:T(1,128)}, u32[]{:S(2)}) copy-start(s32[1,8]{1,0:T(1,128)} %owner_ref.3) | copy-start | bytes 100
  2.1 9.0 %copy-start.4 = (s32[1,8]{1,0:T(1,128)S(1)}, s32[1,8]{1,0:T(1,128)}, u32[]{:S(2)}) copy-start(s32[1,8]{1,0:T(1,128)} %slot_ref.3) | copy-start | bytes 100
  14.0 20.0 %copy-start = (bf16[768,2048]{1,0:T(8,128)(2,1)S(1)}, bf16[768,2048]{1,0:T(8,128)(2,1)}, u32[]{:S(2)}) copy-start(bf16[768,2048]{1,0:T(8,128)(2,1)} %q_ref.1) | copy-start | bytes 9437188
  14.0 16.2 %collective-permute-start.1 = (bf16[2,192,256]{2,1,0:T(8,128)(2,1)S(1)}, bf16[2,192,256]{2,1,0:T(8,128)(2,1)S(1)}, u32[]{:S(2)}, u32[]{:S(2)}) collective-permute-start(bf16[2,192,256]{2,1,0:T(8,128)(2,1)S(1)} %first_block.1), channel_id=1, source_target_pairs={{0,12},{2,14},{4,8},{6,10},{8,4},{10,6},{12,0},{14,2},{1,13},{3,15... | collective-permute-start | bytes 589832 | tf_op jit(solution)/shard_map/ppermute | solution.py:343
  19.5 12.3 %collective-permute-start.4 = (bf16[2,192,256]{2,1,0:T(8,128)(2,1)S(1)}, bf16[2,192,256]{2,1,0:T(8,128)(2,1)S(1)}, u32[]{:S(2)}, u32[]{:S(2)}) collective-permute-start(bf16[2,192,256]{2,1,0:T(8,128)(2,1)S(1)} %get-tuple-element.35), channel_id=1, source_target_pairs={{0,10},{2,8},{4,14},{6,12},{8,2},{10,0},{12,6},{14,4},{1,11},{3,9}... | collective-permute-start | bytes 589832 | tf_op jit(solution)/shard_map/ppermute | solution.py:343
  24.0 19.4 %collective-permute-start.5 = (bf16[2,192,256]{2,1,0:T(8,128)(2,1)S(1)}, bf16[2,192,256]{2,1,0:T(8,128)(2,1)S(1)}, u32[]{:S(2)}, u32[]{:S(2)}) collective-permute-start(bf16[2,192,256]{2,1,0:T(8,128)(2,1)S(1)} %get-tuple-element.36), channel_id=1, source_target_pairs={{0,4},{2,6},{4,0},{6,2},{8,12},{10,14},{12,8},{14,10},{1,5},{3,7},... | collective-permute-start | bytes 589832 | tf_op jit(solution)/shard_map/ppermute | solution.py:343
  24.0 19.4 %collective-permute-start.6 = (bf16[2,192,256]{2,1,0:T(8,128)(2,1)S(1)}, bf16[2,192,256]{2,1,0:T(8,128)(2,1)S(1)}, u32[]{:S(2)}, u32[]{:S(2)}) collective-permute-start(bf16[2,192,256]{2,1,0:T(8,128)(2,1)S(1)} %get-tuple-element.37), channel_id=1, source_target_pairs={{0,6},{2,4},{4,2},{6,0},{8,14},{10,12},{12,10},{14,8},{1,7},{3,5},... | collective-permute-start | bytes 589832 | tf_op jit(solution)/shard_map/ppermute | solution.py:343
  26.0 17.4 %collective-permute-start.7 = (bf16[2,192,256]{2,1,0:T(8,128)(2,1)S(1)}, bf16[2,192,256]{2,1,0:T(8,128)(2,1)S(1)}, u32[]{:S(2)}, u32[]{:S(2)}) collective-permute-start(bf16[2,192,256]{2,1,0:T(8,128)(2,1)S(1)} %get-tuple-element.38), channel_id=1, source_target_pairs={{0,8},{2,10},{4,12},{6,14},{8,0},{10,2},{12,4},{14,6},{1,9},{3,11}... | collective-permute-start | bytes 589832 | tf_op jit(solution)/shard_map/ppermute | solution.py:343
  30.3 21.3 %collective-permute-start.2 = (bf16[2,192,256]{2,1,0:T(8,128)(2,1)S(1)}, bf16[2,192,256]{2,1,0:T(8,128)(2,1)S(1)}, u32[]{:S(2)}, u32[]{:S(2)}) collective-permute-start(bf16[2,192,256]{2,1,0:T(8,128)(2,1)S(1)} %get-tuple-element.31), channel_id=1, source_target_pairs={{0,14},{2,12},{4,10},{6,8},{8,6},{10,4},{12,2},{14,0},{1,15},{3,13... | collective-permute-start | bytes 589832 | tf_op jit(solution)/shard_map/ppermute | solution.py:343
  31.8 19.7 %collective-permute-start.3 = (bf16[2,192,256]{2,1,0:T(8,128)(2,1)S(1)}, bf16[2,192,256]{2,1,0:T(8,128)(2,1)S(1)}, u32[]{:S(2)}, u32[]{:S(2)}) collective-permute-start(bf16[2,192,256]{2,1,0:T(8,128)(2,1)S(1)} %get-tuple-element.32), channel_id=1, source_target_pairs={{0,2},{2,0},{4,6},{6,4},{8,10},{10,8},{12,14},{14,12},{1,3},{3,1},... | collective-permute-start | bytes 589832 | tf_op jit(solution)/shard_map/ppermute | solution.py:343

commit v4 on v3

--- a/solution.py
+++ b/solution.py
@@ -40,32 +40,33 @@
         sin_ref[rows, :] = sine
 
 
-def project(h_ref, rows, gain_ref, wk_ref, wv_ref, acc_k, acc_v, squares, chunk, ready=None):
-    for c in range(h_ref.shape[1] // chunk):
+def project(h_ref, rows, gain_ref, wk_ref, wv_ref, acc_k, acc_v, squares, chunk, ready=None, loaded=None):
+    width = h_ref.shape[1]
+    for c in range(width // chunk):
         if ready is not None:
             ready(c)
-        at = slice(c * chunk, (c + 1) * chunk)
-        h = h_ref[rows, at]
-        scaled = h * gain_ref[:, at]
-        key = jnp.dot(scaled, wk_ref[at, :], preferred_element_type=jnp.float32)
-        value = jnp.dot(scaled, wv_ref[at, :], preferred_element_type=jnp.float32)
+        h = h_ref[rows, c * chunk : (c + 1) * chunk]
         parts = [h[:, j * HD : (j + 1) * HD].astype(jnp.float32) for j in range(chunk // HD)]
         total = sum(p * p for p in parts)
-        if c == 0:
-            acc_k[...], acc_v[...], squares[...] = key, value, total
-        else:
-            acc_k[...] += key
-            acc_v[...] += value
-            squares[...] += total
-
-
-def finish(width, cosine, sine, acc_k, acc_v, squares):
+        squares[...] = total if c == 0 else squares[...] + total
     factor = lax.rsqrt(jnp.sum(squares[...], axis=1, keepdims=True) / width + EPSILON)
+    for c in range(width // chunk):
+        if loaded is not None:
+            loaded(c)
+        at = slice(c * chunk, (c + 1) * chunk)
+        normed = h_ref[rows, at].astype(jnp.float32) * factor * gain_ref[:, at].astype(jnp.float32)
+        normed = normed.astype(jnp.bfloat16)
+        for w_ref, acc in ((wk_ref, acc_k), (wv_ref, acc_v)):
+            product = jnp.dot(normed, w_ref[at, :], preferred_element_type=jnp.float32)
+            acc[...] = product if c == 0 else acc[...] + product
+
+
+def finish(cosine, sine, acc_k, acc_v):
     keys = []
     for h in range(acc_k.shape[1] // HD):
-        x = acc_k[:, h * HD : (h + 1) * HD] * factor
+        x = acc_k[:, h * HD : (h + 1) * HD]
         keys.append((x * cosine + pltpu.roll(x, HD // 2, 1) * sine).astype(jnp.bfloat16))
-    return jnp.concatenate(keys, axis=1), (acc_v[...] * factor).astype(jnp.bfloat16)
+    return jnp.concatenate(keys, axis=1), acc_v[...].astype(jnp.bfloat16)
 
 
 def own_kernel(
@@ -84,18 +85,23 @@
         )
 
     def ready(c):
-        for copy in copies(c):
+        copies(c)[0].wait()
+
+    def loaded(c):
+        for copy in copies(c)[1:]:
             copy.wait()
 
     for c in range(width // chunk):
-        for copy in copies(c):
+        copies(c)[0].start()
+    for c in range(width // chunk):
+        for copy in copies(c)[1:]:
             copy.start()
     rotation_tables(block, offset_ref, cos_pad, sin_pad)
     cos_ref[...] = cos_pad[: cos_ref.shape[0], :]
     sin_ref[...] = sin_pad[: sin_ref.shape[0], :]
-    project(h_ref, slice(None), gain_ref, wk_ref, wv_ref, acc_k, acc_v, squares, chunk, ready)
+    project(h_ref, slice(None), gain_ref, wk_ref, wv_ref, acc_k, acc_v, squares, chunk, ready, loaded)
     here = pl.ds(pl.multiple_of(lax.axis_index("tensor") * rows, rows), rows)
-    keys, values = finish(width, cos_pad[here, :], sin_pad[here, :], acc_k, acc_v, squares)
+    keys, values = finish(cos_pad[here, :], sin_pad[here, :], acc_k, acc_v)
     out_ref[:, :cols] = keys
     out_ref[:, cols:] = values
 
@@ -176,7 +182,7 @@
     local = pl.multiple_of(jnp.clip(start - (1 - mine) * rows, 0, rows - span), 16)
     there = pl.ds(pl.multiple_of((1 - mine) * rows + local, 16), span)
     project(h_ref, pl.ds(local, span), gain_ref, wk_ref, wv_ref, acc_k, acc_v, squares, chunk)
-    keys, values = finish(width, cos_ref[there, :], sin_ref[there, :], acc_k, acc_v, squares)
+    keys, values = finish(cos_ref[there, :], sin_ref[there, :], acc_k, acc_v)
     kv[there, :cols] = keys
     kv[there, cols:] = values
     select_block(block, cols, owner, (offset_ref, length_ref, owner_ref, slot_ref), kv, block_ref)
@@ -216,7 +222,7 @@
     there = pl.ds(pl.multiple_of((1 - mine) * rows, rows), rows)
     here = pl.ds(pl.multiple_of(mine * rows, rows), rows)
     project(h_ref, slice(None), gain_ref, wk_ref, wv_ref, acc_k, acc_v, squares, chunk)
-    keys, values = finish(width, cos_ref[there, :], sin_ref[there, :], acc_k, acc_v, squares)
+    keys, values = finish(cos_ref[there, :], sin_ref[there, :], acc_k, acc_v)
     kv_ref[there, :cols] = keys
     kv_ref[there, cols:] = values
     kv_ref[here, :] = own_ref[...]

time: 52.6 us -> 53.7 us (1.021)
  Pallas kernels: 25.7 us -> 28.8 us
  starting transfers between devices: 10.8 us -> 9.37 us
  waiting for transfers between devices: 13.7 us -> 12.7 us
    ppermute x7, starting transfers between devices: 10.8 us -> 9.29 us  [on_device(): lax.ppermute(a, 'dp', [(p, p ^ k) for p in range(n_dp)])]
    ppermute x1, waiting for transfers between devices: 2.31 us -> 0.9 us  [on_device(): peer = lax.ppermute(hidden, 'tensor', [(0, 1), (1, 0)])]
    pallas_call x1, Pallas kernels: 6.63 us -> 8.04 us  [own_rows(): pl.pallas_call(functools.partial(own_kernel, block, chunk), in_specs=[SME...]
    pallas_call x1, Pallas kernels: 4.92 us -> 6.04 us  [peer_rows(): pl.pallas_call(functools.partial(peer_kernel, far, block, chunk), in_spec...]
    pallas_call x1, Pallas kernels: 2.95 us -> 3.53 us  [first_block(): pl.pallas_call(functools.partial(first_kernel, owner, block, chunk), in_s...]
  transfers between devices with their start and end apart: 8 -> 8, of which waited for: 4 -> 5; matrix products, arithmetic and copies ran while one was open for 1% -> 1% of each run, Pallas kernels for 42% -> 46%
where the time goes in v4:
time: 53.7 us; the launch traced here: 53.1 us
  Pallas kernels  28.8 us (54%)
  waiting for transfers between devices  12.7 us (24%)
  starting transfers between devices  9.37 us (17%)
  local copies, waits for them, and re-layouts  1.41 us (3%)
  between operations  0.86 us (2%)
    ppermute x7, waiting for transfers between devices, on_device(): lax.ppermute(a, 'dp', [(p, p ^ k) for p in range(n_dp)])  11.8 us
    pallas_call x1, Pallas kernels, attend(): pl.pallas_call(functools.partial(attend_kernel, tile, window), grid=(rows...  9.32 us
    ppermute x7, starting transfers between devices, on_device(): lax.ppermute(a, 'dp', [(p, p ^ k) for p in range(n_dp)])  9.29 us
    pallas_call x1, Pallas kernels, own_rows(): pl.pallas_call(functools.partial(own_kernel, block, chunk), in_specs=[SME...  8.04 us
    pallas_call x1, Pallas kernels, peer_rows(): pl.pallas_call(functools.partial(peer_kernel, far, block, chunk), in_spec...  6.04 us
    pallas_call x1, Pallas kernels, first_block(): pl.pallas_call(functools.partial(first_kernel, owner, block, chunk), in_s...  3.53 us
    pallas_call x2, Pallas kernels, place(): pl.pallas_call(functools.partial(gather_kernel, order, block), in_specs=[...  1.87 us
  transfers between devices with their start and end apart: 8, of which 5 were waited for; matrix products, arithmetic and copies ran while one was open for 1% of the time, Pallas kernels for 46%

profile of v4, /device:TPU:16, one launch (start us, length us, event | category | flops | bytes accessed | tf_op | source)
XLA Modules:
  0.0 53.1 jit_solution(16726581227030817249)
XLA Ops:
  0.6 0.1 collective-permute-start
  0.7 0.7 %reshape.9.gain_ref = bf16[1,8192]{1,0:T(2,128)(2,1)S(1)} reshape(bf16[8192]{0:T(1024)(128)(2,1)} %param.11) | data formatting | bytes 32768 | tf_op jit(solution)/shard_map/reshape | solution.py:342
  1.5 0.0 copy-start.1
  1.5 0.6 %copy-done.1 = s32[1,8]{1,0:T(1,128)S(1)} copy-done((s32[1,8]{1,0:T(1,128)S(1)}, s32[1,8]{1,0:T(1,128)}, u32[]{:S(2)}) %copy-start.1) | copy-done | bytes 56
  2.1 8.0 %own_rows.1 = (bf16[384,512]{1,0:T(8,128)(2,1)S(1)}, f32[768,128]{1,0:T(8,128)S(1)}, f32[768,128]{1,0:T(8,128)S(1)}, bf16[8192,256]{1,0:T(8,128)(2,1)S(1)}, bf16[8192,256]{1,0:T(8,128)(2,1)S(1)}) custom-call(s32[1,8]{1,0:T(1,128)S(1)} %copy-done.1, bf16[384,8192]{1,0:T(8,128)(2,1)} %h_hbm.1, bf16[8192,256]{1,0:T(8,128)(2,1)} %wk_hbm.1, ...), custom_call_target="tpu_custom_call" | custom-call | flops 3221225472 | bytes 14680064 | tf_op jit(solution)/shard_map/own_rows/pallas_call | solution.py:114
  10.2 0.9 %collective-permute-done.h_ref = bf16[384,8192]{1,0:T(8,128)(2,1)S(1)} collective-permute-done((bf16[384,8192]{1,0:T(8,128)(2,1)}, bf16[384,8192]{1,0:T(8,128)(2,1)S(1)}, u32[]{:S(2)}, u32[]{:S(2)}) %collective-permute-start) | collective-permute-done | bytes 6291488 | tf_op jit(solution)/shard_map/ppermute | solution.py:344
  11.1 3.5 %first_block.1 = bf16[2,192,256]{2,1,0:T(8,128)(2,1)S(1)} custom-call(s32[1,8]{1,0:T(1,128)S(1)} %copy-done.1, s32[1,8]{1,0:T(1,128)S(1)} %copy-done.2, s32[1,8]{1,0:T(1,128)S(1)} %copy-done.3, s32[1,8]{1,0:T(1,128)S(1)} %copy-done.4, bf16[384,8192]{1,0:T(8,128)(2,1)S(1)} %collective-permute-done.h_ref, bf16[8192,256]{1,0:T(8,128)(2,1)S(1)} %get-tuple-element.23.wk_ref, ...), custom_call_target="tpu_custom_call" | custom-call | flops 1744830464 | bytes 11796480 | tf_op jit(solution)/shard_map/first_block/pallas_call | solution.py:195
  14.6 0.0 copy-start
  14.6 0.5 collective-permute-start.1
  15.1 6.0 %peer_rows.1 = (bf16[768,512]{1,0:T(8,128)(2,1)S(1)}, bf16[2,192,256]{2,1,0:T(8,128)(2,1)S(1)}, bf16[2,192,256]{2,1,0:T(8,128)(2,1)S(1)}, bf16[2,192,256]{2,1,0:...) custom-call(s32[1,8]{1,0:T(1,128)S(1)} %copy-done.1, ...), custom_call_target="tpu_custom_call" | custom-call | flops 3221225472 | bytes 14680064 | tf_op jit(solution)/shard_map/peer_rows/pallas_call | solution.py:238
  21.2 4.5 %collective-permute-start.4 = (bf16[2,192,256]{2,1,0:T(8,128)(2,1)S(1)}, bf16[2,192,256]{2,1,0:T(8,128)(2,1)S(1)}, u32[]{:S(2)}, u32[]{:S(2)}) collective-permute-start(bf16[2,192,256]{2,1,0:T(8,128)(2,1)S(1)} %get-tuple-element.35), channel_id=1, source_target_pairs={{0,10},{2,8},{4,14},{6,12},{8,2},{10,0},{12,6},{14,4},{1,11},{3,9}... | collective-permute-start | bytes 589832 | tf_op jit(solution)/shard_map/ppermute | solution.py:349
  25.7 2.0 %collective-permute-start.6 = (bf16[2,192,256]{2,1,0:T(8,128)(2,1)S(1)}, bf16[2,192,256]{2,1,0:T(8,128)(2,1)S(1)}, u32[]{:S(2)}, u32[]{:S(2)}) collective-permute-start(bf16[2,192,256]{2,1,0:T(8,128)(2,1)S(1)} %get-tuple-element.37), channel_id=1, source_target_pairs={{0,6},{2,4},{4,2},{6,0},{8,14},{10,12},{12,10},{14,8},{1,7},{3,5},... | collective-permute-start | bytes 589832 | tf_op jit(solution)/shard_map/ppermute | solution.py:349
  27.7 0.1 collective-permute-start.7
  27.8 1.9 %collective-permute-done.1.refs_1_ = bf16[2,192,256]{2,1,0:T(8,128)(2,1)S(1)} collective-permute-done((bf16[2,192,256]{2,1,0:T(8,128)(2,1)S(1)}, bf16[2,192,256]{2,1,0:T(8,128)(2,1)S(1)}, u32[]{:S(2)}, u32[]{:S(2)}) %collective-permute-start.1) | collective-permute-done | bytes 196640 | tf_op jit(solution)/shard_map/ppermute | solution.py:349
  29.7 1.5 %collective-permute-start.2 = (bf16[2,192,256]{2,1,0:T(8,128)(2,1)S(1)}, bf16[2,192,256]{2,1,0:T(8,128)(2,1)S(1)}, u32[]{:S(2)}, u32[]{:S(2)}) collective-permute-start(bf16[2,192,256]{2,1,0:T(8,128)(2,1)S(1)} %get-tuple-element.31), channel_id=1, source_target_pairs={{0,14},{2,12},{4,10},{6,8},{8,6},{10,4},{12,2},{14,0},{1,15},{3,13... | collective-permute-start | bytes 589832 | tf_op jit(solution)/shard_map/ppermute | solution.py:349
  31.2 2.0 %collective-permute-done.4.refs_2_ = bf16[2,192,256]{2,1,0:T(8,128)(2,1)S(1)} collective-permute-done((bf16[2,192,256]{2,1,0:T(8,128)(2,1)S(1)}, bf16[2,192,256]{2,1,0:T(8,128)(2,1)S(1)}, u32[]{:S(2)}, u32[]{:S(2)}) %collective-permute-start.4) | collective-permute-done | bytes 196640 | tf_op jit(solution)/shard_map/ppermute | solution.py:349
  33.2 0.6 %collective-permute-start.3 = (bf16[2,192,256]{2,1,0:T(8,128)(2,1)S(1)}, bf16[2,192,256]{2,1,0:T(8,128)(2,1)S(1)}, u32[]{:S(2)}, u32[]{:S(2)}) collective-permute-start(bf16[2,192,256]{2,1,0:T(8,128)(2,1)S(1)} %get-tuple-element.32), channel_id=1, source_target_pairs={{0,2},{2,0},{4,6},{6,4},{8,10},{10,8},{12,14},{14,12},{1,3},{3,1},... | collective-permute-start | bytes 589832 | tf_op jit(solution)/shard_map/ppermute | solution.py:349
  33.9 9.3 %attend.1 = bf16[768,2048]{1,0:T(8,128)(2,1)} custom-call(s32[1,8]{1,0:T(1,128)S(1)} %copy-done.1, bf16[768,2048]{1,0:T(8,128)(2,1)S(1)} %copy-done, bf16[768,512]{1,0:T(8,128)(2,1)S(1)} %get-tuple-element.28.kv_ref), custom_call_target="tpu_custom_call" | custom-call | flops 1610612736 | bytes 6291456 | tf_op jit(solution)/shard_map/attend/pallas_call | solution.py:288
  43.2 0.0 collective-permute-done.5.refs_3_
  43.2 3.6 %collective-permute-done.6.refs_4_ = bf16[2,192,256]{2,1,0:T(8,128)(2,1)S(1)} collective-permute-done((bf16[2,192,256]{2,1,0:T(8,128)(2,1)S(1)}, bf16[2,192,256]{2,1,0:T(8,128)(2,1)S(1)}, u32[]{:S(2)}, u32[]{:S(2)}) %collective-permute-start.6) | collective-permute-done | bytes 196640 | tf_op jit(solution)/shard_map/ppermute | solution.py:349
  46.8 0.0 collective-permute-done.7.refs_5_
  46.8 1.1 %place_first.1 = (bf16[1536,256]{1,0:T(8,128)(2,1)}, bf16[1536,256]{1,0:T(8,128)(2,1)}) custom-call(bf16[2,192,256]{2,1,0:T(8,128)(2,1)S(1)} %get-tuple-element.33.refs_0_, bf16[2,192,256]{2,1,0:T(8,128)(2,1)S(1)} %collective-permute-done.1.refs_1_, bf16[2,192,256]{2,1,0:T(8,128)(2,1)S(1)} %collective-permute-done.4.refs_2_, ...), custom_call_target="tpu_custom_call" | custom-call | tf_op jit(solution)/shard_map/place_first/pallas_call | solution.py:321
  47.9 4.3 %collective-permute-done.2.refs_0_ = bf16[2,192,256]{2,1,0:T(8,128)(2,1)S(1)} collective-permute-done((bf16[2,192,256]{2,1,0:T(8,128)(2,1)S(1)}, bf16[2,192,256]{2,1,0:T(8,128)(2,1)S(1)}, u32[]{:S(2)}, u32[]{:S(2)}) %collective-permute-start.2) | collective-permute-done | bytes 196640 | tf_op jit(solution)/shard_map/ppermute | solution.py:349
  52.2 0.8 %place_rest.1 = (bf16[1536,256]{1,0:T(8,128)(2,1)}, bf16[1536,256]{1,0:T(8,128)(2,1)}) custom-call(bf16[2,192,256]{2,1,0:T(8,128)(2,1)S(1)} %collective-permute-done.2.refs_0_, bf16[2,192,256]{2,1,0:T(8,128)(2,1)S(1)} %collective-permute-done.3.refs_1_, bf16[1536,256]{1,0:T(8,128)(2,1)} %get-tuple-element.39.refs_2_, ...), custom_call_target="tpu_custom_call", output_to_operand_aliasing={{0}: (2, {}), {1}: (3, {})} | custom-call | tf_op jit(solution)/shard_map/place_rest/pallas_call | solution.py:321
  (9 shorter events, 0.0 us)
Async XLA Ops:
  0.6 10.4 %collective-permute-start = (bf16[384,8192]{1,0:T(8,128)(2,1)}, bf16[384,8192]{1,0:T(8,128)(2,1)S(1)}, u32[]{:S(2)}, u32[]{:S(2)}) collective-permute-start(bf16[384,8192]{1,0:T(8,128)(2,1)} %h_hbm.1), channel_id=1, source_target_pairs={{0,1},{1,0},{2,3},{3,2},{4,5},{5,4},{6,7},{7,6},{8,9},{9,8},{10,11... | collective-permute-start | bytes 18874376 | tf_op jit(solution)/shard_map/ppermute | solution.py:344
  1.5 0.7 %copy-start.1 = (s32[1,8]{1,0:T(1,128)S(1)}, s32[1,8]{1,0:T(1,128)}, u32[]{:S(2)}) copy-start(s32[1,8]{1,0:T(1,128)} %offset_ref.7) | copy-start | bytes 100
  2.1 9.0 %copy-start.2 = (s32[1,8]{1,0:T(1,128)S(1)}, s32[1,8]{1,0:T(1,128)}, u32[]{:S(2)}) copy-start(s32[1,8]{1,0:T(1,128)} %length_ref.3) | copy-start | bytes 100
  2.1 9.0 %copy-start.3 = (s32[1,8]{1,0:T(1,128)S(1)}, s32[1,8]{1,0:T(1,128)}, u32[]{:S(2)}) copy-start(s32[1,8]{1,0:T(1,128)} %owner_ref.3) | copy-start | bytes 100
  2.1 9.0 %copy-start.4 = (s32[1,8]{1,0:T(1,128)S(1)}, s32[1,8]{1,0:T(1,128)}, u32[]{:S(2)}) copy-start(s32[1,8]{1,0:T(1,128)} %slot_ref.3) | copy-start | bytes 100
  14.6 19.3 %copy-start = (bf16[768,2048]{1,0:T(8,128)(2,1)S(1)}, bf16[768,2048]{1,0:T(8,128)(2,1)}, u32[]{:S(2)}) copy-start(bf16[768,2048]{1,0:T(8,128)(2,1)} %q_ref.1) | copy-start | bytes 9437188
  14.6 15.1 %collective-permute-start.1 = (bf16[2,192,256]{2,1,0:T(8,128)(2,1)S(1)}, bf16[2,192,256]{2,1,0:T(8,128)(2,1)S(1)}, u32[]{:S(2)}, u32[]{:S(2)}) collective-permute-start(bf16[2,192,256]{2,1,0:T(8,128)(2,1)S(1)} %first_block.1), channel_id=1, source_target_pairs={{0,12},{2,14},{4,8},{6,10},{8,4},{10,6},{12,0},{14,2},{1,13},{3,15... | collective-permute-start | bytes 589832 | tf_op jit(solution)/shard_map/ppermute | solution.py:349
  21.2 12.0 %collective-permute-start.4 = (bf16[2,192,256]{2,1,0:T(8,128)(2,1)S(1)}, bf16[2,192,256]{2,1,0:T(8,128)(2,1)S(1)}, u32[]{:S(2)}, u32[]{:S(2)}) collective-permute-start(bf16[2,192,256]{2,1,0:T(8,128)(2,1)S(1)} %get-tuple-element.35), channel_id=1, source_target_pairs={{0,10},{2,8},{4,14},{6,12},{8,2},{10,0},{12,6},{14,4},{1,11},{3,9}... | collective-permute-start | bytes 589832 | tf_op jit(solution)/shard_map/ppermute | solution.py:349
  25.7 17.5 %collective-permute-start.5 = (bf16[2,192,256]{2,1,0:T(8,128)(2,1)S(1)}, bf16[2,192,256]{2,1,0:T(8,128)(2,1)S(1)}, u32[]{:S(2)}, u32[]{:S(2)}) collective-permute-start(bf16[2,192,256]{2,1,0:T(8,128)(2,1)S(1)} %get-tuple-element.36), channel_id=1, source_target_pairs={{0,4},{2,6},{4,0},{6,2},{8,12},{10,14},{12,8},{14,10},{1,5},{3,7},... | collective-permute-start | bytes 589832 | tf_op jit(solution)/shard_map/ppermute | solution.py:349
  25.7 21.1 %collective-permute-start.6 = (bf16[2,192,256]{2,1,0:T(8,128)(2,1)S(1)}, bf16[2,192,256]{2,1,0:T(8,128)(2,1)S(1)}, u32[]{:S(2)}, u32[]{:S(2)}) collective-permute-start(bf16[2,192,256]{2,1,0:T(8,128)(2,1)S(1)} %get-tuple-element.37), channel_id=1, source_target_pairs={{0,6},{2,4},{4,2},{6,0},{8,14},{10,12},{12,10},{14,8},{1,7},{3,5},... | collective-permute-start | bytes 589832 | tf_op jit(solution)/shard_map/ppermute | solution.py:349
  27.7 19.1 %collective-permute-start.7 = (bf16[2,192,256]{2,1,0:T(8,128)(2,1)S(1)}, bf16[2,192,256]{2,1,0:T(8,128)(2,1)S(1)}, u32[]{:S(2)}, u32[]{:S(2)}) collective-permute-start(bf16[2,192,256]{2,1,0:T(8,128)(2,1)S(1)} %get-tuple-element.38), channel_id=1, source_target_pairs={{0,8},{2,10},{4,12},{6,14},{8,0},{10,2},{12,4},{14,6},{1,9},{3,11}... | collective-permute-start | bytes 589832 | tf_op jit(solution)/shard_map/ppermute | solution.py:349
  29.7 22.5 %collective-permute-start.2 = (bf16[2,192,256]{2,1,0:T(8,128)(2,1)S(1)}, bf16[2,192,256]{2,1,0:T(8,128)(2,1)S(1)}, u32[]{:S(2)}, u32[]{:S(2)}) collective-permute-start(bf16[2,192,256]{2,1,0:T(8,128)(2,1)S(1)} %get-tuple-element.31), channel_id=1, source_target_pairs={{0,14},{2,12},{4,10},{6,8},{8,6},{10,4},{12,2},{14,0},{1,15},{3,13... | collective-permute-start | bytes 589832 | tf_op jit(solution)/shard_map/ppermute | solution.py:349
  33.2 18.9 %collective-permute-start.3 = (bf16[2,192,256]{2,1,0:T(8,128)(2,1)S(1)}, bf16[2,192,256]{2,1,0:T(8,128)(2,1)S(1)}, u32[]{:S(2)}, u32[]{:S(2)}) collective-permute-start(bf16[2,192,256]{2,1,0:T(8,128)(2,1)S(1)} %get-tuple-element.32), channel_id=1, source_target_pairs={{0,2},{2,0},{4,6},{6,4},{8,10},{10,8},{12,14},{14,12},{1,3},{3,1},... | collective-permute-start | bytes 589832 | tf_op jit(solution)/shard_map/ppermute | solution.py:349

commit v5 on v4

--- a/solution.py
+++ b/solution.py
@@ -40,7 +40,7 @@
         sin_ref[rows, :] = sine
 
 
-def project(h_ref, rows, gain_ref, wk_ref, wv_ref, acc_k, acc_v, squares, chunk, ready=None, loaded=None):
+def norm_factor(h_ref, rows, squares, chunk, ready=None):
     width = h_ref.shape[1]
     for c in range(width // chunk):
         if ready is not None:
@@ -49,7 +49,11 @@
         parts = [h[:, j * HD : (j + 1) * HD].astype(jnp.float32) for j in range(chunk // HD)]
         total = sum(p * p for p in parts)
         squares[...] = total if c == 0 else squares[...] + total
-    factor = lax.rsqrt(jnp.sum(squares[...], axis=1, keepdims=True) / width + EPSILON)
+    return lax.rsqrt(jnp.sum(squares[...], axis=1, keepdims=True) / width + EPSILON)
+
+
+def project(h_ref, rows, gain_ref, wk_ref, wv_ref, acc_k, acc_v, factor, chunk, loaded=None):
+    width = h_ref.shape[1]
     for c in range(width // chunk):
         if loaded is not None:
             loaded(c)
@@ -71,7 +75,7 @@
 
 def own_kernel(
     block, chunk, offset_ref, h_hbm, wk_hbm, wv_hbm, gain_ref,
-    out_ref, cos_ref, sin_ref, wk_ref, wv_ref, h_ref, acc_k, acc_v, squares, cos_pad, sin_pad, sems
+    out_ref, factor_ref, cos_ref, sin_ref, wk_ref, wv_ref, h_ref, acc_k, acc_v, squares, cos_pad, sin_pad, sems
 ):
     rows, width = h_hbm.shape
     cols = acc_k.shape[1]
@@ -99,7 +103,9 @@
     rotation_tables(block, offset_ref, cos_pad, sin_pad)
     cos_ref[...] = cos_pad[: cos_ref.shape[0], :]
     sin_ref[...] = sin_pad[: sin_ref.shape[0], :]
-    project(h_ref, slice(None), gain_ref, wk_ref, wv_ref, acc_k, acc_v, squares, chunk, ready, loaded)
+    factor = norm_factor(h_ref, slice(None), squares, chunk, ready)
+    factor_ref[...] = jnp.broadcast_to(factor, factor_ref.shape)
+    project(h_ref, slice(None), gain_ref, wk_ref, wv_ref, acc_k, acc_v, factor, chunk, loaded)
     here = pl.ds(pl.multiple_of(lax.axis_index("tensor") * rows, rows), rows)
     keys, values = finish(cos_pad[here, :], sin_pad[here, :], acc_k, acc_v)
     out_ref[:, :cols] = keys
@@ -114,9 +120,10 @@
     return pl.pallas_call(
         functools.partial(own_kernel, block, chunk),
         in_specs=[SMEM, hbm, hbm, hbm, VMEM],
-        out_specs=[VMEM] * 5,
+        out_specs=[VMEM] * 6,
         out_shape=[
             jax.ShapeDtypeStruct((rows, 2 * cols), jnp.bfloat16),
+            jax.ShapeDtypeStruct((rows, HD), f32),
             jax.ShapeDtypeStruct((tok_rows, HD), f32),
             jax.ShapeDtypeStruct((tok_rows, HD), f32),
             jax.ShapeDtypeStruct(wk.shape, wk.dtype),
@@ -181,7 +188,8 @@
     start = jnp.minimum((offset // 16) * 16, 2 * rows - span)
     local = pl.multiple_of(jnp.clip(start - (1 - mine) * rows, 0, rows - span), 16)
     there = pl.ds(pl.multiple_of((1 - mine) * rows + local, 16), span)
-    project(h_ref, pl.ds(local, span), gain_ref, wk_ref, wv_ref, acc_k, acc_v, squares, chunk)
+    factor = norm_factor(h_ref, pl.ds(local, span), squares, chunk)
+    project(h_ref, pl.ds(local, span), gain_ref, wk_ref, wv_ref, acc_k, acc_v, factor, chunk)
     keys, values = finish(cos_ref[there, :], sin_ref[there, :], acc_k, acc_v)
     kv[there, :cols] = keys
     kv[there, cols:] = values
@@ -213,15 +221,15 @@
 
 def peer_kernel(
     far, block, chunk, offset_ref, length_ref, owner_ref, slot_ref,
-    h_ref, wk_ref, wv_ref, gain_ref, cos_ref, sin_ref, own_ref, kv_ref, *rest
+    h_ref, wk_ref, wv_ref, gain_ref, cos_ref, sin_ref, own_ref, factor_ref, kv_ref, *rest
 ):
-    blocks, (acc_k, acc_v, squares) = rest[: len(far)], rest[len(far) :]
+    blocks, (acc_k, acc_v) = rest[: len(far)], rest[len(far) :]
     rows, width = h_ref.shape
     cols = acc_k.shape[1]
     mine = lax.axis_index("tensor")
     there = pl.ds(pl.multiple_of((1 - mine) * rows, rows), rows)
     here = pl.ds(pl.multiple_of(mine * rows, rows), rows)
-    project(h_ref, slice(None), gain_ref, wk_ref, wv_ref, acc_k, acc_v, squares, chunk)
+    project(h_ref, slice(None), gain_ref, wk_ref, wv_ref, acc_k, acc_v, factor_ref[:, :1], chunk)
     keys, values = finish(cos_ref[there, :], sin_ref[there, :], acc_k, acc_v)
     kv_ref[there, :cols] = keys
     kv_ref[there, cols:] = values
@@ -231,27 +239,26 @@
         select_block(block, cols, jnp.bitwise_xor(lax.axis_index("dp"), k), places, kv_ref, out_ref)
 
 
-def peer_rows(far, block, places, peer, wk, wv, gain, cosine, sine, own, chunk=1024):
+def peer_rows(far, block, places, peer, wk, wv, gain, cosine, sine, own, factor, chunk=1024):
     rows, width = peer.shape
     cols = wk.shape[1]
     tok_rows = cosine.shape[0]
     return pl.pallas_call(
         functools.partial(peer_kernel, far, block, chunk),
-        in_specs=[SMEM] * 4 + [VMEM] * 7,
+        in_specs=[SMEM] * 4 + [VMEM] * 8,
         out_specs=[VMEM] * (1 + len(far)),
         out_shape=[jax.ShapeDtypeStruct((tok_rows, 2 * cols), jnp.bfloat16)]
         + [jax.ShapeDtypeStruct((2, block, cols), jnp.bfloat16)] * len(far),
         scratch_shapes=[
             pltpu.VMEM((rows, cols), jnp.float32),
             pltpu.VMEM((rows, cols), jnp.float32),
-            pltpu.VMEM((rows, HD), jnp.float32),
         ],
         compiler_params=pltpu.CompilerParams(vmem_limit_bytes=28 * MIB),
         cost_estimate=pl.CostEstimate(
             flops=4 * rows * width * cols, bytes_accessed=2 * (rows * width + 2 * width * cols), transcendentals=0
         ),
         name="peer_rows",
-    )(*places, peer, wk, wv, gain, cosine, sine, own)
+    )(*places, peer, wk, wv, gain, cosine, sine, own, factor)
 
 
 def attend_kernel(tile, window, offset_ref, q_ref, kv_ref, out_ref):
@@ -342,7 +349,7 @@
     gain = norm_gain.reshape(1, width)
 
     peer = lax.ppermute(hidden, "tensor", [(0, 1), (1, 0)])
-    own, cosine, sine, wk, wv = own_rows(
+    own, factor, cosine, sine, wk, wv = own_rows(
         block, prompt_offsets, hidden, key_weight, value_weight, gain, tok_rows
     )
     places = [prompt_offsets, prompt_lengths, decode_owner, slot_offsets]
@@ -351,8 +358,9 @@
     far = list(range(half_dp, n_dp))
     near = list(range(1, half_dp))
     order = (far[2], far[1], *near[1:], far[0], *far[3:], near[0], 0)
+    factor = lax.ppermute(factor, "tensor", [(0, 1), (1, 0)])
     first = first_block(order[0], block, places, peer, wk, wv, gain, cosine, sine, own)
-    kv, *blocks = peer_rows(order[1:], block, places, peer, wk, wv, gain, cosine, sine, own)
+    kv, *blocks = peer_rows(order[1:], block, places, peer, wk, wv, gain, cosine, sine, own, factor)
     first = swap(first, order[0])
     first, *blocks[4:-1] = lax.optimization_barrier((first, *blocks[4:-1]))
     received = [first] + [swap(a, k) for k, a in zip(order[1:], blocks)]

time: 53.7 us -> 53.2 us (level)
  starting transfers between devices: 9.37 us -> 11.1 us
  Pallas kernels: 28.8 us -> 27.4 us
    pallas_call x1, Pallas kernels: 6.04 us -> 4.7 us  [peer_rows(): pl.pallas_call(functools.partial(peer_kernel, far, block, chunk), in_spec...]
    ppermute x7, starting transfers between devices: 9.29 us -> 10.5 us  [on_device(): lax.ppermute(a, 'dp', [(p, p ^ k) for p in range(n_dp)])]
    ppermute x0 -> x1, starting transfers between devices: none -> 0.56 us  [on_device(): factor = lax.ppermute(factor, 'tensor', [(0, 1), (1, 0)])]
    ppermute x1, waiting for transfers between devices: 0.9 us -> 0.35 us  [on_device(): peer = lax.ppermute(hidden, 'tensor', [(0, 1), (1, 0)])]
  transfers between devices with their start and end apart: 8 -> 9, of which waited for: 5 -> 5; matrix products, arithmetic and copies ran while one was open for 1% -> 1% of each run, Pallas kernels for 46% -> 50%
where the time goes in v5:
time: 53.2 us; the launch traced here: 52.9 us
  Pallas kernels  27.4 us (52%)
  waiting for transfers between devices  12.2 us (23%)
  starting transfers between devices  11.1 us (21%)
  local copies, waits for them, and re-layouts  1.41 us (3%)
  between operations  0.7 us (1%)
    ppermute x7, waiting for transfers between devices, on_device(): lax.ppermute(a, 'dp', [(p, p ^ k) for p in range(n_dp)])  11.9 us
    ppermute x7, starting transfers between devices, on_device(): lax.ppermute(a, 'dp', [(p, p ^ k) for p in range(n_dp)])  10.5 us
    pallas_call x1, Pallas kernels, attend(): pl.pallas_call(functools.partial(attend_kernel, tile, window), grid=(rows...  9.29 us
    pallas_call x1, Pallas kernels, own_rows(): pl.pallas_call(functools.partial(own_kernel, block, chunk), in_specs=[SME...  8.04 us
    pallas_call x1, Pallas kernels, peer_rows(): pl.pallas_call(functools.partial(peer_kernel, far, block, chunk), in_spec...  4.7 us
    pallas_call x1, Pallas kernels, first_block(): pl.pallas_call(functools.partial(first_kernel, owner, block, chunk), in_s...  3.54 us
    pallas_call x2, Pallas kernels, place(): pl.pallas_call(functools.partial(gather_kernel, order, block), in_specs=[...  1.87 us
  transfers between devices with their start and end apart: 9, of which 5 were waited for; matrix products, arithmetic and copies ran while one was open for 1% of the time, Pallas kernels for 50%

profile of v5, /device:TPU:16, one launch (start us, length us, event | category | flops | bytes accessed | tf_op | source)
XLA Modules:
  0.0 52.9 jit_solution(10626910529750196237)
XLA Ops:
  0.6 0.1 collective-permute-start
  0.7 0.7 %reshape.9.gain_ref = bf16[1,8192]{1,0:T(2,128)(2,1)S(1)} reshape(bf16[8192]{0:T(1024)(128)(2,1)} %param.11) | data formatting | bytes 32768 | tf_op jit(solution)/shard_map/reshape | solution.py:349
  1.5 0.0 copy-start.1
  1.5 0.6 %copy-done.1 = s32[1,8]{1,0:T(1,128)S(1)} copy-done((s32[1,8]{1,0:T(1,128)S(1)}, s32[1,8]{1,0:T(1,128)}, u32[]{:S(2)}) %copy-start.1) | copy-done | bytes 56
  2.1 8.0 %own_rows.1 = (bf16[384,512]{1,0:T(8,128)(2,1)S(1)}, f32[384,128]{1,0:T(8,128)S(1)}, f32[768,128]{1,0:T(8,128)S(1)}, f32[768,128]{1,0:T(8,128)S(1)}, bf16[8192,2...) custom-call(s32[1,8]{1,0:T(1,128)S(1)} %copy-done.1, bf16[384,8192]{1,0:T(8,128)(2,1)} %h_hbm.1, ...), custom_call_target="tpu_custom_call" | custom-call | flops 3221225472 | bytes 14680064 | tf_op jit(solution)/shard_map/own_rows/pallas_call | solution.py:120
  10.2 0.6 %collective-permute-start.1 = (f32[384,128]{1,0:T(8,128)S(1)}, f32[384,128]{1,0:T(8,128)S(1)}, u32[]{:S(2)}, u32[]{:S(2)}) collective-permute-start(f32[384,128]{1,0:T(8,128)S(1)} %get-tuple-element.29), channel_id=1, source_target_pairs={{0,1},{1,0},{2,3},{3,2},{4,5},{5,4},{6,7},{7,6},{8,9},{9,8},{10,11... | collective-permute-start | bytes 589832 | tf_op jit(solution)/shard_map/ppermute | solution.py:361
  10.7 0.3 collective-permute-done.h_ref
  11.1 3.5 %first_block.1 = bf16[2,192,256]{2,1,0:T(8,128)(2,1)S(1)} custom-call(s32[1,8]{1,0:T(1,128)S(1)} %copy-done.1, s32[1,8]{1,0:T(1,128)S(1)} %copy-done.2, s32[1,8]{1,0:T(1,128)S(1)} %copy-done.3, s32[1,8]{1,0:T(1,128)S(1)} %copy-done.4, bf16[384,8192]{1,0:T(8,128)(2,1)S(1)} %collective-permute-done.h_ref, bf16[8192,256]{1,0:T(8,128)(2,1)S(1)} %get-tuple-element.24.wk_ref, ...), custom_call_target="tpu_custom_call" | custom-call | flops 1744830464 | bytes 11796480 | tf_op jit(solution)/shard_map/first_block/pallas_call | solution.py:203
  14.6 0.0 copy-start
  14.6 0.5 collective-permute-start.2
  15.1 0.0 collective-permute-done.1.factor_ref
  15.1 4.7 %peer_rows.1 = (bf16[768,512]{1,0:T(8,128)(2,1)S(1)}, bf16[2,192,256]{2,1,0:T(8,128)(2,1)S(1)}, bf16[2,192,256]{2,1,0:T(8,128)(2,1)S(1)}, bf16[2,192,256]{2,1,0:...) custom-call(s32[1,8]{1,0:T(1,128)S(1)} %copy-done.1, ...), custom_call_target="tpu_custom_call" | custom-call | flops 3221225472 | bytes 14680064 | tf_op jit(solution)/shard_map/peer_rows/pallas_call | solution.py:246
  19.9 4.5 %collective-permute-start.5 = (bf16[2,192,256]{2,1,0:T(8,128)(2,1)S(1)}, bf16[2,192,256]{2,1,0:T(8,128)(2,1)S(1)}, u32[]{:S(2)}, u32[]{:S(2)}) collective-permute-start(bf16[2,192,256]{2,1,0:T(8,128)(2,1)S(1)} %get-tuple-element.37), channel_id=1, source_target_pairs={{0,10},{2,8},{4,14},{6,12},{8,2},{10,0},{12,6},{14,4},{1,11},{3,9}... | collective-permute-start | bytes 589832 | tf_op jit(solution)/shard_map/ppermute | solution.py:356
  24.4 2.0 %collective-permute-start.7 = (bf16[2,192,256]{2,1,0:T(8,128)(2,1)S(1)}, bf16[2,192,256]{2,1,0:T(8,128)(2,1)S(1)}, u32[]{:S(2)}, u32[]{:S(2)}) collective-permute-start(bf16[2,192,256]{2,1,0:T(8,128)(2,1)S(1)} %get-tuple-element.39), channel_id=1, source_target_pairs={{0,6},{2,4},{4,2},{6,0},{8,14},{10,12},{12,10},{14,8},{1,7},{3,5},... | collective-permute-start | bytes 589832 | tf_op jit(solution)/shard_map/ppermute | solution.py:356
  26.3 0.1 collective-permute-start.8
  26.5 4.4 %collective-permute-done.2.refs_1_ = bf16[2,192,256]{2,1,0:T(8,128)(2,1)S(1)} collective-permute-done((bf16[2,192,256]{2,1,0:T(8,128)(2,1)S(1)}, bf16[2,192,256]{2,1,0:T(8,128)(2,1)S(1)}, u32[]{:S(2)}, u32[]{:S(2)}) %collective-permute-start.2) | collective-permute-done | bytes 196640 | tf_op jit(solution)/shard_map/ppermute | solution.py:356
  30.9 1.4 %collective-permute-start.3 = (bf16[2,192,256]{2,1,0:T(8,128)(2,1)S(1)}, bf16[2,192,256]{2,1,0:T(8,128)(2,1)S(1)}, u32[]{:S(2)}, u32[]{:S(2)}) collective-permute-start(bf16[2,192,256]{2,1,0:T(8,128)(2,1)S(1)} %get-tuple-element.33), channel_id=1, source_target_pairs={{0,14},{2,12},{4,10},{6,8},{8,6},{10,4},{12,2},{14,0},{1,15},{3,13... | collective-permute-start | bytes 589832 | tf_op jit(solution)/shard_map/ppermute | solution.py:356
  32.3 0.4 collective-permute-done.5.refs_2_
  32.6 2.0 %collective-permute-start.4 = (bf16[2,192,256]{2,1,0:T(8,128)(2,1)S(1)}, bf16[2,192,256]{2,1,0:T(8,128)(2,1)S(1)}, u32[]{:S(2)}, u32[]{:S(2)}) collective-permute-start(bf16[2,192,256]{2,1,0:T(8,128)(2,1)S(1)} %get-tuple-element.34), channel_id=1, source_target_pairs={{0,2},{2,0},{4,6},{6,4},{8,10},{10,8},{12,14},{14,12},{1,3},{3,1},... | collective-permute-start | bytes 589832 | tf_op jit(solution)/shard_map/ppermute | solution.py:356
  34.6 9.3 %attend.1 = bf16[768,2048]{1,0:T(8,128)(2,1)} custom-call(s32[1,8]{1,0:T(1,128)S(1)} %copy-done.1, bf16[768,2048]{1,0:T(8,128)(2,1)S(1)} %copy-done, bf16[768,512]{1,0:T(8,128)(2,1)S(1)} %get-tuple-element.30.kv_ref), custom_call_target="tpu_custom_call" | custom-call | flops 1610612736 | bytes 6291456 | tf_op jit(solution)/shard_map/attend/pallas_call | solution.py:295
  43.9 1.2 %collective-permute-done.8.refs_5_ = bf16[2,192,256]{2,1,0:T(8,128)(2,1)S(1)} collective-permute-done((bf16[2,192,256]{2,1,0:T(8,128)(2,1)S(1)}, bf16[2,192,256]{2,1,0:T(8,128)(2,1)S(1)}, u32[]{:S(2)}, u32[]{:S(2)}) %collective-permute-start.8) | collective-permute-done | bytes 196640 | tf_op jit(solution)/shard_map/ppermute | solution.py:356
  45.1 1.1 %place_first.1 = (bf16[1536,256]{1,0:T(8,128)(2,1)}, bf16[1536,256]{1,0:T(8,128)(2,1)}) custom-call(bf16[2,192,256]{2,1,0:T(8,128)(2,1)S(1)} %get-tuple-element.35.refs_0_, bf16[2,192,256]{2,1,0:T(8,128)(2,1)S(1)} %collective-permute-done.2.refs_1_, bf16[2,192,256]{2,1,0:T(8,128)(2,1)S(1)} %collective-permute-done.5.refs_2_, ...), custom_call_target="tpu_custom_call" | custom-call | tf_op jit(solution)/shard_map/place_first/pallas_call | solution.py:328
  46.2 5.9 %collective-permute-done.3.refs_0_ = bf16[2,192,256]{2,1,0:T(8,128)(2,1)S(1)} collective-permute-done((bf16[2,192,256]{2,1,0:T(8,128)(2,1)S(1)}, bf16[2,192,256]{2,1,0:T(8,128)(2,1)S(1)}, u32[]{:S(2)}, u32[]{:S(2)}) %collective-permute-start.3) | collective-permute-done | bytes 196640 | tf_op jit(solution)/shard_map/ppermute | solution.py:356
  52.1 0.8 %place_rest.1 = (bf16[1536,256]{1,0:T(8,128)(2,1)}, bf16[1536,256]{1,0:T(8,128)(2,1)}) custom-call(bf16[2,192,256]{2,1,0:T(8,128)(2,1)S(1)} %collective-permute-done.3.refs_0_, bf16[2,192,256]{2,1,0:T(8,128)(2,1)S(1)} %collective-permute-done.4.refs_1_, bf16[1536,256]{1,0:T(8,128)(2,1)} %get-tuple-element.41.refs_2_, ...), custom_call_target="tpu_custom_call", output_to_operand_aliasing={{0}: (2, {}), {1}: (3, {})} | custom-call | tf_op jit(solution)/shard_map/place_rest/pallas_call | solution.py:328
  (11 shorter events, 0.0 us)
Async XLA Ops:
  0.6 10.4 %collective-permute-start = (bf16[384,8192]{1,0:T(8,128)(2,1)}, bf16[384,8192]{1,0:T(8,128)(2,1)S(1)}, u32[]{:S(2)}, u32[]{:S(2)}) collective-permute-start(bf16[384,8192]{1,0:T(8,128)(2,1)} %h_hbm.1), channel_id=1, source_target_pairs={{0,1},{1,0},{2,3},{3,2},{4,5},{5,4},{6,7},{7,6},{8,9},{9,8},{10,11... | collective-permute-start | bytes 18874376 | tf_op jit(solution)/shard_map/ppermute | solution.py:351
  1.5 0.7 %copy-start.1 = (s32[1,8]{1,0:T(1,128)S(1)}, s32[1,8]{1,0:T(1,128)}, u32[]{:S(2)}) copy-start(s32[1,8]{1,0:T(1,128)} %offset_ref.7) | copy-start | bytes 100
  2.1 9.0 %copy-start.2 = (s32[1,8]{1,0:T(1,128)S(1)}, s32[1,8]{1,0:T(1,128)}, u32[]{:S(2)}) copy-start(s32[1,8]{1,0:T(1,128)} %length_ref.3) | copy-start | bytes 100
  2.1 9.0 %copy-start.3 = (s32[1,8]{1,0:T(1,128)S(1)}, s32[1,8]{1,0:T(1,128)}, u32[]{:S(2)}) copy-start(s32[1,8]{1,0:T(1,128)} %owner_ref.3) | copy-start | bytes 100
  2.1 9.0 %copy-start.4 = (s32[1,8]{1,0:T(1,128)S(1)}, s32[1,8]{1,0:T(1,128)}, u32[]{:S(2)}) copy-start(s32[1,8]{1,0:T(1,128)} %slot_ref.3) | copy-start | bytes 100
  10.2 5.0 %collective-permute-start.1 = (f32[384,128]{1,0:T(8,128)S(1)}, f32[384,128]{1,0:T(8,128)S(1)}, u32[]{:S(2)}, u32[]{:S(2)}) collective-permute-start(f32[384,128]{1,0:T(8,128)S(1)} %get-tuple-element.29), channel_id=1, source_target_pairs={{0,1},{1,0},{2,3},{3,2},{4,5},{5,4},{6,7},{7,6},{8,9},{9,8},{10,11... | collective-permute-start | bytes 589832 | tf_op jit(solution)/shard_map/ppermute | solution.py:361
  14.6 20.0 %copy-start = (bf16[768,2048]{1,0:T(8,128)(2,1)S(1)}, bf16[768,2048]{1,0:T(8,128)(2,1)}, u32[]{:S(2)}) copy-start(bf16[768,2048]{1,0:T(8,128)(2,1)} %q_ref.1) | copy-start | bytes 9437188
  14.6 16.2 %collective-permute-start.2 = (bf16[2,192,256]{2,1,0:T(8,128)(2,1)S(1)}, bf16[2,192,256]{2,1,0:T(8,128)(2,1)S(1)}, u32[]{:S(2)}, u32[]{:S(2)}) collective-permute-start(bf16[2,192,256]{2,1,0:T(8,128)(2,1)S(1)} %first_block.1), channel_id=1, source_target_pairs={{0,12},{2,14},{4,8},{6,10},{8,4},{10,6},{12,0},{14,2},{1,13},{3,15... | collective-permute-start | bytes 589832 | tf_op jit(solution)/shard_map/ppermute | solution.py:356
  19.9 12.8 %collective-permute-start.5 = (bf16[2,192,256]{2,1,0:T(8,128)(2,1)S(1)}, bf16[2,192,256]{2,1,0:T(8,128)(2,1)S(1)}, u32[]{:S(2)}, u32[]{:S(2)}) collective-permute-start(bf16[2,192,256]{2,1,0:T(8,128)(2,1)S(1)} %get-tuple-element.37), channel_id=1, source_target_pairs={{0,10},{2,8},{4,14},{6,12},{8,2},{10,0},{12,6},{14,4},{1,11},{3,9}... | collective-permute-start | bytes 589832 | tf_op jit(solution)/shard_map/ppermute | solution.py:356
  24.4 19.5 %collective-permute-start.6 = (bf16[2,192,256]{2,1,0:T(8,128)(2,1)S(1)}, bf16[2,192,256]{2,1,0:T(8,128)(2,1)S(1)}, u32[]{:S(2)}, u32[]{:S(2)}) collective-permute-start(bf16[2,192,256]{2,1,0:T(8,128)(2,1)S(1)} %get-tuple-element.38), channel_id=1, source_target_pairs={{0,4},{2,6},{4,0},{6,2},{8,12},{10,14},{12,8},{14,10},{1,5},{3,7},... | collective-permute-start | bytes 589832 | tf_op jit(solution)/shard_map/ppermute | solution.py:356
  24.4 19.5 %collective-permute-start.7 = (bf16[2,192,256]{2,1,0:T(8,128)(2,1)S(1)}, bf16[2,192,256]{2,1,0:T(8,128)(2,1)S(1)}, u32[]{:S(2)}, u32[]{:S(2)}) collective-permute-start(bf16[2,192,256]{2,1,0:T(8,128)(2,1)S(1)} %get-tuple-element.39), channel_id=1, source_target_pairs={{0,6},{2,4},{4,2},{6,0},{8,14},{10,12},{12,10},{14,8},{1,7},{3,5},... | collective-permute-start | bytes 589832 | tf_op jit(solution)/shard_map/ppermute | solution.py:356
  26.3 18.8 %collective-permute-start.8 = (bf16[2,192,256]{2,1,0:T(8,128)(2,1)S(1)}, bf16[2,192,256]{2,1,0:T(8,128)(2,1)S(1)}, u32[]{:S(2)}, u32[]{:S(2)}) collective-permute-start(bf16[2,192,256]{2,1,0:T(8,128)(2,1)S(1)} %get-tuple-element.40), channel_id=1, source_target_pairs={{0,8},{2,10},{4,12},{6,14},{8,0},{10,2},{12,4},{14,6},{1,9},{3,11}... | collective-permute-start | bytes 589832 | tf_op jit(solution)/shard_map/ppermute | solution.py:356
  30.9 21.3 %collective-permute-start.3 = (bf16[2,192,256]{2,1,0:T(8,128)(2,1)S(1)}, bf16[2,192,256]{2,1,0:T(8,128)(2,1)S(1)}, u32[]{:S(2)}, u32[]{:S(2)}) collective-permute-start(bf16[2,192,256]{2,1,0:T(8,128)(2,1)S(1)} %get-tuple-element.33), channel_id=1, source_target_pairs={{0,14},{2,12},{4,10},{6,8},{8,6},{10,4},{12,2},{14,0},{1,15},{3,13... | collective-permute-start | bytes 589832 | tf_op jit(solution)/shard_map/ppermute | solution.py:356
  32.6 19.5 %collective-permute-start.4 = (bf16[2,192,256]{2,1,0:T(8,128)(2,1)S(1)}, bf16[2,192,256]{2,1,0:T(8,128)(2,1)S(1)}, u32[]{:S(2)}, u32[]{:S(2)}) collective-permute-start(bf16[2,192,256]{2,1,0:T(8,128)(2,1)S(1)} %get-tuple-element.34), channel_id=1, source_target_pairs={{0,2},{2,0},{4,6},{6,4},{8,10},{10,8},{12,14},{14,12},{1,3},{3,1},... | collective-permute-start | bytes 589832 | tf_op jit(solution)/shard_map/ppermute | solution.py:356

commit v6 on v5

--- a/solution.py
+++ b/solution.py
@@ -74,8 +74,8 @@
 
 
 def own_kernel(
-    block, chunk, offset_ref, h_hbm, wk_hbm, wv_hbm, gain_ref,
-    out_ref, factor_ref, cos_ref, sin_ref, wk_ref, wv_ref, h_ref, acc_k, acc_v, squares, cos_pad, sin_pad, sems
+    chunk, h_hbm, wk_hbm, wv_hbm, gain_ref,
+    key_ref, value_ref, factor_ref, wk_ref, wv_ref, h_ref, acc_k, acc_v, squares, sems
 ):
     rows, width = h_hbm.shape
     cols = acc_k.shape[1]
@@ -100,32 +100,52 @@
     for c in range(width // chunk):
         for copy in copies(c)[1:]:
             copy.start()
+    factor = norm_factor(h_ref, slice(None), squares, chunk, ready)
+    factor_ref[...] = jnp.broadcast_to(factor, factor_ref.shape)
+    project(h_ref, slice(None), gain_ref, wk_ref, wv_ref, acc_k, acc_v, factor, chunk, loaded)
+    key_ref[...] = acc_k[...]
+    value_ref[...] = acc_v[...].astype(jnp.bfloat16)
+
+
+def rotate_kernel(block, offset_ref, key_ref, value_ref, out_ref, cos_ref, sin_ref, cos_pad, sin_pad):
+    rows, cols = key_ref.shape
     rotation_tables(block, offset_ref, cos_pad, sin_pad)
     cos_ref[...] = cos_pad[: cos_ref.shape[0], :]
     sin_ref[...] = sin_pad[: sin_ref.shape[0], :]
-    factor = norm_factor(h_ref, slice(None), squares, chunk, ready)
-    factor_ref[...] = jnp.broadcast_to(factor, factor_ref.shape)
-    project(h_ref, slice(None), gain_ref, wk_ref, wv_ref, acc_k, acc_v, factor, chunk, loaded)
     here = pl.ds(pl.multiple_of(lax.axis_index("tensor") * rows, rows), rows)
-    keys, values = finish(cos_pad[here, :], sin_pad[here, :], acc_k, acc_v)
+    keys, values = finish(cos_pad[here, :], sin_pad[here, :], key_ref, value_ref)
     out_ref[:, :cols] = keys
     out_ref[:, cols:] = values
 
 
-def own_rows(block, offsets, hidden, wk, wv, gain, tok_rows, chunk=1024):
+def rotate_own(block, offsets, keys, values):
+    rows, cols = keys.shape
+    table = jax.ShapeDtypeStruct((2 * rows, HD), jnp.float32)
+    pad = pltpu.VMEM((2 * rows + block, HD), jnp.float32)
+    return pl.pallas_call(
+        functools.partial(rotate_kernel, block),
+        in_specs=[SMEM, VMEM, VMEM],
+        out_specs=[VMEM] * 3,
+        out_shape=[jax.ShapeDtypeStruct((rows, 2 * cols), jnp.bfloat16), table, table],
+        scratch_shapes=[pad, pad],
+        compiler_params=pltpu.CompilerParams(vmem_limit_bytes=28 * MIB),
+        name="rotate_own",
+    )(offsets, keys, values)
+
+
+def own_rows(hidden, wk, wv, gain, chunk=1024):
     rows, width = hidden.shape
     cols = wk.shape[1]
     hbm = pl.BlockSpec(memory_space=pltpu.HBM)
     f32 = jnp.float32
     return pl.pallas_call(
-        functools.partial(own_kernel, block, chunk),
-        in_specs=[SMEM, hbm, hbm, hbm, VMEM],
-        out_specs=[VMEM] * 6,
+        functools.partial(own_kernel, chunk),
+        in_specs=[hbm, hbm, hbm, VMEM],
+        out_specs=[VMEM] * 5,
         out_shape=[
-            jax.ShapeDtypeStruct((rows, 2 * cols), jnp.bfloat16),
+            jax.ShapeDtypeStruct((rows, cols), f32),
+            jax.ShapeDtypeStruct((rows, cols), jnp.bfloat16),
             jax.ShapeDtypeStruct((rows, HD), f32),
-            jax.ShapeDtypeStruct((tok_rows, HD), f32),
-            jax.ShapeDtypeStruct((tok_rows, HD), f32),
             jax.ShapeDtypeStruct(wk.shape, wk.dtype),
             jax.ShapeDtypeStruct(wv.shape, wv.dtype),
         ],
@@ -134,16 +154,14 @@
             pltpu.VMEM((rows, cols), f32),
             pltpu.VMEM((rows, cols), f32),
             pltpu.VMEM((rows, HD), f32),
-            pltpu.VMEM((tok_rows + block, HD), f32),
-            pltpu.VMEM((tok_rows + block, HD), f32),
             pltpu.SemaphoreType.DMA((width // chunk, 3)),
         ],
-        compiler_params=pltpu.CompilerParams(vmem_limit_bytes=44 * MIB),
+        compiler_params=pltpu.CompilerParams(vmem_limit_bytes=45 * MIB),
         cost_estimate=pl.CostEstimate(
             flops=4 * rows * width * cols, bytes_accessed=2 * (rows * width + 2 * width * cols), transcendentals=0
         ),
         name="own_rows",
-    )(offsets, hidden, wk, wv, gain)
+    )(hidden, wk, wv, gain)
 
 
 def select_block(block, cols, owner, places, kv_ref, out_ref):
@@ -173,7 +191,7 @@
 
 def first_kernel(
     owner, block, chunk, offset_ref, length_ref, owner_ref, slot_ref,
-    h_ref, wk_ref, wv_ref, gain_ref, cos_ref, sin_ref, own_ref, block_ref, kv, acc_k, acc_v, squares
+    h_ref, wk_ref, wv_ref, gain_ref, cos_ref, sin_ref, own_ref, factor_ref, block_ref, kv, acc_k, acc_v
 ):
     rows, width = h_ref.shape
     cols = acc_k.shape[1]
@@ -188,7 +206,7 @@
     start = jnp.minimum((offset // 16) * 16, 2 * rows - span)
     local = pl.multiple_of(jnp.clip(start - (1 - mine) * rows, 0, rows - span), 16)
     there = pl.ds(pl.multiple_of((1 - mine) * rows + local, 16), span)
-    factor = norm_factor(h_ref, pl.ds(local, span), squares, chunk)
+    factor = factor_ref[pl.ds(local, span), :1]
     project(h_ref, pl.ds(local, span), gain_ref, wk_ref, wv_ref, acc_k, acc_v, factor, chunk)
     keys, values = finish(cos_ref[there, :], sin_ref[there, :], acc_k, acc_v)
     kv[there, :cols] = keys
@@ -196,27 +214,26 @@
     select_block(block, cols, owner, (offset_ref, length_ref, owner_ref, slot_ref), kv, block_ref)
 
 
-def first_block(owner, block, places, peer, wk, wv, gain, cosine, sine, own, chunk=1024):
+def first_block(owner, block, places, peer, wk, wv, gain, cosine, sine, own, factor, chunk=1024):
     rows, width = peer.shape
     cols = wk.shape[1]
     span = block + 16
     return pl.pallas_call(
         functools.partial(first_kernel, owner, block, chunk),
-        in_specs=[SMEM] * 4 + [VMEM] * 7,
+        in_specs=[SMEM] * 4 + [VMEM] * 8,
         out_specs=VMEM,
         out_shape=jax.ShapeDtypeStruct((2, block, cols), jnp.bfloat16),
         scratch_shapes=[
             pltpu.VMEM((2 * rows, 2 * cols), jnp.bfloat16),
             pltpu.VMEM((span, cols), jnp.float32),
             pltpu.VMEM((span, cols), jnp.float32),
-            pltpu.VMEM((span, HD), jnp.float32),
         ],
         compiler_params=pltpu.CompilerParams(vmem_limit_bytes=28 * MIB),
         cost_estimate=pl.CostEstimate(
             flops=4 * span * width * cols, bytes_accessed=2 * (span * width + 2 * width * cols), transcendentals=0
         ),
         name="first_block",
-    )(*places, peer, wk, wv, gain, cosine, sine, own)
+    )(*places, peer, wk, wv, gain, cosine, sine, own, factor)
 
 
 def peer_kernel(
@@ -349,9 +366,8 @@
     gain = norm_gain.reshape(1, width)
 
     peer = lax.ppermute(hidden, "tensor", [(0, 1), (1, 0)])
-    own, factor, cosine, sine, wk, wv = own_rows(
-        block, prompt_offsets, hidden, key_weight, value_weight, gain, tok_rows
-    )
+    own_k, own_v, factor, wk, wv = own_rows(hidden, key_weight, value_weight, gain)
+    own, cosine, sine = rotate_own(block, prompt_offsets, own_k, own_v)
     places = [prompt_offsets, prompt_lengths, decode_owner, slot_offsets]
     swap = lambda a, k: lax.ppermute(a, "dp", [(p, p ^ k) for p in range(n_dp)]) if k else a
     half_dp = n_dp // 2
@@ -359,7 +375,7 @@
     near = list(range(1, half_dp))
     order = (far[2], far[1], *near[1:], far[0], *far[3:], near[0], 0)
     factor = lax.ppermute(factor, "tensor", [(0, 1), (1, 0)])
-    first = first_block(order[0], block, places, peer, wk, wv, gain, cosine, sine, own)
+    first = first_block(order[0], block, places, peer, wk, wv, gain, cosine, sine, own, factor)
     kv, *blocks = peer_rows(order[1:], block, places, peer, wk, wv, gain, cosine, sine, own, factor)
     first = swap(first, order[0])
     first, *blocks[4:-1] = lax.optimization_barrier((first, *blocks[4:-1]))

time: 53.2 us -> 52.6 us (0.989)
  local copies, waits for them, and re-layouts: 1.41 us -> 0.77 us
    pallas_call x1, Pallas kernels: 3.54 us -> 2.85 us  [first_block(): pl.pallas_call(functools.partial(first_kernel, owner, block, chunk), in_s...]
    unnamed x10, local copies, waits for them, and re-layouts: 0.67 us -> 0.03 us
    pallas_call x1 -> x2, Pallas kernels: 8.04 us -> 8.52 us  [the longest x1 7.37 us: own_rows(): pl.pallas_call(functools.partial(own_kernel, chunk), in_specs=[hbm, hbm,...]
  transfers between devices with their start and end apart: 9 -> 9, of which waited for: 5 -> 5; matrix products, arithmetic and copies ran while one was open for 1% -> 1% of each run, Pallas kernels for 50% -> 45%
where the time goes in v6:
time: 52.6 us; the launch traced here: 52.3 us
  Pallas kernels  27.2 us (52%)
  waiting for transfers between devices  12.5 us (24%)
  starting transfers between devices  11.1 us (21%)
  local copies, waits for them, and re-layouts  0.77 us (1%)
  between operations  0.74 us (1%)
    ppermute x7, waiting for transfers between devices, on_device(): lax.ppermute(a, 'dp', [(p, p ^ k) for p in range(n_dp)])  12 us
    ppermute x7, starting transfers between devices, on_device(): lax.ppermute(a, 'dp', [(p, p ^ k) for p in range(n_dp)])  10.4 us
    pallas_call x1, Pallas kernels, attend(): pl.pallas_call(functools.partial(attend_kernel, tile, window), grid=(rows...  9.29 us
    pallas_call x1, Pallas kernels, own_rows(): pl.pallas_call(functools.partial(own_kernel, chunk), in_specs=[hbm, hbm,...  7.37 us
    pallas_call x1, Pallas kernels, peer_rows(): pl.pallas_call(functools.partial(peer_kernel, far, block, chunk), in_spec...  4.64 us
    pallas_call x1, Pallas kernels, first_block(): pl.pallas_call(functools.partial(first_kernel, owner, block, chunk), in_s...  2.85 us
    pallas_call x2, Pallas kernels, place(): pl.pallas_call(functools.partial(gather_kernel, order, block), in_specs=[...  1.87 us
    pallas_call x1, Pallas kernels, rotate_own(): pl.pallas_call(functools.partial(rotate_kernel, block), in_specs=[SMEM, V...  1.15 us
  transfers between devices with their start and end apart: 9, of which 5 were waited for; matrix products, arithmetic and copies ran while one was open for 1% of the time, Pallas kernels for 45%

profile of v6, /device:TPU:16, one launch (start us, length us, event | category | flops | bytes accessed | tf_op | source)
XLA Modules:
  0.0 52.3 jit_solution(582124552269149497)
XLA Ops:
  0.6 0.1 collective-permute-start
  0.7 0.7 %reshape.9.gain_ref = bf16[1,8192]{1,0:T(2,128)(2,1)S(1)} reshape(bf16[8192]{0:T(1024)(128)(2,1)} %param.11) | data formatting | bytes 32768 | tf_op jit(solution)/shard_map/reshape | solution.py:366
  1.5 0.0 copy-start.1
  1.5 0.0 copy-start.2
  1.5 0.0 copy-start.3
  1.5 7.4 %own_rows.1 = (f32[384,256]{1,0:T(8,128)S(1)}, bf16[384,256]{1,0:T(8,128)(2,1)S(1)}, f32[384,128]{1,0:T(8,128)S(1)}, bf16[8192,256]{1,0:T(8,128)(2,1)S(1)}, bf16[8192,256]{1,0:T(8,128)(2,1)S(1)}) custom-call(bf16[384,8192]{1,0:T(8,128)(2,1)} %h_hbm.1, bf16[8192,256]{1,0:T(8,128)(2,1)} %wk_hbm.1, bf16[8192,256]{1,0:T(8,128)(2,1)} %wv_hbm.1, ...), custom_call_target="tpu_custom_call" | custom-call | flops 3221225472 | bytes 14680064 | tf_op jit(solution)/shard_map/own_rows/pallas_call | solution.py:141
  8.9 0.6 %collective-permute-start.1 = (f32[384,128]{1,0:T(8,128)S(1)}, f32[384,128]{1,0:T(8,128)S(1)}, u32[]{:S(2)}, u32[]{:S(2)}) collective-permute-start(f32[384,128]{1,0:T(8,128)S(1)} %get-tuple-element.33), channel_id=1, source_target_pairs={{0,1},{1,0},{2,3},{3,2},{4,5},{5,4},{6,7},{7,6},{8,9},{9,8},{10,11... | collective-permute-start | bytes 589832 | tf_op jit(solution)/shard_map/ppermute | solution.py:377
  9.4 1.2 %rotate_own.1 = (bf16[384,512]{1,0:T(8,128)(2,1)S(1)}, f32[768,128]{1,0:T(8,128)S(1)}, f32[768,128]{1,0:T(8,128)S(1)}) custom-call(s32[1,8]{1,0:T(1,128)S(1)} %copy-done.1, f32[384,256]{1,0:T(8,128)S(1)} %get-tuple-element.28.key_ref, bf16[384,256]{1,0:T(8,128)(2,1)S(1)} %get-tuple-element.29.value_ref), custom_call_target="tpu_custom_call" | custom-call | tf_op jit(solution)/shard_map/rotate_own/pallas_call | solution.py:125
  10.6 0.5 %collective-permute-done.1.factor_ref = f32[384,128]{1,0:T(8,128)S(1)} collective-permute-done((f32[384,128]{1,0:T(8,128)S(1)}, f32[384,128]{1,0:T(8,128)S(1)}, u32[]{:S(2)}, u32[]{:S(2)}) %collective-permute-start.1) | collective-permute-done | bytes 196640 | tf_op jit(solution)/shard_map/ppermute | solution.py:377
  11.2 2.9 %first_block.1 = bf16[2,192,256]{2,1,0:T(8,128)(2,1)S(1)} custom-call(s32[1,8]{1,0:T(1,128)S(1)} %copy-done.1, s32[1,8]{1,0:T(1,128)S(1)} %copy-done.2, s32[1,8]{1,0:T(1,128)S(1)} %copy-done.3, s32[1,8]{1,0:T(1,128)S(1)} %copy-done.4, bf16[384,8192]{1,0:T(8,128)(2,1)S(1)} %collective-permute-done.h_ref, bf16[8192,256]{1,0:T(8,128)(2,1)S(1)} %get-tuple-element.26.wk_ref, ...), custom_call_target="tpu_custom_call" | custom-call | flops 1744830464 | bytes 11796480 | tf_op jit(solution)/shard_map/first_block/pallas_call | solution.py:221
  14.0 0.5 collective-permute-start.2
  14.5 4.6 %peer_rows.1 = (bf16[768,512]{1,0:T(8,128)(2,1)S(1)}, bf16[2,192,256]{2,1,0:T(8,128)(2,1)S(1)}, bf16[2,192,256]{2,1,0:T(8,128)(2,1)S(1)}, bf16[2,192,256]{2,1,0:...) custom-call(s32[1,8]{1,0:T(1,128)S(1)} %copy-done.1, ...), custom_call_target="tpu_custom_call" | custom-call | flops 3221225472 | bytes 14680064 | tf_op jit(solution)/shard_map/peer_rows/pallas_call | solution.py:263
  19.2 4.5 %collective-permute-start.5 = (bf16[2,192,256]{2,1,0:T(8,128)(2,1)S(1)}, bf16[2,192,256]{2,1,0:T(8,128)(2,1)S(1)}, u32[]{:S(2)}, u32[]{:S(2)}) collective-permute-start(bf16[2,192,256]{2,1,0:T(8,128)(2,1)S(1)} %get-tuple-element.41), channel_id=1, source_target_pairs={{0,10},{2,8},{4,14},{6,12},{8,2},{10,0},{12,6},{14,4},{1,11},{3,9}... | collective-permute-start | bytes 589832 | tf_op jit(solution)/shard_map/ppermute | solution.py:372
  23.7 2.0 %collective-permute-start.7 = (bf16[2,192,256]{2,1,0:T(8,128)(2,1)S(1)}, bf16[2,192,256]{2,1,0:T(8,128)(2,1)S(1)}, u32[]{:S(2)}, u32[]{:S(2)}) collective-permute-start(bf16[2,192,256]{2,1,0:T(8,128)(2,1)S(1)} %get-tuple-element.43), channel_id=1, source_target_pairs={{0,6},{2,4},{4,2},{6,0},{8,14},{10,12},{12,10},{14,8},{1,7},{3,5},... | collective-permute-start | bytes 589832 | tf_op jit(solution)/shard_map/ppermute | solution.py:372
  25.7 0.1 collective-permute-start.8
  25.8 4.5 %collective-permute-done.2.refs_1_ = bf16[2,192,256]{2,1,0:T(8,128)(2,1)S(1)} collective-permute-done((bf16[2,192,256]{2,1,0:T(8,128)(2,1)S(1)}, bf16[2,192,256]{2,1,0:T(8,128)(2,1)S(1)}, u32[]{:S(2)}, u32[]{:S(2)}) %collective-permute-start.2) | collective-permute-done | bytes 196640 | tf_op jit(solution)/shard_map/ppermute | solution.py:372
  30.3 1.4 %collective-permute-start.3 = (bf16[2,192,256]{2,1,0:T(8,128)(2,1)S(1)}, bf16[2,192,256]{2,1,0:T(8,128)(2,1)S(1)}, u32[]{:S(2)}, u32[]{:S(2)}) collective-permute-start(bf16[2,192,256]{2,1,0:T(8,128)(2,1)S(1)} %get-tuple-element.37), channel_id=1, source_target_pairs={{0,14},{2,12},{4,10},{6,8},{8,6},{10,4},{12,2},{14,0},{1,15},{3,13... | collective-permute-start | bytes 589832 | tf_op jit(solution)/shard_map/ppermute | solution.py:372
  31.7 0.4 collective-permute-done.5.refs_2_
  32.1 1.9 %collective-permute-start.4 = (bf16[2,192,256]{2,1,0:T(8,128)(2,1)S(1)}, bf16[2,192,256]{2,1,0:T(8,128)(2,1)S(1)}, u32[]{:S(2)}, u32[]{:S(2)}) collective-permute-start(bf16[2,192,256]{2,1,0:T(8,128)(2,1)S(1)} %get-tuple-element.38), channel_id=1, source_target_pairs={{0,2},{2,0},{4,6},{6,4},{8,10},{10,8},{12,14},{14,12},{1,3},{3,1},... | collective-permute-start | bytes 589832 | tf_op jit(solution)/shard_map/ppermute | solution.py:372
  34.0 9.3 %attend.1 = bf16[768,2048]{1,0:T(8,128)(2,1)} custom-call(s32[1,8]{1,0:T(1,128)S(1)} %copy-done.1, bf16[768,2048]{1,0:T(8,128)(2,1)S(1)} %copy-done, bf16[768,512]{1,0:T(8,128)(2,1)S(1)} %get-tuple-element.34.kv_ref), custom_call_target="tpu_custom_call" | custom-call | flops 1610612736 | bytes 6291456 | tf_op jit(solution)/shard_map/attend/pallas_call | solution.py:312
  43.3 1.4 %collective-permute-done.8.refs_5_ = bf16[2,192,256]{2,1,0:T(8,128)(2,1)S(1)} collective-permute-done((bf16[2,192,256]{2,1,0:T(8,128)(2,1)S(1)}, bf16[2,192,256]{2,1,0:T(8,128)(2,1)S(1)}, u32[]{:S(2)}, u32[]{:S(2)}) %collective-permute-start.8) | collective-permute-done | bytes 196640 | tf_op jit(solution)/shard_map/ppermute | solution.py:372
  44.7 1.1 %place_first.1 = (bf16[1536,256]{1,0:T(8,128)(2,1)}, bf16[1536,256]{1,0:T(8,128)(2,1)}) custom-call(bf16[2,192,256]{2,1,0:T(8,128)(2,1)S(1)} %get-tuple-element.39.refs_0_, bf16[2,192,256]{2,1,0:T(8,128)(2,1)S(1)} %collective-permute-done.2.refs_1_, bf16[2,192,256]{2,1,0:T(8,128)(2,1)S(1)} %collective-permute-done.5.refs_2_, ...), custom_call_target="tpu_custom_call" | custom-call | tf_op jit(solution)/shard_map/place_first/pallas_call | solution.py:345
  45.8 5.7 %collective-permute-done.3.refs_0_ = bf16[2,192,256]{2,1,0:T(8,128)(2,1)S(1)} collective-permute-done((bf16[2,192,256]{2,1,0:T(8,128)(2,1)S(1)}, bf16[2,192,256]{2,1,0:T(8,128)(2,1)S(1)}, u32[]{:S(2)}, u32[]{:S(2)}) %collective-permute-start.3) | collective-permute-done | bytes 196640 | tf_op jit(solution)/shard_map/ppermute | solution.py:372
  51.5 0.8 %place_rest.1 = (bf16[1536,256]{1,0:T(8,128)(2,1)}, bf16[1536,256]{1,0:T(8,128)(2,1)}) custom-call(bf16[2,192,256]{2,1,0:T(8,128)(2,1)S(1)} %collective-permute-done.3.refs_0_, bf16[2,192,256]{2,1,0:T(8,128)(2,1)S(1)} %collective-permute-done.4.refs_1_, bf16[1536,256]{1,0:T(8,128)(2,1)} %get-tuple-element.45.refs_2_, ...), custom_call_target="tpu_custom_call", output_to_operand_aliasing={{0}: (2, {}), {1}: (3, {})} | custom-call | tf_op jit(solution)/shard_map/place_rest/pallas_call | solution.py:345
  (12 shorter events, 0.0 us)
Async XLA Ops:
  0.6 10.5 %collective-permute-start = (bf16[384,8192]{1,0:T(8,128)(2,1)}, bf16[384,8192]{1,0:T(8,128)(2,1)S(1)}, u32[]{:S(2)}, u32[]{:S(2)}) collective-permute-start(bf16[384,8192]{1,0:T(8,128)(2,1)} %h_hbm.1), channel_id=1, source_target_pairs={{0,1},{1,0},{2,3},{3,2},{4,5},{5,4},{6,7},{7,6},{8,9},{9,8},{10,11... | collective-permute-start | bytes 18874376 | tf_op jit(solution)/shard_map/ppermute | solution.py:368
  1.5 8.0 %copy-start.1 = (s32[1,8]{1,0:T(1,128)S(1)}, s32[1,8]{1,0:T(1,128)}, u32[]{:S(2)}) copy-start(s32[1,8]{1,0:T(1,128)} %offset_ref.7) | copy-start | bytes 100
  1.5 9.7 %copy-start.2 = (s32[1,8]{1,0:T(1,128)S(1)}, s32[1,8]{1,0:T(1,128)}, u32[]{:S(2)}) copy-start(s32[1,8]{1,0:T(1,128)} %length_ref.3) | copy-start | bytes 100
  1.5 9.7 %copy-start.3 = (s32[1,8]{1,0:T(1,128)S(1)}, s32[1,8]{1,0:T(1,128)}, u32[]{:S(2)}) copy-start(s32[1,8]{1,0:T(1,128)} %owner_ref.3) | copy-start | bytes 100
  1.5 9.7 %copy-start.4 = (s32[1,8]{1,0:T(1,128)S(1)}, s32[1,8]{1,0:T(1,128)}, u32[]{:S(2)}) copy-start(s32[1,8]{1,0:T(1,128)} %slot_ref.3) | copy-start | bytes 100
  8.9 2.3 %collective-permute-start.1 = (f32[384,128]{1,0:T(8,128)S(1)}, f32[384,128]{1,0:T(8,128)S(1)}, u32[]{:S(2)}, u32[]{:S(2)}) collective-permute-start(f32[384,128]{1,0:T(8,128)S(1)} %get-tuple-element.33), channel_id=1, source_target_pairs={{0,1},{1,0},{2,3},{3,2},{4,5},{5,4},{6,7},{7,6},{8,9},{9,8},{10,11... | collective-permute-start | bytes 589832 | tf_op jit(solution)/shard_map/ppermute | solution.py:377
  14.0 20.0 %copy-start = (bf16[768,2048]{1,0:T(8,128)(2,1)S(1)}, bf16[768,2048]{1,0:T(8,128)(2,1)}, u32[]{:S(2)}) copy-start(bf16[768,2048]{1,0:T(8,128)(2,1)} %q_ref.1) | copy-start | bytes 9437188
  14.0 16.2 %collective-permute-start.2 = (bf16[2,192,256]{2,1,0:T(8,128)(2,1)S(1)}, bf16[2,192,256]{2,1,0:T(8,128)(2,1)S(1)}, u32[]{:S(2)}, u32[]{:S(2)}) collective-permute-start(bf16[2,192,256]{2,1,0:T(8,128)(2,1)S(1)} %first_block.1), channel_id=1, source_target_pairs={{0,12},{2,14},{4,8},{6,10},{8,4},{10,6},{12,0},{14,2},{1,13},{3,15... | collective-permute-start | bytes 589832 | tf_op jit(solution)/shard_map/ppermute | solution.py:372
  19.2 12.9 %collective-permute-start.5 = (bf16[2,192,256]{2,1,0:T(8,128)(2,1)S(1)}, bf16[2,192,256]{2,1,0:T(8,128)(2,1)S(1)}, u32[]{:S(2)}, u32[]{:S(2)}) collective-permute-start(bf16[2,192,256]{2,1,0:T(8,128)(2,1)S(1)} %get-tuple-element.41), channel_id=1, source_target_pairs={{0,10},{2,8},{4,14},{6,12},{8,2},{10,0},{12,6},{14,4},{1,11},{3,9}... | collective-permute-start | bytes 589832 | tf_op jit(solution)/shard_map/ppermute | solution.py:372
  23.7 19.6 %collective-permute-start.6 = (bf16[2,192,256]{2,1,0:T(8,128)(2,1)S(1)}, bf16[2,192,256]{2,1,0:T(8,128)(2,1)S(1)}, u32[]{:S(2)}, u32[]{:S(2)}) collective-permute-start(bf16[2,192,256]{2,1,0:T(8,128)(2,1)S(1)} %get-tuple-element.42), channel_id=1, source_target_pairs={{0,4},{2,6},{4,0},{6,2},{8,12},{10,14},{12,8},{14,10},{1,5},{3,7},... | collective-permute-start | bytes 589832 | tf_op jit(solution)/shard_map/ppermute | solution.py:372
  23.7 19.6 %collective-permute-start.7 = (bf16[2,192,256]{2,1,0:T(8,128)(2,1)S(1)}, bf16[2,192,256]{2,1,0:T(8,128)(2,1)S(1)}, u32[]{:S(2)}, u32[]{:S(2)}) collective-permute-start(bf16[2,192,256]{2,1,0:T(8,128)(2,1)S(1)} %get-tuple-element.43), channel_id=1, source_target_pairs={{0,6},{2,4},{4,2},{6,0},{8,14},{10,12},{12,10},{14,8},{1,7},{3,5},... | collective-permute-start | bytes 589832 | tf_op jit(solution)/shard_map/ppermute | solution.py:372
  25.7 19.1 %collective-permute-start.8 = (bf16[2,192,256]{2,1,0:T(8,128)(2,1)S(1)}, bf16[2,192,256]{2,1,0:T(8,128)(2,1)S(1)}, u32[]{:S(2)}, u32[]{:S(2)}) collective-permute-start(bf16[2,192,256]{2,1,0:T(8,128)(2,1)S(1)} %get-tuple-element.44), channel_id=1, source_target_pairs={{0,8},{2,10},{4,12},{6,14},{8,0},{10,2},{12,4},{14,6},{1,9},{3,11}... | collective-permute-start | bytes 589832 | tf_op jit(solution)/shard_map/ppermute | solution.py:372
  30.3 21.3 %collective-permute-start.3 = (bf16[2,192,256]{2,1,0:T(8,128)(2,1)S(1)}, bf16[2,192,256]{2,1,0:T(8,128)(2,1)S(1)}, u32[]{:S(2)}, u32[]{:S(2)}) collective-permute-start(bf16[2,192,256]{2,1,0:T(8,128)(2,1)S(1)} %get-tuple-element.37), channel_id=1, source_target_pairs={{0,14},{2,12},{4,10},{6,8},{8,6},{10,4},{12,2},{14,0},{1,15},{3,13... | collective-permute-start | bytes 589832 | tf_op jit(solution)/shard_map/ppermute | solution.py:372
  32.1 19.4 %collective-permute-start.4 = (bf16[2,192,256]{2,1,0:T(8,128)(2,1)S(1)}, bf16[2,192,256]{2,1,0:T(8,128)(2,1)S(1)}, u32[]{:S(2)}, u32[]{:S(2)}) collective-permute-start(bf16[2,192,256]{2,1,0:T(8,128)(2,1)S(1)} %get-tuple-element.38), channel_id=1, source_target_pairs={{0,2},{2,0},{4,6},{6,4},{8,10},{10,8},{12,14},{14,12},{1,3},{3,1},... | collective-permute-start | bytes 589832 | tf_op jit(solution)/shard_map/ppermute | solution.py:372

commit v7 on v6

--- a/solution.py
+++ b/solution.py
@@ -276,6 +276,25 @@
         ),
         name="peer_rows",
     )(*places, peer, wk, wv, gain, cosine, sine, own, factor)
+
+
+def rest_kernel(owners, block, offset_ref, length_ref, owner_ref, slot_ref, kv_ref, *blocks):
+    cols = kv_ref.shape[1] // 2
+    places = (offset_ref, length_ref, owner_ref, slot_ref)
+    for k, out_ref in zip(owners, blocks):
+        select_block(block, cols, jnp.bitwise_xor(lax.axis_index("dp"), k), places, kv_ref, out_ref)
+
+
+def rest_blocks(owners, block, places, kv):
+    one = jax.ShapeDtypeStruct((2, block, kv.shape[1] // 2), jnp.bfloat16)
+    return pl.pallas_call(
+        functools.partial(rest_kernel, owners, block),
+        in_specs=[SMEM] * 4 + [VMEM],
+        out_specs=[VMEM] * len(owners),
+        out_shape=[one] * len(owners),
+        compiler_params=pltpu.CompilerParams(vmem_limit_bytes=28 * MIB),
+        name="rest_blocks",
+    )(*places, kv)
 
 
 def attend_kernel(tile, window, offset_ref, q_ref, kv_ref, out_ref):
@@ -376,9 +395,9 @@
     order = (far[2], far[1], *near[1:], far[0], *far[3:], near[0], 0)
     factor = lax.ppermute(factor, "tensor", [(0, 1), (1, 0)])
     first = first_block(order[0], block, places, peer, wk, wv, gain, cosine, sine, own, factor)
-    kv, *blocks = peer_rows(order[1:], block, places, peer, wk, wv, gain, cosine, sine, own, factor)
-    first = swap(first, order[0])
-    first, *blocks[4:-1] = lax.optimization_barrier((first, *blocks[4:-1]))
+    kv, *blocks = peer_rows(order[1:5], block, places, peer, wk, wv, gain, cosine, sine, own, factor)
+    first, later = lax.optimization_barrier((swap(first, order[0]), kv))
+    blocks += rest_blocks(order[5:], block, places, later)
     received = [first] + [swap(a, k) for k, a in zip(order[1:], blocks)]
     attended = attend(prompt_offsets, queries, kv, block)
     cache = jax.ShapeDtypeStruct((n_dp * block, cols), jnp.bfloat16)

time: 52.6 us -> 52.6 us (level)
  Pallas kernels: 27.2 us -> 28 us
    pallas_call x0 -> x1, Pallas kernels: none -> 0.91 us  [rest_blocks(): pl.pallas_call(functools.partial(rest_kernel, owners, block), in_specs=[S...]
  transfers between devices with their start and end apart: 9 -> 9, of which waited for: 5 -> 4; matrix products, arithmetic and copies ran while one was open for 1% -> 1% of each run, Pallas kernels for 45% -> 47%
where the time goes in v7:
time: 52.6 us; the launch traced here: 52.3 us
  Pallas kernels  28 us (53%)
  waiting for transfers between devices  12.2 us (23%)
  starting transfers between devices  10.6 us (20%)
  local copies, waits for them, and re-layouts  0.77 us (1%)
  between operations  0.75 us (1%)
    ppermute x7, waiting for transfers between devices, on_device(): lax.ppermute(a, 'dp', [(p, p ^ k) for p in range(n_dp)])  11.7 us
    ppermute x7, starting transfers between devices, on_device(): lax.ppermute(a, 'dp', [(p, p ^ k) for p in range(n_dp)])  9.94 us
    pallas_call x1, Pallas kernels, attend(): pl.pallas_call(functools.partial(attend_kernel, tile, window), grid=(rows...  9.33 us
    pallas_call x1, Pallas kernels, own_rows(): pl.pallas_call(functools.partial(own_kernel, chunk), in_specs=[hbm, hbm,...  7.37 us
    pallas_call x1, Pallas kernels, peer_rows(): pl.pallas_call(functools.partial(peer_kernel, far, block, chunk), in_spec...  4.49 us
    pallas_call x1, Pallas kernels, first_block(): pl.pallas_call(functools.partial(first_kernel, owner, block, chunk), in_s...  2.85 us
    pallas_call x2, Pallas kernels, place(): pl.pallas_call(functools.partial(gather_kernel, order, block), in_specs=[...  1.87 us
    pallas_call x1, Pallas kernels, rotate_own(): pl.pallas_call(functools.partial(rotate_kernel, block), in_specs=[SMEM, V...  1.15 us
  transfers between devices with their start and end apart: 9, of which 4 were waited for; matrix products, arithmetic and copies ran while one was open for 1% of the time, Pallas kernels for 47%

profile of v7, /device:TPU:16, one launch (start us, length us, event | category | flops | bytes accessed | tf_op | source)
XLA Modules:
  0.0 52.3 jit_solution(17529813701258377355)
XLA Ops:
  0.6 0.1 collective-permute-start
  0.7 0.7 %reshape.9.gain_ref = bf16[1,8192]{1,0:T(2,128)(2,1)S(1)} reshape(bf16[8192]{0:T(1024)(128)(2,1)} %param.11) | data formatting | bytes 32768 | tf_op jit(solution)/shard_map/reshape | solution.py:385
  1.5 0.0 copy-start.1
  1.5 0.0 copy-start.2
  1.5 0.0 copy-start.4
  1.5 7.4 %own_rows.1 = (f32[384,256]{1,0:T(8,128)S(1)}, bf16[384,256]{1,0:T(8,128)(2,1)S(1)}, f32[384,128]{1,0:T(8,128)S(1)}, bf16[8192,256]{1,0:T(8,128)(2,1)S(1)}, bf16[8192,256]{1,0:T(8,128)(2,1)S(1)}) custom-call(bf16[384,8192]{1,0:T(8,128)(2,1)} %h_hbm.1, bf16[8192,256]{1,0:T(8,128)(2,1)} %wk_hbm.1, bf16[8192,256]{1,0:T(8,128)(2,1)} %wv_hbm.1, ...), custom_call_target="tpu_custom_call" | custom-call | flops 3221225472 | bytes 14680064 | tf_op jit(solution)/shard_map/own_rows/pallas_call | solution.py:141
  8.9 0.6 %collective-permute-start.1 = (f32[384,128]{1,0:T(8,128)S(1)}, f32[384,128]{1,0:T(8,128)S(1)}, u32[]{:S(2)}, u32[]{:S(2)}) collective-permute-start(f32[384,128]{1,0:T(8,128)S(1)} %get-tuple-element.32), channel_id=1, source_target_pairs={{0,1},{1,0},{2,3},{3,2},{4,5},{5,4},{6,7},{7,6},{8,9},{9,8},{10,11... | collective-permute-start | bytes 589832 | tf_op jit(solution)/shard_map/ppermute | solution.py:396
  9.4 1.2 %rotate_own.1 = (bf16[384,512]{1,0:T(8,128)(2,1)S(1)}, f32[768,128]{1,0:T(8,128)S(1)}, f32[768,128]{1,0:T(8,128)S(1)}) custom-call(s32[1,8]{1,0:T(1,128)S(1)} %copy-done.1, f32[384,256]{1,0:T(8,128)S(1)} %get-tuple-element.27.key_ref, bf16[384,256]{1,0:T(8,128)(2,1)S(1)} %get-tuple-element.28.value_ref), custom_call_target="tpu_custom_call" | custom-call | tf_op jit(solution)/shard_map/rotate_own/pallas_call | solution.py:125
  10.6 0.5 %collective-permute-done.1.factor_ref = f32[384,128]{1,0:T(8,128)S(1)} collective-permute-done((f32[384,128]{1,0:T(8,128)S(1)}, f32[384,128]{1,0:T(8,128)S(1)}, u32[]{:S(2)}, u32[]{:S(2)}) %collective-permute-start.1) | collective-permute-done | bytes 196640 | tf_op jit(solution)/shard_map/ppermute | solution.py:396
  11.2 2.9 %first_block.1 = bf16[2,192,256]{2,1,0:T(8,128)(2,1)S(1)} custom-call(s32[1,8]{1,0:T(1,128)S(1)} %copy-done.1, s32[1,8]{1,0:T(1,128)S(1)} %copy-done.2, s32[1,8]{1,0:T(1,128)S(1)} %copy-done.3, s32[1,8]{1,0:T(1,128)S(1)} %copy-done.4, bf16[384,8192]{1,0:T(8,128)(2,1)S(1)} %collective-permute-done.h_ref, bf16[8192,256]{1,0:T(8,128)(2,1)S(1)} %get-tuple-element.25.wk_ref, ...), custom_call_target="tpu_custom_call" | custom-call | flops 1744830464 | bytes 11796480 | tf_op jit(solution)/shard_map/first_block/pallas_call | solution.py:221
  14.0 0.5 collective-permute-start.2
  14.5 4.5 %peer_rows.1 = (bf16[768,512]{1,0:T(8,128)(2,1)S(1)}, bf16[2,192,256]{2,1,0:T(8,128)(2,1)S(1)}, bf16[2,192,256]{2,1,0:T(8,128)(2,1)S(1)}, bf16[2,192,256]{2,1,0:T(8,128)(2,1)S(1)}, bf16[2,192,256]{2,1,0:T(8,128)(2,1)S(1)}) custom-call(s32[1,8]{1,0:T(1,128)S(1)} %copy-done.1, s32[1,8]{1,0:T(1,128)S(1)} %copy-done.2, s32[1,8]{1,0:T(1,128)S(1)} %copy-done.3, ...), custom_call_target="tpu_custom_call" | custom-call | flops 3221225472 | bytes 14680064 | tf_op jit(solution)/shard_map/peer_rows/pallas_call | solution.py:263
  19.0 4.5 %collective-permute-start.5 = (bf16[2,192,256]{2,1,0:T(8,128)(2,1)S(1)}, bf16[2,192,256]{2,1,0:T(8,128)(2,1)S(1)}, u32[]{:S(2)}, u32[]{:S(2)}) collective-permute-start(bf16[2,192,256]{2,1,0:T(8,128)(2,1)S(1)} %get-tuple-element.39), channel_id=1, source_target_pairs={{0,10},{2,8},{4,14},{6,12},{8,2},{10,0},{12,6},{14,4},{1,11},{3,9}... | collective-permute-start | bytes 589832 | tf_op jit(solution)/shard_map/ppermute | solution.py:391
  23.5 2.0 %collective-permute-start.7 = (bf16[2,192,256]{2,1,0:T(8,128)(2,1)S(1)}, bf16[2,192,256]{2,1,0:T(8,128)(2,1)S(1)}, u32[]{:S(2)}, u32[]{:S(2)}) collective-permute-start(bf16[2,192,256]{2,1,0:T(8,128)(2,1)S(1)} %get-tuple-element.41), channel_id=1, source_target_pairs={{0,6},{2,4},{4,2},{6,0},{8,14},{10,12},{12,10},{14,8},{1,7},{3,5},... | collective-permute-start | bytes 589832 | tf_op jit(solution)/shard_map/ppermute | solution.py:391
  25.5 0.1 collective-permute-start.8
  25.6 4.6 %collective-permute-done.2.refs_1_ = bf16[2,192,256]{2,1,0:T(8,128)(2,1)S(1)} collective-permute-done((bf16[2,192,256]{2,1,0:T(8,128)(2,1)S(1)}, bf16[2,192,256]{2,1,0:T(8,128)(2,1)S(1)}, u32[]{:S(2)}, u32[]{:S(2)}) %collective-permute-start.2) | collective-permute-done | bytes 196640 | tf_op jit(solution)/shard_map/ppermute | solution.py:391
  30.3 0.9 %rest_blocks.1 = (bf16[2,192,256]{2,1,0:T(8,128)(2,1)S(1)}, bf16[2,192,256]{2,1,0:T(8,128)(2,1)S(1)}, bf16[2,192,256]{2,1,0:T(8,128)(2,1)S(1)}) custom-call(s32[1,8]{1,0:T(1,128)S(1)} %copy-done.1, s32[1,8]{1,0:T(1,128)S(1)} %copy-done.2, s32[1,8]{1,0:T(1,128)S(1)} %copy-done.3, s32[1,8]{1,0:T(1,128)S(1)} %copy-done.4, ...), custom_call_target="tpu_custom_call" | custom-call | tf_op jit(solution)/shard_map/rest_blocks/pallas_call | solution.py:290
  31.2 1.5 %collective-permute-start.3 = (bf16[2,192,256]{2,1,0:T(8,128)(2,1)S(1)}, bf16[2,192,256]{2,1,0:T(8,128)(2,1)S(1)}, u32[]{:S(2)}, u32[]{:S(2)}) collective-permute-start(bf16[2,192,256]{2,1,0:T(8,128)(2,1)S(1)} %get-tuple-element.35), channel_id=1, source_target_pairs={{0,14},{2,12},{4,10},{6,8},{8,6},{10,4},{12,2},{14,0},{1,15},{3,13... | collective-permute-start | bytes 589832 | tf_op jit(solution)/shard_map/ppermute | solution.py:391
  32.7 1.4 %collective-permute-start.4 = (bf16[2,192,256]{2,1,0:T(8,128)(2,1)S(1)}, bf16[2,192,256]{2,1,0:T(8,128)(2,1)S(1)}, u32[]{:S(2)}, u32[]{:S(2)}) collective-permute-start(bf16[2,192,256]{2,1,0:T(8,128)(2,1)S(1)} %get-tuple-element.36), channel_id=1, source_target_pairs={{0,2},{2,0},{4,6},{6,4},{8,10},{10,8},{12,14},{14,12},{1,3},{3,1},... | collective-permute-start | bytes 589832 | tf_op jit(solution)/shard_map/ppermute | solution.py:391
  34.0 9.3 %attend.1 = bf16[768,2048]{1,0:T(8,128)(2,1)} custom-call(s32[1,8]{1,0:T(1,128)S(1)} %copy-done.1, bf16[768,2048]{1,0:T(8,128)(2,1)S(1)} %copy-done, bf16[768,512]{1,0:T(8,128)(2,1)S(1)} %get-tuple-element.34.kv_ref), custom_call_target="tpu_custom_call" | custom-call | flops 1610612736 | bytes 6291456 | tf_op jit(solution)/shard_map/attend/pallas_call | solution.py:331
  43.3 1.5 %collective-permute-done.8.refs_5_ = bf16[2,192,256]{2,1,0:T(8,128)(2,1)S(1)} collective-permute-done((bf16[2,192,256]{2,1,0:T(8,128)(2,1)S(1)}, bf16[2,192,256]{2,1,0:T(8,128)(2,1)S(1)}, u32[]{:S(2)}, u32[]{:S(2)}) %collective-permute-start.8) | collective-permute-done | bytes 196640 | tf_op jit(solution)/shard_map/ppermute | solution.py:391
  44.9 1.1 %place_first.1 = (bf16[1536,256]{1,0:T(8,128)(2,1)}, bf16[1536,256]{1,0:T(8,128)(2,1)}) custom-call(bf16[2,192,256]{2,1,0:T(8,128)(2,1)S(1)} %get-tuple-element.37.refs_0_, bf16[2,192,256]{2,1,0:T(8,128)(2,1)S(1)} %collective-permute-done.2.refs_1_, bf16[2,192,256]{2,1,0:T(8,128)(2,1)S(1)} %collective-permute-done.5.refs_2_, ...), custom_call_target="tpu_custom_call" | custom-call | tf_op jit(solution)/shard_map/place_first/pallas_call | solution.py:364
  46.0 5.6 %collective-permute-done.3.refs_0_ = bf16[2,192,256]{2,1,0:T(8,128)(2,1)S(1)} collective-permute-done((bf16[2,192,256]{2,1,0:T(8,128)(2,1)S(1)}, bf16[2,192,256]{2,1,0:T(8,128)(2,1)S(1)}, u32[]{:S(2)}, u32[]{:S(2)}) %collective-permute-start.3) | collective-permute-done | bytes 196640 | tf_op jit(solution)/shard_map/ppermute | solution.py:391
  51.5 0.8 %place_rest.1 = (bf16[1536,256]{1,0:T(8,128)(2,1)}, bf16[1536,256]{1,0:T(8,128)(2,1)}) custom-call(bf16[2,192,256]{2,1,0:T(8,128)(2,1)S(1)} %collective-permute-done.3.refs_0_, bf16[2,192,256]{2,1,0:T(8,128)(2,1)S(1)} %collective-permute-done.4.refs_1_, bf16[1536,256]{1,0:T(8,128)(2,1)} %get-tuple-element.43.refs_2_, ...), custom_call_target="tpu_custom_call", output_to_operand_aliasing={{0}: (2, {}), {1}: (3, {})} | custom-call | tf_op jit(solution)/shard_map/place_rest/pallas_call | solution.py:364
  (13 shorter events, 0.0 us)
Async XLA Ops:
  0.6 10.5 %collective-permute-start = (bf16[384,8192]{1,0:T(8,128)(2,1)}, bf16[384,8192]{1,0:T(8,128)(2,1)S(1)}, u32[]{:S(2)}, u32[]{:S(2)}) collective-permute-start(bf16[384,8192]{1,0:T(8,128)(2,1)} %h_hbm.1), channel_id=1, source_target_pairs={{0,1},{1,0},{2,3},{3,2},{4,5},{5,4},{6,7},{7,6},{8,9},{9,8},{10,11... | collective-permute-start | bytes 18874376 | tf_op jit(solution)/shard_map/ppermute | solution.py:387
  1.5 8.0 %copy-start.1 = (s32[1,8]{1,0:T(1,128)S(1)}, s32[1,8]{1,0:T(1,128)}, u32[]{:S(2)}) copy-start(s32[1,8]{1,0:T(1,128)} %offset_ref.9) | copy-start | bytes 100
  1.5 9.7 %copy-start.2 = (s32[1,8]{1,0:T(1,128)S(1)}, s32[1,8]{1,0:T(1,128)}, u32[]{:S(2)}) copy-start(s32[1,8]{1,0:T(1,128)} %length_ref.5) | copy-start | bytes 100
  1.5 9.7 %copy-start.3 = (s32[1,8]{1,0:T(1,128)S(1)}, s32[1,8]{1,0:T(1,128)}, u32[]{:S(2)}) copy-start(s32[1,8]{1,0:T(1,128)} %owner_ref.5) | copy-start | bytes 100
  1.5 9.7 %copy-start.4 = (s32[1,8]{1,0:T(1,128)S(1)}, s32[1,8]{1,0:T(1,128)}, u32[]{:S(2)}) copy-start(s32[1,8]{1,0:T(1,128)} %slot_ref.5) | copy-start | bytes 100
  8.9 2.3 %collective-permute-start.1 = (f32[384,128]{1,0:T(8,128)S(1)}, f32[384,128]{1,0:T(8,128)S(1)}, u32[]{:S(2)}, u32[]{:S(2)}) collective-permute-start(f32[384,128]{1,0:T(8,128)S(1)} %get-tuple-element.32), channel_id=1, source_target_pairs={{0,1},{1,0},{2,3},{3,2},{4,5},{5,4},{6,7},{7,6},{8,9},{9,8},{10,11... | collective-permute-start | bytes 589832 | tf_op jit(solution)/shard_map/ppermute | solution.py:396
  14.0 20.0 %copy-start = (bf16[768,2048]{1,0:T(8,128)(2,1)S(1)}, bf16[768,2048]{1,0:T(8,128)(2,1)}, u32[]{:S(2)}) copy-start(bf16[768,2048]{1,0:T(8,128)(2,1)} %q_ref.1) | copy-start | bytes 9437188
  14.0 16.2 %collective-permute-start.2 = (bf16[2,192,256]{2,1,0:T(8,128)(2,1)S(1)}, bf16[2,192,256]{2,1,0:T(8,128)(2,1)S(1)}, u32[]{:S(2)}, u32[]{:S(2)}) collective-permute-start(bf16[2,192,256]{2,1,0:T(8,128)(2,1)S(1)} %first_block.1), channel_id=1, source_target_pairs={{0,12},{2,14},{4,8},{6,10},{8,4},{10,6},{12,0},{14,2},{1,13},{3,15... | collective-permute-start | bytes 589832 | tf_op jit(solution)/shard_map/ppermute | solution.py:391
  19.0 13.6 %collective-permute-start.5 = (bf16[2,192,256]{2,1,0:T(8,128)(2,1)S(1)}, bf16[2,192,256]{2,1,0:T(8,128)(2,1)S(1)}, u32[]{:S(2)}, u32[]{:S(2)}) collective-permute-start(bf16[2,192,256]{2,1,0:T(8,128)(2,1)S(1)} %get-tuple-element.39), channel_id=1, source_target_pairs={{0,10},{2,8},{4,14},{6,12},{8,2},{10,0},{12,6},{14,4},{1,11},{3,9}... | collective-permute-start | bytes 589832 | tf_op jit(solution)/shard_map/ppermute | solution.py:391
  23.5 19.8 %collective-permute-start.6 = (bf16[2,192,256]{2,1,0:T(8,128)(2,1)S(1)}, bf16[2,192,256]{2,1,0:T(8,128)(2,1)S(1)}, u32[]{:S(2)}, u32[]{:S(2)}) collective-permute-start(bf16[2,192,256]{2,1,0:T(8,128)(2,1)S(1)} %get-tuple-element.40), channel_id=1, source_target_pairs={{0,4},{2,6},{4,0},{6,2},{8,12},{10,14},{12,8},{14,10},{1,5},{3,7},... | collective-permute-start | bytes 589832 | tf_op jit(solution)/shard_map/ppermute | solution.py:391
  23.5 19.8 %collective-permute-start.7 = (bf16[2,192,256]{2,1,0:T(8,128)(2,1)S(1)}, bf16[2,192,256]{2,1,0:T(8,128)(2,1)S(1)}, u32[]{:S(2)}, u32[]{:S(2)}) collective-permute-start(bf16[2,192,256]{2,1,0:T(8,128)(2,1)S(1)} %get-tuple-element.41), channel_id=1, source_target_pairs={{0,6},{2,4},{4,2},{6,0},{8,14},{10,12},{12,10},{14,8},{1,7},{3,5},... | collective-permute-start | bytes 589832 | tf_op jit(solution)/shard_map/ppermute | solution.py:391
  25.5 19.4 %collective-permute-start.8 = (bf16[2,192,256]{2,1,0:T(8,128)(2,1)S(1)}, bf16[2,192,256]{2,1,0:T(8,128)(2,1)S(1)}, u32[]{:S(2)}, u32[]{:S(2)}) collective-permute-start(bf16[2,192,256]{2,1,0:T(8,128)(2,1)S(1)} %get-tuple-element.42), channel_id=1, source_target_pairs={{0,8},{2,10},{4,12},{6,14},{8,0},{10,2},{12,4},{14,6},{1,9},{3,11}... | collective-permute-start | bytes 589832 | tf_op jit(solution)/shard_map/ppermute | solution.py:391
  31.2 20.3 %collective-permute-start.3 = (bf16[2,192,256]{2,1,0:T(8,128)(2,1)S(1)}, bf16[2,192,256]{2,1,0:T(8,128)(2,1)S(1)}, u32[]{:S(2)}, u32[]{:S(2)}) collective-permute-start(bf16[2,192,256]{2,1,0:T(8,128)(2,1)S(1)} %get-tuple-element.35), channel_id=1, source_target_pairs={{0,14},{2,12},{4,10},{6,8},{8,6},{10,4},{12,2},{14,0},{1,15},{3,13... | collective-permute-start | bytes 589832 | tf_op jit(solution)/shard_map/ppermute | solution.py:391
  32.7 18.9 %collective-permute-start.4 = (bf16[2,192,256]{2,1,0:T(8,128)(2,1)S(1)}, bf16[2,192,256]{2,1,0:T(8,128)(2,1)S(1)}, u32[]{:S(2)}, u32[]{:S(2)}) collective-permute-start(bf16[2,192,256]{2,1,0:T(8,128)(2,1)S(1)} %get-tuple-element.36), channel_id=1, source_target_pairs={{0,2},{2,0},{4,6},{6,4},{8,10},{10,8},{12,14},{14,12},{1,3},{3,1},... | collective-permute-start | bytes 589832 | tf_op jit(solution)/shard_map/ppermute | solution.py:391
